TPU v7x, 512 devices: a whole 4x8x8 slice. The times are simulated.
512 devices in a mesh: gx: 32 (over x, y), gy: 16 (over z, core).
Axes of the slice: x: 4, y: 8, z: 8, core: 2. Of those that a mesh axis runs over, the one named last changes fastest.
Arguments:
- right_side: float32 [256, 128, 128], P('gx', 'gy'), may hold values from -12 to 12
- coefficient: float32 [256, 128, 128], P('gx', 'gy'), may hold values from 0.3 to 3
- previous: float32 [256, 128, 128], P('gx', 'gy'), may hold values from -6 to 6
Outputs:
- potential: float32 [256, 128, 128], P('gx', 'gy')
All inputs are finite; a program needn't handle non-finite values.
Results may differ from a plain program's by a relative error of at most 0.00002.
Values sent between devices are 32-bit elements; how exact they have to be, the bound alone decides.
No kernel may reach another device: no remote copies, remote signals or barrier semaphores. Data moves between devices by JAX's collectives and lax.ppermute only.
A program may use at most 64 MiB of HBM per device.

v0:
```python
import jax
import jax.numpy as jnp
from jax import lax
from jax.sharding import PartitionSpec as P

LEVELS = 6
PRE_SWEEPS = 2
POST_SWEEPS = 2
COARSE_SWEEPS = 8


relaxation = 0.8


def extended(block, sides, width):
    for axis, dim in sides:
        count = lax.axis_size(axis)
        forward = [(i, i + 1) for i in range(count - 1)]
        backward = [(target, source) for source, target in forward]
        low = lax.ppermute(
            lax.slice_in_dim(block, block.shape[dim] - width, None, axis=dim), axis, forward
        )
        high = lax.ppermute(lax.slice_in_dim(block, 0, width, axis=dim), axis, backward)
        block = jnp.concatenate([low, block, high], axis=dim)
    return block


def neighbours(padded):
    return [
        padded[2:, 1:-1, 1:-1],
        padded[:-2, 1:-1, 1:-1],
        padded[1:-1, 2:, 1:-1],
        padded[1:-1, :-2, 1:-1],
        padded[1:-1, 1:-1, 2:],
        padded[1:-1, 1:-1, :-2],
    ]


def face_weights(padded_coeff, coeff):
    return [0.5 * (coeff + other) for other in neighbours(padded_coeff)]


def operate(padded_field, field, weights, diagonal, factor):
    others = neighbours(padded_field)
    offdiag = weights[0] * others[0]
    for number in range(1, 6):
        offdiag = offdiag + weights[number] * others[number]
    return factor * (diagonal * field - offdiag)


def restrict(values):
    sizes_here = values.shape
    blocks = values.reshape(sizes_here[0] // 2, 2, sizes_here[1] // 2, 2, sizes_here[2] // 2, 2)
    return jnp.mean(blocks, axis=(1, 3, 5))


def prolong(values):
    sizes_here = values.shape
    spread = jnp.broadcast_to(
        values[:, None, :, None, :, None], (sizes_here[0], 2, sizes_here[1], 2, sizes_here[2], 2)
    )
    return spread.reshape(2 * sizes_here[0], 2 * sizes_here[1], 2 * sizes_here[2])


def descend(degree, field, source, coeff):
    factor = 0.25**degree
    weights = face_weights(jnp.pad(coeff, 1), coeff)
    diagonal = weights[0] + weights[1] + weights[2] + weights[3] + weights[4] + weights[5]
    inverse = relaxation / (factor * diagonal)

    def sweep_once(current):
        return current + inverse * (
            source - operate(jnp.pad(current, 1), current, weights, diagonal, factor)
        )

    if degree == LEVELS - 1:
        for number in range(COARSE_SWEEPS):
            field = sweep_once(field)
        return field
    for number in range(PRE_SWEEPS):
        field = sweep_once(field)
    residual = source - operate(jnp.pad(field, 1), field, weights, diagonal, factor)
    coarse_source = restrict(residual)
    correction = descend(
        degree + 1, jnp.zeros(coarse_source.shape, jnp.float32), coarse_source, restrict(coeff)
    )
    field = field + prolong(correction)
    for number in range(POST_SWEEPS):
        field = sweep_once(field)
    return field


def extend_field(values):
    padded = extended(values, (("gx", 0), ("gy", 1)), 1)
    return jnp.pad(padded, ((0, 0), (0, 0), (1, 1)))


def extend_coeff(values):
    padded = extended(values, (("gx", 0), ("gy", 1)), 1)
    return jnp.pad(padded, ((0, 0), (0, 0), (1, 1)))


def shard_descend(degree, field, source, coeff, bottom):
    factor = 0.25**degree
    weights = face_weights(extend_coeff(coeff), coeff)
    diagonal = weights[0] + weights[1] + weights[2] + weights[3] + weights[4] + weights[5]
    inverse = relaxation / (factor * diagonal)

    def sweep_once(current):
        return current + inverse * (
            source - operate(extend_field(current), current, weights, diagonal, factor)
        )

    if degree == 0:
        remaining = PRE_SWEEPS
    else:
        field = inverse * source
        remaining = PRE_SWEEPS - 1
    for number in range(remaining):
        field = sweep_once(field)
    residual = source - operate(extend_field(field), field, weights, diagonal, factor)
    coarse_source = restrict(residual)
    coarse_coeff = restrict(coeff)
    if degree + 1 < bottom:
        correction = shard_descend(degree + 1, None, coarse_source, coarse_coeff, bottom)
    else:
        whole_source, whole_coeff = (
            lax.all_gather(coarse_source, "gy", axis=1, tiled=True),
            lax.all_gather(coarse_coeff, "gy", axis=1, tiled=True),
        )
        whole_source, whole_coeff = (
            lax.all_gather(whole_source, "gx", axis=0, tiled=True),
            lax.all_gather(whole_coeff, "gx", axis=0, tiled=True),
        )
        whole_correction = descend(
            degree + 1, jnp.zeros(whole_source.shape, jnp.float32), whole_source, whole_coeff
        )
        extent = coarse_source.shape
        offset_x = lax.axis_index("gx") * extent[0]
        offset_y = lax.axis_index("gy") * extent[1]
        correction = lax.dynamic_slice(whole_correction, (offset_x, offset_y, jnp.int32(0)), extent)
    field = field + prolong(correction)
    for number in range(POST_SWEEPS):
        field = sweep_once(field)
    return field


def shards(right_side, coefficient, previous):
    bottom = 2
    return shard_descend(0, previous, right_side, coefficient, bottom)


def solution(mesh):
    return jax.shard_map(
        shards,
        mesh=mesh,
        in_specs=(P("gx", "gy", None), P("gx", "gy", None), P("gx", "gy", None)),
        out_specs=P("gx", "gy", None),
        check_vma=False,
    )
```

profile of v0, /device:TPU:195, one launch (start us, length us, event | category | flops | bytes accessed | tf_op | source)
XLA Modules:
  0.0 439.5 jit_solution(5479572995044764086)
XLA Ops:
  10.8 5.6 %collective-permute-start.4 = (f32[1,8,128]{2,1,0:T(8,128)S(1)}, f32[1,8,128]{2,1,0:T(8,128)S(1)}, u32[]{:S(2)}, u32[]{:S(2)}) collective-permute-start(f32[1,8,128]{2,1,0:T(8,128)S(1)} %get-tuple-element.70), channel_id=1, source_target_pairs={{16,0},{32,16},{48,32},{64,48},{80,64},{96,80},{112,96},{128,112},... | collective-permute-start | bytes 12296 | tf_op jit(solution)/shard_map/ppermute | solution.py:23
  23.3 5.1 %collective-permute-start.3 = (f32[10,1,128]{2,1,0:T(1,128)S(1)}, f32[10,1,128]{2,1,0:T(1,128)S(1)}, u32[]{:S(2)}, u32[]{:S(2)}) collective-permute-start(f32[10,1,128]{2,1,0:T(1,128)S(1)} %get-tuple-element.56), channel_id=1, source_target_pairs={{0,1},{1,2},{2,3},{3,4},{4,5},{5,6},{6,7},{7,8},{8,9},{9,10},{10,1... | collective-permute-start | bytes 15368 | tf_op jit(solution)/shard_map/ppermute | solution.py:20
  30.4 4.9 %collective-permute-start.7 = (f32[10,1,128]{2,1,0:T(1,128)S(1)}, f32[10,1,128]{2,1,0:T(1,128)S(1)}, u32[]{:S(2)}, u32[]{:S(2)}) collective-permute-start(f32[10,1,128]{2,1,0:T(1,128)S(1)} %get-tuple-element.58), channel_id=1, source_target_pairs={{0,1},{1,2},{2,3},{3,4},{4,5},{5,6},{6,7},{7,8},{8,9},{9,10},{10,1... | collective-permute-start | bytes 15368 | tf_op jit(solution)/shard_map/ppermute | solution.py:20
  49.9 6.0 %collective-permute-start.11 = (f32[10,1,128]{2,1,0:T(1,128)S(1)}, f32[10,1,128]{2,1,0:T(1,128)S(1)}, u32[]{:S(2)}, u32[]{:S(2)}) collective-permute-start(f32[10,1,128]{2,1,0:T(1,128)S(1)} %get-tuple-element.54), channel_id=1, source_target_pairs={{0,1},{1,2},{2,3},{3,4},{4,5},{5,6},{6,7},{7,8},{8,9},{9,10},{10,1... | collective-permute-start | bytes 15368 | tf_op jit(solution)/shard_map/ppermute | solution.py:20
  55.9 13.7 %all_gather.12 = f32[2,32,32]{2,0,1:T(2,128)S(1)} all-gather(f32[2,2,32]{2,0,1:T(2,128)S(1)} %copy.5), channel_id=1, replica_groups=mesh['gx'=32,'gy'=16] {'gy'}, dimensions={1}, use_global_device_ids=true | all-gather | bytes 8704 | tf_op jit(solution)/shard_map/all_gather | solution.py:129
  69.9 5.8 %collective-permute-start.16 = (f32[1,8,128]{2,1,0:T(8,128)S(1)}, f32[1,8,128]{2,1,0:T(8,128)S(1)}, u32[]{:S(2)}, u32[]{:S(2)}) collective-permute-start(f32[1,8,128]{2,1,0:T(8,128)S(1)} %get-tuple-element.65), channel_id=1, source_target_pairs={{16,0},{32,16},{48,32},{64,48},{80,64},{96,80},{112,96},{128,112},... | collective-permute-start | bytes 12296 | tf_op jit(solution)/shard_map/ppermute | solution.py:23
  86.4 4.9 %collective-permute-start.19 = (f32[10,1,128]{2,1,0:T(1,128)S(1)}, f32[10,1,128]{2,1,0:T(1,128)S(1)}, u32[]{:S(2)}, u32[]{:S(2)}) collective-permute-start(f32[10,1,128]{2,1,0:T(1,128)S(1)} %get-tuple-element.52), channel_id=1, source_target_pairs={{0,1},{1,2},{2,3},{3,4},{4,5},{5,6},{6,7},{7,8},{8,9},{9,10},{10,1... | collective-permute-start | bytes 15368 | tf_op jit(solution)/shard_map/ppermute | solution.py:20
  94.8 5.5 %collective-permute-start.20 = (f32[1,4,64]{2,1,0:T(4,128)S(1)}, f32[1,4,64]{2,1,0:T(4,128)S(1)}, u32[]{:S(2)}, u32[]{:S(2)}) collective-permute-start(f32[1,4,64]{2,1,0:T(4,128)S(1)} %get-tuple-element.89), channel_id=1, source_target_pairs={{16,0},{32,16},{48,32},{64,48},{80,64},{96,80},{112,96},{128,112},... | collective-permute-start | bytes 3080 | tf_op jit(solution)/shard_map/ppermute | solution.py:23
  102.2 39.0 %all_gather.13 = f32[64,32,32]{2,1,0:T(8,128)S(1)} all-gather(f32[2,32,32]{2,1,0:T(8,128)S(1)} %copy.6), channel_id=1, replica_groups=mesh['gx'=32,'gy'=16] {'gx'}, dimensions={0}, use_global_device_ids=true | all-gather | bytes 270336 | tf_op jit(solution)/shard_map/all_gather | solution.py:133
  141.9 18.7 %reshape.56 = f32[32,2,16,2,16,2]{1,0,5,4,3,2:T(8,128)} reshape(f32[64,32,32]{0,2,1:T(8,128)S(1)} %copy.8) | data formatting | bytes 524288 | tf_op jit(solution)/shard_map/reshape | solution.py:53
  160.6 7.1 %reduce_sum.94 = f32[32,16,16]{0,2,1:T(8,128)S(1)} reduce(f32[32,2,16,2,16,2]{1,0,5,4,3,2:T(8,128)} %reshape.56, f32[]{:T(128)} %constant.18.clone.1), dimensions={1,3,5}, to_apply=%region_4.5 | reduce | flops 57344 | bytes 294916 | tf_op jit(solution)/shard_map/reduce_sum | solution.py:54
  167.7 12.9 %collective-permute-start.22 = (f32[6,1,64]{2,1,0:T(1,128)S(1)}, f32[6,1,64]{2,1,0:T(1,128)S(1)}, u32[]{:S(2)}, u32[]{:S(2)}) collective-permute-start(f32[6,1,64]{2,1,0:T(1,128)S(1)} %get-tuple-element.79), channel_id=1, source_target_pairs={{1,0},{2,1},{3,2},{4,3},{5,4},{6,5},{7,6},{8,7},{9,8},{10,9},{11,1... | collective-permute-start | bytes 4616 | tf_op jit(solution)/shard_map/ppermute | solution.py:23
  180.7 6.4 %collective-permute-start.23 = (f32[6,1,64]{2,1,0:T(1,128)S(1)}, f32[6,1,64]{2,1,0:T(1,128)S(1)}, u32[]{:S(2)}, u32[]{:S(2)}) collective-permute-start(f32[6,1,64]{2,1,0:T(1,128)S(1)} %get-tuple-element.78), channel_id=1, source_target_pairs={{0,1},{1,2},{2,3},{3,4},{4,5},{5,6},{6,7},{7,8},{8,9},{9,10},{10,1... | collective-permute-start | bytes 4616 | tf_op jit(solution)/shard_map/ppermute | solution.py:20
  200.2 6.1 %collective-permute-start.27 = (f32[6,1,64]{2,1,0:T(1,128)S(1)}, f32[6,1,64]{2,1,0:T(1,128)S(1)}, u32[]{:S(2)}, u32[]{:S(2)}) collective-permute-start(f32[6,1,64]{2,1,0:T(1,128)S(1)} %get-tuple-element.76), channel_id=1, source_target_pairs={{0,1},{1,2},{2,3},{3,4},{4,5},{5,6},{6,7},{7,8},{8,9},{9,10},{10,1... | collective-permute-start | bytes 4616 | tf_op jit(solution)/shard_map/ppermute | solution.py:20
  207.7 16.7 %all_gather.14 = f32[2,32,32]{2,0,1:T(2,128)S(1)} all-gather(f32[2,2,32]{2,0,1:T(2,128)S(1)} %copy.14), channel_id=1, replica_groups=mesh['gx'=32,'gy'=16] {'gy'}, dimensions={1}, use_global_device_ids=true | all-gather | bytes 8704 | tf_op jit(solution)/shard_map/all_gather | solution.py:128
  224.4 36.6 %all_gather.15 = f32[64,32,32]{2,1,0:T(8,128)S(1)} all-gather(f32[2,32,32]{2,1,0:T(8,128)S(1)} %copy.15), channel_id=1, replica_groups=mesh['gx'=32,'gy'=16] {'gx'}, dimensions={0}, use_global_device_ids=true | all-gather | bytes 270336 | tf_op jit(solution)/shard_map/all_gather | solution.py:132
  268.4 19.5 %reshape.57 = f32[32,2,16,2,16,2]{1,0,5,4,3,2:T(8,128)} reshape(f32[64,32,32]{0,2,1:T(8,128)} %fusion.36) | data formatting | bytes 524288 | tf_op jit(solution)/shard_map/reshape | solution.py:53
  287.9 7.1 %reduce_sum.95 = f32[32,16,16]{0,2,1:T(8,128)S(1)} reduce(f32[32,2,16,2,16,2]{1,0,5,4,3,2:T(8,128)} %reshape.57, f32[]{:T(128)} %constant.18.clone.1), dimensions={1,3,5}, to_apply=%region_5.6 | reduce | flops 57344 | bytes 294916 | tf_op jit(solution)/shard_map/reduce_sum | solution.py:54
  327.2 6.6 %broadcast_in_dim.48 = f32[32,2,16,2,16,2]{1,0,5,4,3,2:T(8,128)} broadcast(f32[32,16,16]{0,2,1:T(8,128)S(1)} %fusion.152), dimensions={0,2,4} | broadcast | bytes 294912 | tf_op jit(solution)/shard_map/broadcast_in_dim | solution.py:59
  333.8 15.4 %reshape.62 = f32[64,32,32]{0,2,1:T(8,128)} reshape(f32[32,2,16,2,16,2]{1,0,5,4,3,2:T(8,128)} %broadcast_in_dim.48) | data formatting | bytes 524288 | tf_op jit(solution)/shard_map/reshape | solution.py:62
  354.4 4.6 %collective-permute-start.28 = (f32[1,4,64]{2,1,0:T(4,128)S(1)}, f32[1,4,64]{2,1,0:T(4,128)S(1)}, u32[]{:S(2)}, u32[]{:S(2)}) collective-permute-start(f32[1,4,64]{2,1,0:T(4,128)S(1)} %get-tuple-element.85), channel_id=1, source_target_pairs={{16,0},{32,16},{48,32},{64,48},{80,64},{96,80},{112,96},{128,112},... | collective-permute-start | bytes 3080 | tf_op jit(solution)/shard_map/ppermute | solution.py:23
  365.4 14.4 %collective-permute-start.30 = (f32[6,1,64]{2,1,0:T(1,128)S(1)}, f32[6,1,64]{2,1,0:T(1,128)S(1)}, u32[]{:S(2)}, u32[]{:S(2)}) collective-permute-start(f32[6,1,64]{2,1,0:T(1,128)S(1)} %get-tuple-element.75), channel_id=1, source_target_pairs={{1,0},{2,1},{3,2},{4,3},{5,4},{6,5},{7,6},{8,7},{9,8},{10,9},{11,1... | collective-permute-start | bytes 4616 | tf_op jit(solution)/shard_map/ppermute | solution.py:23
  414.7 5.2 %collective-permute-start.39 = (f32[10,1,128]{2,1,0:T(1,128)S(1)}, f32[10,1,128]{2,1,0:T(1,128)S(1)}, u32[]{:S(2)}, u32[]{:S(2)}) collective-permute-start(f32[10,1,128]{2,1,0:T(1,128)S(1)} %get-tuple-element.50), channel_id=1, source_target_pairs={{0,1},{1,2},{2,3},{3,4},{4,5},{5,6},{6,7},{7,8},{8,9},{9,10},{10,1... | collective-permute-start | bytes 15368 | tf_op jit(solution)/shard_map/ppermute | solution.py:20
  431.4 6.4 %collective-permute-start.43 = (f32[10,1,128]{2,1,0:T(1,128)S(1)}, f32[10,1,128]{2,1,0:T(1,128)S(1)}, u32[]{:S(2)}, u32[]{:S(2)}) collective-permute-start(f32[10,1,128]{2,1,0:T(1,128)S(1)} %get-tuple-element.48), channel_id=1, source_target_pairs={{0,1},{1,2},{2,3},{3,4},{4,5},{5,6},{6,7},{7,8},{8,9},{9,10},{10,1... | collective-permute-start | bytes 15368 | tf_op jit(solution)/shard_map/ppermute | solution.py:20
  (301 shorter events, 163.5 us)
Async XLA Ops:
  0.7 18.8 %collective-permute-start.1 = (f32[1,8,128]{2,1,0:T(8,128)S(1)}, f32[1,8,128]{2,1,0:T(8,128)S(1)}, u32[]{:S(2)}, u32[]{:S(2)}) collective-permute-start(f32[1,8,128]{2,1,0:T(8,128)S(1)} %get-tuple-element.68), channel_id=1, source_target_pairs={{0,16},{16,32},{32,48},{48,64},{64,80},{80,96},{96,112},{112,128},... | collective-permute-start | bytes 12296 | tf_op jit(solution)/shard_map/ppermute | solution.py:20
  3.9 15.6 %collective-permute-start = (f32[1,8,128]{2,1,0:T(8,128)S(1)}, f32[1,8,128]{2,1,0:T(8,128)S(1)}, u32[]{:S(2)}, u32[]{:S(2)}) collective-permute-start(f32[1,8,128]{2,1,0:T(8,128)S(1)} %get-tuple-element.69), channel_id=1, source_target_pairs={{16,0},{32,16},{48,32},{64,48},{80,64},{96,80},{112,96},{128,112},... | collective-permute-start | bytes 12296 | tf_op jit(solution)/shard_map/ppermute | solution.py:23
  8.8 19.6 %collective-permute-start.5 = (f32[1,8,128]{2,1,0:T(8,128)S(1)}, f32[1,8,128]{2,1,0:T(8,128)S(1)}, u32[]{:S(2)}, u32[]{:S(2)}) collective-permute-start(f32[1,8,128]{2,1,0:T(8,128)S(1)} %get-tuple-element.71), channel_id=1, source_target_pairs={{0,16},{16,32},{32,48},{48,64},{64,80},{80,96},{96,112},{112,128},... | collective-permute-start | bytes 12296 | tf_op jit(solution)/shard_map/ppermute | solution.py:20
  10.8 17.7 %collective-permute-start.4 = (f32[1,8,128]{2,1,0:T(8,128)S(1)}, f32[1,8,128]{2,1,0:T(8,128)S(1)}, u32[]{:S(2)}, u32[]{:S(2)}) collective-permute-start(f32[1,8,128]{2,1,0:T(8,128)S(1)} %get-tuple-element.70), channel_id=1, source_target_pairs={{16,0},{32,16},{48,32},{64,48},{80,64},{96,80},{112,96},{128,112},... | collective-permute-start | bytes 12296 | tf_op jit(solution)/shard_map/ppermute | solution.py:23
  19.6 15.7 %collective-permute-start.2 = (f32[10,1,128]{2,1,0:T(1,128)S(1)}, f32[10,1,128]{2,1,0:T(1,128)S(1)}, u32[]{:S(2)}, u32[]{:S(2)}) collective-permute-start(f32[10,1,128]{2,1,0:T(1,128)S(1)} %get-tuple-element.57), channel_id=1, source_target_pairs={{1,0},{2,1},{3,2},{4,3},{5,4},{6,5},{7,6},{8,7},{9,8},{10,9},{11,1... | collective-permute-start | bytes 15368 | tf_op jit(solution)/shard_map/ppermute | solution.py:23
  23.3 12.0 %collective-permute-start.3 = (f32[10,1,128]{2,1,0:T(1,128)S(1)}, f32[10,1,128]{2,1,0:T(1,128)S(1)}, u32[]{:S(2)}, u32[]{:S(2)}) collective-permute-start(f32[10,1,128]{2,1,0:T(1,128)S(1)} %get-tuple-element.56), channel_id=1, source_target_pairs={{0,1},{1,2},{2,3},{3,4},{4,5},{5,6},{6,7},{7,8},{8,9},{9,10},{10,1... | collective-permute-start | bytes 15368 | tf_op jit(solution)/shard_map/ppermute | solution.py:20
  36.3 11.7 %collective-permute-start.8 = (f32[1,8,128]{2,1,0:T(8,128)S(1)}, f32[1,8,128]{2,1,0:T(8,128)S(1)}, u32[]{:S(2)}, u32[]{:S(2)}) collective-permute-start(f32[1,8,128]{2,1,0:T(8,128)S(1)} %get-tuple-element.67), channel_id=1, source_target_pairs={{16,0},{32,16},{48,32},{64,48},{80,64},{96,80},{112,96},{128,112},... | collective-permute-start | bytes 12296 | tf_op jit(solution)/shard_map/ppermute | solution.py:23
  38.3 9.7 %collective-permute-start.9 = (f32[1,8,128]{2,1,0:T(8,128)S(1)}, f32[1,8,128]{2,1,0:T(8,128)S(1)}, u32[]{:S(2)}, u32[]{:S(2)}) collective-permute-start(f32[1,8,128]{2,1,0:T(8,128)S(1)} %get-tuple-element.66), channel_id=1, source_target_pairs={{0,16},{16,32},{32,48},{48,64},{64,80},{80,96},{96,112},{112,128},... | collective-permute-start | bytes 12296 | tf_op jit(solution)/shard_map/ppermute | solution.py:20
  41.6 36.0 %collective-permute-start.12 = (f32[1,4,64]{2,1,0:T(4,128)S(1)}, f32[1,4,64]{2,1,0:T(4,128)S(1)}, u32[]{:S(2)}, u32[]{:S(2)}) collective-permute-start(f32[1,4,64]{2,1,0:T(4,128)S(1)} %get-tuple-element.90), channel_id=1, source_target_pairs={{16,0},{32,16},{48,32},{64,48},{80,64},{96,80},{112,96},{128,112},... | collective-permute-start | bytes 3080 | tf_op jit(solution)/shard_map/ppermute | solution.py:23
  45.7 32.0 %collective-permute-start.13 = (f32[1,4,64]{2,1,0:T(4,128)S(1)}, f32[1,4,64]{2,1,0:T(4,128)S(1)}, u32[]{:S(2)}, u32[]{:S(2)}) collective-permute-start(f32[1,4,64]{2,1,0:T(4,128)S(1)} %get-tuple-element.91), channel_id=1, source_target_pairs={{0,16},{16,32},{32,48},{48,64},{64,80},{80,96},{96,112},{112,128},... | collective-permute-start | bytes 3080 | tf_op jit(solution)/shard_map/ppermute | solution.py:20
  48.0 21.6 %collective-permute-start.10 = (f32[10,1,128]{2,1,0:T(1,128)S(1)}, f32[10,1,128]{2,1,0:T(1,128)S(1)}, u32[]{:S(2)}, u32[]{:S(2)}) collective-permute-start(f32[10,1,128]{2,1,0:T(1,128)S(1)} %get-tuple-element.55), channel_id=1, source_target_pairs={{1,0},{2,1},{3,2},{4,3},{5,4},{6,5},{7,6},{8,7},{9,8},{10,9},{11,1... | collective-permute-start | bytes 15368 | tf_op jit(solution)/shard_map/ppermute | solution.py:23
  49.9 19.7 %collective-permute-start.11 = (f32[10,1,128]{2,1,0:T(1,128)S(1)}, f32[10,1,128]{2,1,0:T(1,128)S(1)}, u32[]{:S(2)}, u32[]{:S(2)}) collective-permute-start(f32[10,1,128]{2,1,0:T(1,128)S(1)} %get-tuple-element.54), channel_id=1, source_target_pairs={{0,1},{1,2},{2,3},{3,4},{4,5},{5,6},{6,7},{7,8},{8,9},{9,10},{10,1... | collective-permute-start | bytes 15368 | tf_op jit(solution)/shard_map/ppermute | solution.py:20
  69.9 14.5 %collective-permute-start.16 = (f32[1,8,128]{2,1,0:T(8,128)S(1)}, f32[1,8,128]{2,1,0:T(8,128)S(1)}, u32[]{:S(2)}, u32[]{:S(2)}) collective-permute-start(f32[1,8,128]{2,1,0:T(8,128)S(1)} %get-tuple-element.65), channel_id=1, source_target_pairs={{16,0},{32,16},{48,32},{64,48},{80,64},{96,80},{112,96},{128,112},... | collective-permute-start | bytes 12296 | tf_op jit(solution)/shard_map/ppermute | solution.py:23
  75.7 8.8 %collective-permute-start.17 = (f32[1,8,128]{2,1,0:T(8,128)S(1)}, f32[1,8,128]{2,1,0:T(8,128)S(1)}, u32[]{:S(2)}, u32[]{:S(2)}) collective-permute-start(f32[1,8,128]{2,1,0:T(8,128)S(1)} %get-tuple-element.64), channel_id=1, source_target_pairs={{0,16},{16,32},{32,48},{48,64},{64,80},{80,96},{96,112},{112,128},... | collective-permute-start | bytes 12296 | tf_op jit(solution)/shard_map/ppermute | solution.py:20
  77.7 13.6 %collective-permute-start.14 = (f32[6,1,64]{2,1,0:T(1,128)S(1)}, f32[6,1,64]{2,1,0:T(1,128)S(1)}, u32[]{:S(2)}, u32[]{:S(2)}) collective-permute-start(f32[6,1,64]{2,1,0:T(1,128)S(1)} %get-tuple-element.81), channel_id=1, source_target_pairs={{1,0},{2,1},{3,2},{4,3},{5,4},{6,5},{7,6},{8,7},{9,8},{10,9},{11,1... | collective-permute-start | bytes 4616 | tf_op jit(solution)/shard_map/ppermute | solution.py:23
  80.1 11.3 %collective-permute-start.15 = (f32[6,1,64]{2,1,0:T(1,128)S(1)}, f32[6,1,64]{2,1,0:T(1,128)S(1)}, u32[]{:S(2)}, u32[]{:S(2)}) collective-permute-start(f32[6,1,64]{2,1,0:T(1,128)S(1)} %get-tuple-element.80), channel_id=1, source_target_pairs={{0,1},{1,2},{2,3},{3,4},{4,5},{5,6},{6,7},{7,8},{8,9},{9,10},{10,1... | collective-permute-start | bytes 4616 | tf_op jit(solution)/shard_map/ppermute | solution.py:20
  94.8 72.9 %collective-permute-start.20 = (f32[1,4,64]{2,1,0:T(4,128)S(1)}, f32[1,4,64]{2,1,0:T(4,128)S(1)}, u32[]{:S(2)}, u32[]{:S(2)}) collective-permute-start(f32[1,4,64]{2,1,0:T(4,128)S(1)} %get-tuple-element.89), channel_id=1, source_target_pairs={{16,0},{32,16},{48,32},{64,48},{80,64},{96,80},{112,96},{128,112},... | collective-permute-start | bytes 3080 | tf_op jit(solution)/shard_map/ppermute | solution.py:23
  100.3 67.4 %collective-permute-start.21 = (f32[1,4,64]{2,1,0:T(4,128)S(1)}, f32[1,4,64]{2,1,0:T(4,128)S(1)}, u32[]{:S(2)}, u32[]{:S(2)}) collective-permute-start(f32[1,4,64]{2,1,0:T(4,128)S(1)} %get-tuple-element.88), channel_id=1, source_target_pairs={{0,16},{16,32},{32,48},{48,64},{64,80},{80,96},{96,112},{112,128},... | collective-permute-start | bytes 3080 | tf_op jit(solution)/shard_map/ppermute | solution.py:20
  167.7 20.8 %collective-permute-start.22 = (f32[6,1,64]{2,1,0:T(1,128)S(1)}, f32[6,1,64]{2,1,0:T(1,128)S(1)}, u32[]{:S(2)}, u32[]{:S(2)}) collective-permute-start(f32[6,1,64]{2,1,0:T(1,128)S(1)} %get-tuple-element.79), channel_id=1, source_target_pairs={{1,0},{2,1},{3,2},{4,3},{5,4},{6,5},{7,6},{8,7},{9,8},{10,9},{11,1... | collective-permute-start | bytes 4616 | tf_op jit(solution)/shard_map/ppermute | solution.py:23
  198.3 8.7 %collective-permute-start.26 = (f32[6,1,64]{2,1,0:T(1,128)S(1)}, f32[6,1,64]{2,1,0:T(1,128)S(1)}, u32[]{:S(2)}, u32[]{:S(2)}) collective-permute-start(f32[6,1,64]{2,1,0:T(1,128)S(1)} %get-tuple-element.77), channel_id=1, source_target_pairs={{1,0},{2,1},{3,2},{4,3},{5,4},{6,5},{7,6},{8,7},{9,8},{10,9},{11,1... | collective-permute-start | bytes 4616 | tf_op jit(solution)/shard_map/ppermute | solution.py:23
  365.4 17.2 %collective-permute-start.30 = (f32[6,1,64]{2,1,0:T(1,128)S(1)}, f32[6,1,64]{2,1,0:T(1,128)S(1)}, u32[]{:S(2)}, u32[]{:S(2)}) collective-permute-start(f32[6,1,64]{2,1,0:T(1,128)S(1)} %get-tuple-element.75), channel_id=1, source_target_pairs={{1,0},{2,1},{3,2},{4,3},{5,4},{6,5},{7,6},{8,7},{9,8},{10,9},{11,1... | collective-permute-start | bytes 4616 | tf_op jit(solution)/shard_map/ppermute | solution.py:23
  392.0 8.7 %collective-permute-start.34 = (f32[6,1,64]{2,1,0:T(1,128)S(1)}, f32[6,1,64]{2,1,0:T(1,128)S(1)}, u32[]{:S(2)}, u32[]{:S(2)}) collective-permute-start(f32[6,1,64]{2,1,0:T(1,128)S(1)} %get-tuple-element.73), channel_id=1, source_target_pairs={{1,0},{2,1},{3,2},{4,3},{5,4},{6,5},{7,6},{8,7},{9,8},{10,9},{11,1... | collective-permute-start | bytes 4616 | tf_op jit(solution)/shard_map/ppermute | solution.py:23
  411.4 8.5 %collective-permute-start.38 = (f32[10,1,128]{2,1,0:T(1,128)S(1)}, f32[10,1,128]{2,1,0:T(1,128)S(1)}, u32[]{:S(2)}, u32[]{:S(2)}) collective-permute-start(f32[10,1,128]{2,1,0:T(1,128)S(1)} %get-tuple-element.51), channel_id=1, source_target_pairs={{1,0},{2,1},{3,2},{4,3},{5,4},{6,5},{7,6},{8,7},{9,8},{10,9},{11,1... | collective-permute-start | bytes 15368 | tf_op jit(solution)/shard_map/ppermute | solution.py:23
  429.4 8.5 %collective-permute-start.42 = (f32[10,1,128]{2,1,0:T(1,128)S(1)}, f32[10,1,128]{2,1,0:T(1,128)S(1)}, u32[]{:S(2)}, u32[]{:S(2)}) collective-permute-start(f32[10,1,128]{2,1,0:T(1,128)S(1)} %get-tuple-element.49), channel_id=1, source_target_pairs={{1,0},{2,1},{3,2},{4,3},{5,4},{6,5},{7,6},{8,7},{9,8},{10,9},{11,1... | collective-permute-start | bytes 15368 | tf_op jit(solution)/shard_map/ppermute | solution.py:23
  (74 other events, 1940.9 us)
where the time goes:
time: 442 us; the launch traced here: 439 us
  starting transfers between devices  176 us (40%)
  blocking collectives  106 us (24%)
  local copies, waits for them, and re-layouts  86.6 us (20%)
  other arithmetic  47.3 us (11%)
  waiting for transfers between devices  21.7 us (5%)
    ppermute x22, starting transfers between devices, extended(): lax.ppermute(lax.slice_in_dim(block, 0, width, axis=dim), axis, backward)  91.3 us
    ppermute x22, starting transfers between devices, extended(): lax.ppermute(lax.slice_in_dim(block, block.shape[dim] - width, None, axis...  84.8 us
    reshape x7, local copies, waits for them, and re-layouts, restrict(): values.reshape(sizes_here[0] // 2, 2, sizes_here[1] // 2, 2, sizes_here[2...  48.2 us
    all_gather x1, blocking collectives, shard_descend(): lax.all_gather(whole_coeff, 'gx', axis=0, tiled=True)  39 us
    all_gather x1, blocking collectives, shard_descend(): lax.all_gather(whole_source, 'gx', axis=0, tiled=True)  36.6 us
    reshape x5, local copies, waits for them, and re-layouts, prolong(): spread.reshape(2 * sizes_here[0], 2 * sizes_here[1], 2 * sizes_here[2])  21.7 us
    ppermute x22, waiting for transfers between devices, extended(): lax.ppermute(lax.slice_in_dim(block, block.shape[dim] - width, None, axis...  21.7 us
    reduce_sum x10, other arithmetic, restrict(): return jnp.mean(blocks, axis=(1, 3, 5))  18.7 us
  transfers between devices with their start and end apart: 44, of which 12 were waited for; matrix products, arithmetic and copies ran while one was open for 8% of the time, Pallas kernels for 0%

commit v1 on v0

v1 whole, which is shorter than its diff:
```python
import jax
import jax.numpy as jnp
from jax import lax
from jax.experimental import pallas as pl
from jax.experimental.pallas import tpu as pltpu
from jax.sharding import PartitionSpec as P

RELAX = 0.8
KEEP = 1.0 - RELAX
HALO = 7
ROWS = 24
COARSE_SWEEPS = 8
VMEM = 48 * 1024 * 1024
EXACT = lax.Precision.HIGHEST


def lanes(x, n):
    return pltpu.roll(x, (-n) % x.shape[1], axis=1)


def rows(x, n):
    return pltpu.roll(x, (-n) % x.shape[0], axis=0)


def iota(shape, dim):
    return lax.broadcasted_iota(jnp.int32, shape, dim)


class Window:
    def __init__(self, step, planes):
        self.step = step
        self.planes = planes
        lane = iota((ROWS, 128), 1)
        self.last = lane >= 128 - step
        self.edge = (lane < step) | self.last

    def weights(self, coeff):
        first, end = self.planes
        self.wx, self.wy, self.wz, self.diag, self.inv = {}, {}, {}, {}, {}
        for i in range(first - 1, end):
            self.wx[i] = coeff[i] + coeff[i + 1]
        for i in range(first, end):
            k = coeff[i]
            wy = k + rows(k, self.step)
            wz = jnp.where(self.last, 0.0, k + lanes(k, self.step))
            diag = self.wx[i] + self.wx[i - 1] + (wy + rows(wy, -self.step))
            diag = diag + (wz + lanes(wz, -self.step)) + jnp.where(self.edge, k, 0.0)
            self.wy[i], self.wz[i], self.diag[i] = wy, wz, diag
            self.inv[i] = jnp.where(k > 0.0, RELAX / diag, 0.0)

    def around(self, v, i):
        c = v[i]
        wy, wz, step = self.wy[i], self.wz[i], self.step
        total = self.wx[i] * v[i + 1] + self.wx[i - 1] * v[i - 1]
        total = total + (wy * rows(c, step) + rows(wy * c, -step))
        return total + (wz * lanes(c, step) + lanes(wz * c, -step))

    def sweep(self, v, source, first, end):
        return {
            i: KEEP * v[i] + self.inv[i] * (source[i] + self.around(v, i)) for i in range(first, end)
        }

    def residual(self, v, source, first, end):
        return {i: source[i] - self.diag[i] * v[i] + self.around(v, i) for i in range(first, end)}


class Stored:
    def __init__(self, ref, first):
        self.ref, self.first = ref, first

    def __getitem__(self, i):
        return self.ref[i - self.first]

    def __setitem__(self, i, value):
        self.ref[i - self.first] = value


def block_sum(low, high, step):
    s = low + high
    s = s + rows(s, step)
    return s + lanes(s, step)


def down_kernel(mid, low, high, packed, v0_out, k0_out, f0_out, k1_out, f1_out):
    def field(which):
        return {
            i - HALO: jnp.concatenate([low[which, i], mid[which, i], high[which, i]], axis=0)
            for i in range(mid.shape[1])
        }

    source, coeff, v = field(0), field(1), field(2)
    source = {i: 2.0 * source[i] for i in range(-6, 14)}

    fine = Window(1, (-6, 14))
    fine.weights(coeff)
    v = fine.sweep(v, source, -6, 14)
    v = fine.sweep(v, source, -5, 13)
    for i in range(-2, 10):
        v0_out[i + 2] = v[i]
        k0_out[i + 2] = coeff[i]
    for i in range(-1, 9):
        f0_out[i + 1] = source[i]
    r = fine.residual(v, source, -4, 12)

    source = {i: 0.5 * block_sum(r[2 * i], r[2 * i + 1], 1) for i in range(-2, 6)}
    coeff = {i: 0.125 * block_sum(coeff[2 * i], coeff[2 * i + 1], 1) for i in range(-3, 7)}
    for i in range(-2, 6):
        f1_out[i + 2] = source[i]
    for i in range(-3, 7):
        k1_out[i + 3] = coeff[i]
    middle = Window(2, (-2, 6))
    middle.weights(coeff)
    v = {i: middle.inv[i] * source[i] for i in range(-2, 6)}
    v = middle.sweep(v, source, -1, 5)
    even = iota((8, 128), 1) % 2 == 0
    for i in range(4):
        c = v[i][8:16]
        c = jnp.where(even, c, lanes(rows(c, 2), -1))
        packed[2 * i + 2 : 2 * i + 3, :] = c[0:1]
        packed[2 * i + 3 : 2 * i + 4, :] = c[4:5]
    r = middle.residual(v, source, 0, 4)

    source = [0.5 * block_sum(r[2 * i], r[2 * i + 1], 2)[8:16] for i in range(2)]
    coeff = [0.125 * block_sum(coeff[2 * i], coeff[2 * i + 1], 2)[8:16] for i in range(2)]
    table = jnp.concatenate(source + coeff, axis=0)
    pick = jnp.where(iota((128, 128), 0) == 4 * (iota((128, 128), 1) % 32), 1.0, 0.0)
    table = jnp.dot(table, pick, precision=EXACT, preferred_element_type=jnp.float32)
    group = iota((16, 128), 1) // 32
    chosen = iota((16, 128), 0) == 4 * group
    for c in range(2):
        one = jnp.where(chosen, table[16 * c : 16 * c + 16], 0.0)
        packed[c : c + 1, :] = jnp.sum(one, axis=0, keepdims=True)


class Coarse:
    def __init__(self, coeff, nxp, nxm, nyp, nym, ylast, yedge, zstep):
        self.nxp, self.nxm, self.nyp, self.nym, self.zstep = nxp, nxm, nyp, nym, zstep
        z = iota(coeff[0].shape, 1) % 32
        zlast = z >= 32 - zstep
        zedge = (z < zstep) | zlast
        self.wp = [k + n for k, n in zip(coeff, nxp(coeff))]
        self.wm = [k + n for k, n in zip(coeff, nxm(coeff))]
        self.wy = [jnp.where(ylast, 0.0, k + nyp(k)) for k in coeff]
        self.wz = [jnp.where(zlast, 0.0, k + lanes(k, zstep)) for k in coeff]
        self.diag = []
        for k, wp, wm, wy, wz in zip(coeff, self.wp, self.wm, self.wy, self.wz):
            diag = wp + wm + (wy + nym(wy)) + (wz + lanes(wz, -zstep))
            self.diag.append(diag + (jnp.where(yedge, k, 0.0) + jnp.where(zedge, k, 0.0)))
        self.inv = [RELAX / d for d in self.diag]

    def around(self, v):
        out = []
        for c, p, m, wp, wm, wy, wz in zip(
            v, self.nxp(v), self.nxm(v), self.wp, self.wm, self.wy, self.wz
        ):
            total = wp * p + wm * m
            total = total + (wy * self.nyp(c) + self.nym(wy * c))
            out.append(total + (wz * lanes(c, self.zstep) + lanes(wz * c, -self.zstep)))
        return out

    def first(self, source):
        return [i * f for i, f in zip(self.inv, source)]

    def sweep(self, v, source):
        around = self.around(v)
        return [KEEP * c + i * (f + t) for c, i, f, t in zip(v, self.inv, source, around)]

    def sweeps(self, v, source, count):
        step = lambda _, v: tuple(self.sweep(list(v), source))
        return list(lax.fori_loop(0, count, step, tuple(v)))

    def residual(self, v, source):
        around = self.around(v)
        return [f - d * c + t for c, d, f, t in zip(v, self.diag, source, around)]


def above(c):
    return jnp.concatenate([c[8:], rows(c[:8], 1)], axis=0)


def below(c):
    return jnp.concatenate([rows(c[8:], -1), c[:8]], axis=0)


UNROLL = 8
PAD = 3


def up_kernel(
    place, gathered, v0, k0, f0, k1, f1, vmid, vlow, vhigh, out,
    k2, f2, va, vb, wxi, wxe, wyi, wye, wz2, diag2, inv2, sum2, e3,
):
    gx, gy = place[0], place[1]
    lane = iota((16, 128), 1)
    row = iota((16, 128), 0)
    group, z = lane // 32, lane % 32
    xl, yl = group // 2, group % 2
    zero = jnp.zeros((16, 128), jnp.float32)

    for ref in (k2, f2, va, vb, wxi, wxe, wyi, wye, wz2, inv2):
        for i in range(PAD):
            ref[i] = zero
            ref[32 + PAD + i] = zero
    for i in range(32):
        for c, ref in ((0, f2), (1, k2)):
            for core in range(2):
                here = pl.ds(64 * core + 2 * i + c, 8, stride=128)
                ref[i + PAD, 8 * core : 8 * core + 8] = gathered[here, :]

    def sides(c):
        up, down = lanes(c, 32), lanes(c, -32)
        inner = jnp.where(yl == 0, up, down)
        outer = jnp.where(yl == 1, above(down), below(up))
        return inner, outer

    yout = ((yl == 1) & (row == 15)) | ((yl == 0) & (row == 0))
    zlast = z == 31
    zedge = zlast | (z == 0)

    def each(field, body):
        def steps(step, turned):
            before, here = turned
            for u in range(UNROLL):
                i = PAD + UNROLL * step + u
                after = lanes(field[i + 1], 64)
                body(i, field[i], here, jnp.where(xl == 1, after, before))
                before, here = here, after
            return before, here

        lax.fori_loop(0, 32 // UNROLL, steps, (zero, lanes(field[PAD], 64)))

    def summed(k):
        k = k + lanes(k, 64)
        return k + lanes(k, 32)

    def prepare(i, k, inner, outer):
        a, b = k + inner, k + outer
        yi, yo = sides(k)
        c = k + yi
        e = jnp.where(yout, 0.0, k + yo)
        w = jnp.where(zlast, 0.0, k + lanes(k, 1))
        diag = (a + b) + (c + e) + (w + lanes(w, -1))
        diag = diag + (jnp.where(yout, k, 0.0) + jnp.where(zedge, k, 0.0))
        inv = RELAX / diag
        wxi[i], wxe[i], wyi[i], wye[i], wz2[i], diag2[i], inv2[i] = a, b, c, e, w, diag, inv
        va[i] = inv * f2[i]
        sum2[i] = summed(k)

    each(k2, prepare)

    def around2(i, c, inner, outer):
        yi, yo = sides(c)
        w = wz2[i]
        total = wxi[i] * inner + wxe[i] * outer
        total = total + (wyi[i] * yi + wye[i] * yo)
        return total + (w * lanes(c, 1) + lanes(w * c, -1))

    def sweep2(i, c, inner, outer):
        return KEEP * c + inv2[i] * (f2[i] + around2(i, c, inner, outer))

    def first2(i, c, inner, outer):
        vb[i] = sweep2(i, c, inner, outer)

    def four(q):
        t = jnp.where(group == 0, sum2[4 * q + PAD], sum2[4 * q + PAD + 1])
        t = jnp.where(group == 2, sum2[4 * q + PAD + 2], t)
        t = jnp.where(group == 3, sum2[4 * q + PAD + 3], t)
        return t + lanes(t, 1)

    c3 = [0.125 * four(q) for q in range(8)]
    each(va, first2)

    def residual2(i, c, inner, outer):
        sum2[i] = summed(f2[i] - diag2[i] * c + around2(i, c, inner, outer))

    each(vb, residual2)
    f3 = [0.5 * four(q) for q in range(8)]

    def plus3(v):
        up = [lanes(c, 32) for c in v] + [zero]
        return [jnp.where(group < 3, up[q], up[q + 1]) for q in range(8)]

    def minus3(v):
        down = [zero] + [lanes(c, -32) for c in v]
        return [jnp.where(group > 0, down[q + 1], down[q]) for q in range(8)]

    level3 = Coarse(c3, plus3, minus3, above, below, row == 15, (row == 0) | (row == 15), 2)
    v3 = level3.sweep(level3.first(f3), f3)
    r3 = level3.residual(v3, f3)

    def restrict(values, x, y, zz):
        s = [t + lanes(t, x) for t in values]
        s = [y(t) for t in s]
        return [t + lanes(t, zz) for t in s]

    cores = lambda t: t[:8] + t[8:]
    f4 = [0.5 * s for s in restrict(r3, 32, cores, 2)]
    c4 = [0.125 * s for s in restrict(c3, 32, cores, 2)]
    zero8 = zero[:8]
    row8, lane8, group8 = row[:8], lane[:8], group[:8]

    def plus4(v):
        turn = [lanes(c, 64) for c in v] + [zero8]
        return [jnp.where(group8 < 2, turn[q], turn[q + 1]) for q in range(8)]

    def minus4(v):
        turn = [zero8] + [lanes(c, 64) for c in v]
        return [jnp.where(group8 < 2, turn[q], turn[q + 1]) for q in range(8)]

    def next_rows(n):
        return lambda c: rows(c, n)

    level4 = Coarse(
        c4, plus4, minus4, next_rows(1), next_rows(-1), row8 == 7, (row8 == 0) | (row8 == 7), 4
    )
    v4 = level4.sweep(level4.first(f4), f4)
    r4 = level4.residual(v4, f4)

    pair = lambda t: t + rows(t, 1)
    f5 = [0.5 * s for s in restrict(r4, 64, pair, 4)]
    c5 = [0.125 * s for s in restrict(c4, 64, pair, 4)]
    level5 = Coarse(
        c5,
        lambda v: v[1:] + [zero8],
        lambda v: [zero8] + v[:-1],
        next_rows(2),
        next_rows(-2),
        row8 >= 6,
        (row8 < 2) | (row8 >= 6),
        8,
    )
    v5 = level5.sweeps(level5.first(f5), f5, COARSE_SWEEPS - 1)

    def spread(c, bit):
        return jnp.where((iota(c.shape, 1) & bit) != 0, lanes(c, -bit), c)

    v5 = [jnp.where((row8 & 1) != 0, rows(c, -1), c) for c in v5]
    v4 = [c + spread(e, 4) for c, e in zip(v4, v5)]
    v4 = level4.sweeps(v4, f4, 2)

    v4 = [spread(jnp.where(group8 % 2 == 1, lanes(c, -32), c), 2) for c in v4]
    v3 = [c + jnp.concatenate([e, e], axis=0) for c, e in zip(v3, v4)]
    v3 = level3.sweeps(v3, f3, 2)

    for q in range(8):
        e3[q] = spread(v3[q], 1)
    for t in range(5):
        p = gx + t - 2
        inside = (p >= 0) & (p < 32)
        p = jnp.clip(p, 0, 31)
        e = jnp.where(group == jnp.where(inside, p % 4, -1), e3[p // 4], 0.0)
        va[gx + t - 2 + PAD] = vb[gx + t - 2 + PAD] + summed(e)

    def some(read, write, first, end):
        turned = [lanes(read[gx + t + PAD], 64) for t in range(first - 1, end + 1)]
        for u, t in enumerate(range(first, end)):
            i = gx + t + PAD
            outer = jnp.where(xl == 1, turned[u + 2], turned[u])
            write[i] = sweep2(i, read[i], turned[u + 1], outer)

    some(va, vb, -2, 3)
    some(vb, va, -1, 2)

    window = jnp.concatenate([va[gx + t + PAD] for t in range(-1, 2)], axis=1)
    shape = (ROWS, 16)
    column = 2 * (iota(shape, 1) % 8) + iota(shape, 1) // 8
    choose = jnp.where(column == gy - 1 + iota(shape, 0) // 8, 1.0, 0.0)
    window = jnp.dot(choose, window, precision=EXACT, preferred_element_type=jnp.float32)
    wide = jnp.concatenate([window[:, 128 * a : 128 * a + 128] for a in range(3)], axis=0)
    shape = (3 * ROWS, 128)
    wide = jnp.where((iota(shape, 1) // 32) % 2 == (iota(shape, 0) // 4) % 2, wide, 0.0)
    source_lane, target = iota((128, 256), 0), iota((128, 256), 1)
    place_it = (source_lane // 64 == target // 128) & (source_lane % 32 == (target % 128) // 4)
    wide = jnp.dot(
        wide, jnp.where(place_it, 1.0, 0.0), precision=EXACT, preferred_element_type=jnp.float32
    )

    def correction(i):
        a, x = (i + 4) // 4, ((i + 4) % 4) // 2
        return wide[ROWS * a : ROWS * a + ROWS, 128 * x : 128 * x + 128]

    middle = Window(2, (-2, 6))
    middle.weights(Stored(k1, -3))
    source = Stored(f1, -2)
    upper_half = iota((8, 128), 0) >= 4
    second = (iota((ROWS, 128), 0) & 2) != 0

    def received(i):
        n = 2 * i + 8
        c = [jnp.where(upper_half, r[n + 1 : n + 2], r[n : n + 1]) for r in (vlow, vmid, vhigh)]
        c = jnp.concatenate(c, axis=0)
        return jnp.where(second, lanes(c, 1), c)

    v = {i: received(i) + correction(i) for i in range(-3, 7)}
    v = middle.sweep(v, source, -2, 6)
    v = middle.sweep(v, source, -1, 5)

    odd_lane = iota((ROWS, 128), 1) % 2 == 1
    odd_row = iota((ROWS, 128), 0) % 2 == 1
    fine = Window(1, (-1, 9))
    fine.weights(Stored(k0, -2))
    source = Stored(f0, -1)
    base = Stored(v0, -2)
    spread1 = {}
    for i in range(-1, 5):
        c = jnp.where(odd_lane, lanes(v[i], -1), v[i])
        spread1[i] = jnp.where(odd_row, rows(c, -1), c)
    v = {i: base[i] + spread1[i // 2] for i in range(-2, 10)}
    v = fine.sweep(v, source, -1, 9)
    v = fine.sweep(v, source, 0, 8)
    for i in range(8):
        out[i] = v[i][8:16]


def f32(*shape):
    return jax.ShapeDtypeStruct(shape, jnp.float32)


def shift(x, axis, by):
    count = lax.axis_size(axis)
    return lax.ppermute(x, axis, [(i, i + by) for i in range(count) if 0 <= i + by < count])


def to_all(x, axis):
    copies = jnp.broadcast_to(x[None], (lax.axis_size(axis),) + x.shape)
    return lax.all_to_all(copies, axis, 0, 0)


def shards(right_side, coefficient, previous):
    gx, gy = lax.axis_index("gx"), lax.axis_index("gy")
    place = jnp.stack([gx, gy]).astype(jnp.int32)
    own = jnp.stack([right_side, coefficient, previous])
    mid = jnp.concatenate(
        [shift(own[:, -HALO:], "gx", 1), own, shift(own[:, :HALO], "gx", -1)], axis=1
    )
    low, high = shift(mid, "gy", 1), shift(mid, "gy", -1)

    params = pltpu.CompilerParams(vmem_limit_bytes=VMEM)
    scalars = pl.BlockSpec(memory_space=pltpu.SMEM)
    array = pl.BlockSpec(memory_space=pltpu.VMEM)
    packed, v0, k0, f0, k1, f1 = pl.pallas_call(
        down_kernel,
        in_specs=[array] * 3,
        out_shape=(
            f32(10, 128),
            f32(12, ROWS, 128),
            f32(12, ROWS, 128),
            f32(10, ROWS, 128),
            f32(10, ROWS, 128),
            f32(8, ROWS, 128),
        ),
        compiler_params=params,
        name="down",
    )(mid, low, high)

    blocks = to_all(packed.reshape(1, 1280), "gx")
    gathered = to_all(blocks[:, :, :256].reshape(64, 128), "gy").reshape(1024, 128)
    v1 = jnp.pad(blocks[:, 0, 256:], ((1, 1), (0, 0)))
    vmid = lax.dynamic_slice(v1, (gx, jnp.int32(0)), (3, 1024)).reshape(24, 128)
    vlow, vhigh = shift(vmid, "gy", 1), shift(vmid, "gy", -1)

    plane = pltpu.VMEM((32 + 2 * PAD, 16, 128), jnp.float32)
    return pl.pallas_call(
        up_kernel,
        in_specs=[scalars] + [array] * 9,
        out_shape=f32(8, 8, 128),
        scratch_shapes=[plane] * 12 + [pltpu.VMEM((8, 16, 128), jnp.float32)],
        compiler_params=params,
        name="up",
    )(place, gathered, v0, k0, f0, k1, f1, vmid, vlow, vhigh)


def solution(mesh):
    spec = P("gx", "gy", None)
    return jax.shard_map(
        shards, mesh=mesh, in_specs=(spec,) * 3, out_specs=spec, check_vma=False
    )
```

time: 442 us -> 83 us (0.19)
  the two profiles are of different devices: /device:TPU:195 before, /device:TPU:1 now
where the time goes in v1:
time: 83 us; the launch traced here: 82.5 us
  starting transfers between devices  33.4 us (40%)
  waiting for transfers between devices  18.9 us (23%)
  blocking collectives  17.9 us (22%)
  Pallas kernels  10.2 us (12%)
  local copies, waits for them, and re-layouts  1.05 us (1%)
  other arithmetic  0.9 us (1%)
    ppermute x6, starting transfers between devices, shift(): lax.ppermute(x, axis, [(i, i + by) for i in range(count) if 0 <= i + by <...  20 us
    all_to_all x1, blocking collectives, to_all(): return lax.all_to_all(copies, axis, 0, 0)  17.9 us
    ppermute x6, waiting for transfers between devices, shift(): lax.ppermute(x, axis, [(i, i + by) for i in range(count) if 0 <= i + by <...  15.8 us
    all_to_all x1, starting transfers between devices, to_all(): return lax.all_to_all(copies, axis, 0, 0)  13.4 us
    pallas_call x1, Pallas kernels, shards(): pl.pallas_call(up_kernel, in_specs=[scalars] + [array] * 9, out_shape=f32...  8.48 us
    all_to_all x1, waiting for transfers between devices, to_all(): return lax.all_to_all(copies, axis, 0, 0)  3.08 us
    pallas_call x1, Pallas kernels, shards(): pl.pallas_call(down_kernel, in_specs=[array] * 3, out_shape=(f32(10, 128)...  1.72 us
  transfers between devices with their start and end apart: 7, of which 6 were waited for; matrix products, arithmetic and copies ran while one was open for 0% of the time, Pallas kernels for 0%

profile of v1, /device:TPU:1, one launch (start us, length us, event | category | flops | bytes accessed | tf_op | source)
XLA Modules:
  0.0 82.5 jit_solution(9770732014816774811)
XLA Ops:
  0.0 0.8 pad_maximum_fusion.1
  0.8 0.0 copy-start.1
  0.8 0.0 copy-start.2
  0.8 4.0 %collective-permute-start = (f32[3,7,8,128]{3,2,1,0:T(8,128)S(1)}, f32[3,7,8,128]{3,2,1,0:T(8,128)S(1)}, u32[]{:S(2)}, u32[]{:S(2)}) collective-permute-start(f32[3,7,8,128]{3,2,1,0:T(8,128)S(1)} %get-tuple-element.17), channel_id=1, source_target_pairs={{0,16},{16,32},{32,48},{48,64},{64,80},{80,96},{96,112},{112,128},... | collective-permute-start | bytes 258056 | tf_op jit(solution)/shard_map/ppermute | solution.py:421
  4.9 1.3 %collective-permute-start.1 = (f32[3,7,8,128]{3,2,1,0:T(8,128)S(1)}, f32[3,7,8,128]{3,2,1,0:T(8,128)S(1)}, u32[]{:S(2)}, u32[]{:S(2)}) collective-permute-start(f32[3,7,8,128]{3,2,1,0:T(8,128)S(1)} %get-tuple-element.18), channel_id=1, source_target_pairs={{16,0},{32,16},{48,32},{64,48},{80,64},{96,80},{112,96},{128,112},... | collective-permute-start | bytes 258056 | tf_op jit(solution)/shard_map/ppermute | solution.py:421
  6.2 0.3 collective-permute-done
  6.5 3.6 %collective-permute-done.1 = f32[3,7,8,128]{3,2,1,0:T(8,128)S(1)} collective-permute-done((f32[3,7,8,128]{3,2,1,0:T(8,128)S(1)}, f32[3,7,8,128]{3,2,1,0:T(8,128)S(1)}, u32[]{:S(2)}, u32[]{:S(2)}) %collective-permute-start.1) | collective-permute-done | bytes 86048 | tf_op jit(solution)/shard_map/ppermute | solution.py:421
  10.1 0.0 copy-done.1
  10.2 7.2 %collective-permute-start.3 = (f32[3,22,8,128]{3,2,1,0:T(8,128)S(1)}, f32[3,22,8,128]{3,2,1,0:T(8,128)S(1)}, u32[]{:S(2)}, u32[]{:S(2)}) collective-permute-start(f32[3,22,8,128]{3,2,1,0:T(8,128)S(1)} %pad_maximum_fusion.mid), channel_id=1, source_target_pairs={{1,0},{2,1},{3,2},{4,3},{5,4},{6,5},{7,6},{8,7},{9,8},{10,9},{11,1... | collective-permute-start | bytes 811016 | tf_op jit(solution)/shard_map/ppermute | solution.py:421
  17.4 1.9 %collective-permute-start.2 = (f32[3,22,8,128]{3,2,1,0:T(8,128)S(1)}, f32[3,22,8,128]{3,2,1,0:T(8,128)S(1)}, u32[]{:S(2)}, u32[]{:S(2)}) collective-permute-start(f32[3,22,8,128]{3,2,1,0:T(8,128)S(1)} %pad_maximum_fusion.mid), channel_id=1, source_target_pairs={{0,1},{1,2},{2,3},{3,4},{4,5},{5,6},{6,7},{7,8},{8,9},{9,10},{10,1... | collective-permute-start | bytes 811016 | tf_op jit(solution)/shard_map/ppermute | solution.py:421
  19.3 1.0 %collective-permute-done.3.high = f32[3,22,8,128]{3,2,1,0:T(8,128)S(1)} collective-permute-done((f32[3,22,8,128]{3,2,1,0:T(8,128)S(1)}, f32[3,22,8,128]{3,2,1,0:T(8,128)S(1)}, u32[]{:S(2)}, u32[]{:S(2)}) %collective-permute-start.3) | collective-permute-done | bytes 270368 | tf_op jit(solution)/shard_map/ppermute | solution.py:421
  20.3 2.4 %collective-permute-done.2.low = f32[3,22,8,128]{3,2,1,0:T(8,128)S(1)} collective-permute-done((f32[3,22,8,128]{3,2,1,0:T(8,128)S(1)}, f32[3,22,8,128]{3,2,1,0:T(8,128)S(1)}, u32[]{:S(2)}, u32[]{:S(2)}) %collective-permute-start.2) | collective-permute-done | bytes 270368 | tf_op jit(solution)/shard_map/ppermute | solution.py:421
  22.7 1.7 %down.1 = (f32[10,128]{1,0:T(8,128)S(1)}, f32[12,24,128]{2,1,0:T(8,128)S(1)}, f32[12,24,128]{2,1,0:T(8,128)S(1)}, f32[10,24,128]{2,1,0:T(8,128)S(1)}, f32[10,24,...) custom-call(f32[3,22,8,128]{3,2,1,0:T(8,128)S(1)} %pad_maximum_fusion.mid, f32[3,22,8,128]{3,2,1,0:T(8,128)S(1)} %collective-permute-done.2.low, ...), custom_call_target="tpu_custom_call" | custom-call | tf_op jit(solution)/shard_map/down/pallas_call | solution.py:441
  24.4 0.1 broadcast_in_dim.15
  24.5 17.9 %all_to_all.10 = f32[32,1,1280]{2,1,0:T(1,128)S(1)} all-to-all(f32[32,1,1280]{2,1,0:T(1,128)S(1)} %broadcast_in_dim.15), channel_id=1, replica_groups=mesh['gx'=32,'gy'=16] {'gx'}, dimensions={0} | all-to-all | bytes 327680 | tf_op jit(solution)/shard_map/all_to_all | solution.py:426
  42.4 0.9 %broadcast_in_dim.17 = f32[16,64,128]{2,1,0:T(8,128)} broadcast(f32[64,128]{1,0:T(8,128)S(1)} %bitcast.14), dimensions={1,2} | broadcast | bytes 557056 | tf_op jit(solution)/shard_map/broadcast_in_dim | solution.py:425
  43.3 13.4 %all-to-all-start.1 = ((f32[16,64,128]{2,1,0:T(8,128)}), f32[16,64,128]{2,1,0:T(8,128)S(1)}, u32[]{:S(2)}, u32[]{:S(2)}) async-start(f32[16,64,128]{2,1,0:T(8,128)} %broadcast_in_dim.17), calls=%async_computation.1 | async-start | bytes 1048576 | tf_op jit(solution)/shard_map/all_to_all | solution.py:426
  56.7 2.0 %collective-permute-start.5 = (f32[24,128]{1,0:T(8,128)S(1)}, f32[24,128]{1,0:T(8,128)S(1)}, u32[]{:S(2)}, u32[]{:S(2)}) collective-permute-start(f32[24,128]{1,0:T(8,128)S(1)} %reshape.11.vmid), channel_id=1, source_target_pairs={{1,0},{2,1},{3,2},{4,3},{5,4},{6,5},{7,6},{8,7},{9,8},{10,9},{11,1... | collective-permute-start | bytes 36872 | tf_op jit(solution)/shard_map/ppermute | solution.py:421
  58.8 3.5 %collective-permute-start.4 = (f32[24,128]{1,0:T(8,128)S(1)}, f32[24,128]{1,0:T(8,128)S(1)}, u32[]{:S(2)}, u32[]{:S(2)}) collective-permute-start(f32[24,128]{1,0:T(8,128)S(1)} %reshape.11.vmid), channel_id=1, source_target_pairs={{0,1},{1,2},{2,3},{3,4},{4,5},{5,6},{6,7},{7,8},{8,9},{9,10},{10,1... | collective-permute-start | bytes 36872 | tf_op jit(solution)/shard_map/ppermute | solution.py:421
  62.3 0.1 pad_add_fusion.place
  62.4 8.5 %collective-permute-done.5.vhigh = f32[24,128]{1,0:T(8,128)S(1)} collective-permute-done((f32[24,128]{1,0:T(8,128)S(1)}, f32[24,128]{1,0:T(8,128)S(1)}, u32[]{:S(2)}, u32[]{:S(2)}) %collective-permute-start.5) | collective-permute-done | bytes 12320 | tf_op jit(solution)/shard_map/ppermute | solution.py:421
  70.9 0.0 collective-permute-done.4.vlow
  70.9 3.1 %all-to-all-done.1 = f32[16,64,128]{2,1,0:T(8,128)S(1)} async-done(((f32[16,64,128]{2,1,0:T(8,128)}), f32[16,64,128]{2,1,0:T(8,128)S(1)}, u32[]{:S(2)}, u32[]{:S(2)}) %all-to-all-start.1) | async-done | bytes 524320 | tf_op jit(solution)/shard_map/all_to_all | solution.py:426
  74.0 8.5 %up.1 = f32[8,8,128]{2,1,0:T(8,128)} custom-call(s32[2]{0:T(128)S(1)} %pad_add_fusion.place, f32[1024,128]{1,0:T(8,128)S(1)} %bitcast.11, f32[12,24,128]{2,1,0:T(8,128)S(1)} %get-tuple-element.12.v0, f32[12,24,128]{2,1,0:T(8,128)S(1)} %get-tuple-element.13.k0, f32[10,24,128]{2,1,0:T(8,128)S(1)} %get-tuple-element.14.f0, ...), custom_call_target="tpu_custom_call" | custom-call | tf_op jit(solution)/shard_map/up/pallas_call | solution.py:463
  (10 shorter events, 0.1 us)
Async XLA Ops:
  0.8 9.3 %copy-start = (f32[8,8,128]{2,1,0:T(8,128)S(1)}, f32[8,8,128]{2,1,0:T(8,128)}, u32[]{:S(2)}) copy-start(f32[8,8,128]{2,1,0:T(8,128)} %param.5) | copy-start | bytes 98308
  0.8 9.3 %copy-start.1 = (f32[8,8,128]{2,1,0:T(8,128)S(1)}, f32[8,8,128]{2,1,0:T(8,128)}, u32[]{:S(2)}) copy-start(f32[8,8,128]{2,1,0:T(8,128)} %param.4) | copy-start | bytes 98308
  0.8 9.3 %copy-start.2 = (f32[8,8,128]{2,1,0:T(8,128)S(1)}, f32[8,8,128]{2,1,0:T(8,128)}, u32[]{:S(2)}) copy-start(f32[8,8,128]{2,1,0:T(8,128)} %param.3) | copy-start | bytes 98308
  0.8 5.6 %collective-permute-start = (f32[3,7,8,128]{3,2,1,0:T(8,128)S(1)}, f32[3,7,8,128]{3,2,1,0:T(8,128)S(1)}, u32[]{:S(2)}, u32[]{:S(2)}) collective-permute-start(f32[3,7,8,128]{3,2,1,0:T(8,128)S(1)} %get-tuple-element.17), channel_id=1, source_target_pairs={{0,16},{16,32},{32,48},{48,64},{64,80},{80,96},{96,112},{112,128},... | collective-permute-start | bytes 258056 | tf_op jit(solution)/shard_map/ppermute | solution.py:421
  4.9 5.2 %collective-permute-start.1 = (f32[3,7,8,128]{3,2,1,0:T(8,128)S(1)}, f32[3,7,8,128]{3,2,1,0:T(8,128)S(1)}, u32[]{:S(2)}, u32[]{:S(2)}) collective-permute-start(f32[3,7,8,128]{3,2,1,0:T(8,128)S(1)} %get-tuple-element.18), channel_id=1, source_target_pairs={{16,0},{32,16},{48,32},{64,48},{80,64},{96,80},{112,96},{128,112},... | collective-permute-start | bytes 258056 | tf_op jit(solution)/shard_map/ppermute | solution.py:421
  10.2 10.1 %collective-permute-start.3 = (f32[3,22,8,128]{3,2,1,0:T(8,128)S(1)}, f32[3,22,8,128]{3,2,1,0:T(8,128)S(1)}, u32[]{:S(2)}, u32[]{:S(2)}) collective-permute-start(f32[3,22,8,128]{3,2,1,0:T(8,128)S(1)} %pad_maximum_fusion.mid), channel_id=1, source_target_pairs={{1,0},{2,1},{3,2},{4,3},{5,4},{6,5},{7,6},{8,7},{9,8},{10,9},{11,1... | collective-permute-start | bytes 811016 | tf_op jit(solution)/shard_map/ppermute | solution.py:421
  17.4 5.3 %collective-permute-start.2 = (f32[3,22,8,128]{3,2,1,0:T(8,128)S(1)}, f32[3,22,8,128]{3,2,1,0:T(8,128)S(1)}, u32[]{:S(2)}, u32[]{:S(2)}) collective-permute-start(f32[3,22,8,128]{3,2,1,0:T(8,128)S(1)} %pad_maximum_fusion.mid), channel_id=1, source_target_pairs={{0,1},{1,2},{2,3},{3,4},{4,5},{5,6},{6,7},{7,8},{8,9},{9,10},{10,1... | collective-permute-start | bytes 811016 | tf_op jit(solution)/shard_map/ppermute | solution.py:421
  43.3 30.7 %all-to-all-start.1 = ((f32[16,64,128]{2,1,0:T(8,128)}), f32[16,64,128]{2,1,0:T(8,128)S(1)}, u32[]{:S(2)}, u32[]{:S(2)}) async-start(f32[16,64,128]{2,1,0:T(8,128)} %broadcast_in_dim.17), calls=%async_computation.1 | async-start | bytes 1048576 | tf_op jit(solution)/shard_map/all_to_all | solution.py:426
  56.7 14.2 %collective-permute-start.5 = (f32[24,128]{1,0:T(8,128)S(1)}, f32[24,128]{1,0:T(8,128)S(1)}, u32[]{:S(2)}, u32[]{:S(2)}) collective-permute-start(f32[24,128]{1,0:T(8,128)S(1)} %reshape.11.vmid), channel_id=1, source_target_pairs={{1,0},{2,1},{3,2},{4,3},{5,4},{6,5},{7,6},{8,7},{9,8},{10,9},{11,1... | collective-permute-start | bytes 36872 | tf_op jit(solution)/shard_map/ppermute | solution.py:421
  58.8 12.1 %collective-permute-start.4 = (f32[24,128]{1,0:T(8,128)S(1)}, f32[24,128]{1,0:T(8,128)S(1)}, u32[]{:S(2)}, u32[]{:S(2)}) collective-permute-start(f32[24,128]{1,0:T(8,128)S(1)} %reshape.11.vmid), channel_id=1, source_target_pairs={{0,1},{1,2},{2,3},{3,4},{4,5},{5,6},{6,7},{7,8},{8,9},{9,10},{10,1... | collective-permute-start | bytes 36872 | tf_op jit(solution)/shard_map/ppermute | solution.py:421

commit v2 on v1

--- a/solution.py
+++ b/solution.py
@@ -11,7 +11,6 @@
 ROWS = 24
 COARSE_SWEEPS = 8
 VMEM = 48 * 1024 * 1024
-EXACT = lax.Precision.HIGHEST
 
 
 def lanes(x, n):
@@ -30,21 +29,33 @@
     def __init__(self, step, planes):
         self.step = step
         self.planes = planes
-        lane = iota((ROWS, 128), 1)
-        self.last = lane >= 128 - step
-        self.edge = (lane < step) | self.last
+
+    def given(self, wx, wy, wz, inv):
+        first = self.planes[0]
+        self.wx, self.wy = Stored(wx, first - 1), Stored(wy, first)
+        self.wz, self.inv = Stored(wz, first), Stored(inv, first)
+
+    def hand_on(self, planes, wx, wy, wz, inv):
+        first, end = planes
+        for i in range(first - 1, end):
+            wx[i - first + 1] = self.wx[i]
+        for i in range(first, end):
+            wy[i - first], wz[i - first], inv[i - first] = self.wy[i], self.wz[i], self.inv[i]
 
     def weights(self, coeff):
         first, end = self.planes
+        lane = iota((ROWS, 128), 1)
+        last = lane >= 128 - self.step
+        edge = (lane < self.step) | last
         self.wx, self.wy, self.wz, self.diag, self.inv = {}, {}, {}, {}, {}
         for i in range(first - 1, end):
             self.wx[i] = coeff[i] + coeff[i + 1]
         for i in range(first, end):
             k = coeff[i]
             wy = k + rows(k, self.step)
-            wz = jnp.where(self.last, 0.0, k + lanes(k, self.step))
+            wz = jnp.where(last, 0.0, k + lanes(k, self.step))
             diag = self.wx[i] + self.wx[i - 1] + (wy + rows(wy, -self.step))
-            diag = diag + (wz + lanes(wz, -self.step)) + jnp.where(self.edge, k, 0.0)
+            diag = diag + (wz + lanes(wz, -self.step)) + jnp.where(edge, k, 0.0)
             self.wy[i], self.wz[i], self.diag[i] = wy, wz, diag
             self.inv[i] = jnp.where(k > 0.0, RELAX / diag, 0.0)
 
@@ -81,7 +92,9 @@
     return s + lanes(s, step)
 
 
-def down_kernel(mid, low, high, packed, v0_out, k0_out, f0_out, k1_out, f1_out):
+def down_kernel(
+    mid, low, high, packed, v0_out, f0_out, f1_out, wx0, wy0, wz0, inv0, wx1, wy1, wz1, inv1
+):
     def field(which):
         return {
             i - HALO: jnp.concatenate([low[which, i], mid[which, i], high[which, i]], axis=0)
@@ -97,19 +110,18 @@
     v = fine.sweep(v, source, -5, 13)
     for i in range(-2, 10):
         v0_out[i + 2] = v[i]
-        k0_out[i + 2] = coeff[i]
     for i in range(-1, 9):
         f0_out[i + 1] = source[i]
+    fine.hand_on((-1, 9), wx0, wy0, wz0, inv0)
     r = fine.residual(v, source, -4, 12)
 
     source = {i: 0.5 * block_sum(r[2 * i], r[2 * i + 1], 1) for i in range(-2, 6)}
     coeff = {i: 0.125 * block_sum(coeff[2 * i], coeff[2 * i + 1], 1) for i in range(-3, 7)}
     for i in range(-2, 6):
         f1_out[i + 2] = source[i]
-    for i in range(-3, 7):
-        k1_out[i + 3] = coeff[i]
     middle = Window(2, (-2, 6))
     middle.weights(coeff)
+    middle.hand_on((-2, 6), wx1, wy1, wz1, inv1)
     v = {i: middle.inv[i] * source[i] for i in range(-2, 6)}
     v = middle.sweep(v, source, -1, 5)
     even = iota((8, 128), 1) % 2 == 0
@@ -122,14 +134,14 @@
 
     source = [0.5 * block_sum(r[2 * i], r[2 * i + 1], 2)[8:16] for i in range(2)]
     coeff = [0.125 * block_sum(coeff[2 * i], coeff[2 * i + 1], 2)[8:16] for i in range(2)]
-    table = jnp.concatenate(source + coeff, axis=0)
-    pick = jnp.where(iota((128, 128), 0) == 4 * (iota((128, 128), 1) % 32), 1.0, 0.0)
-    table = jnp.dot(table, pick, precision=EXACT, preferred_element_type=jnp.float32)
-    group = iota((16, 128), 1) // 32
-    chosen = iota((16, 128), 0) == 4 * group
-    for c in range(2):
-        one = jnp.where(chosen, table[16 * c : 16 * c + 16], 0.0)
-        packed[c : c + 1, :] = jnp.sum(one, axis=0, keepdims=True)
+    lane, row = iota((8, 128), 1), iota((8, 128), 0)
+    group = lane // 32
+    pick = 4 * (lane % 32)
+    for c, planes in enumerate((source, coeff)):
+        dense = [jnp.take_along_axis(t, pick, axis=1) for t in planes]
+        dense = jnp.where(group < 2, dense[0], dense[1])
+        dense = jnp.where(row == 4 * (group % 2), dense, 0.0)
+        packed[c : c + 1, :] = jnp.sum(dense, axis=0, keepdims=True)
 
 
 class Coarse:
@@ -182,13 +194,13 @@
     return jnp.concatenate([rows(c[8:], -1), c[:8]], axis=0)
 
 
-UNROLL = 8
+UNROLL = 10
 PAD = 3
 
 
 def up_kernel(
-    place, gathered, v0, k0, f0, k1, f1, vmid, vlow, vhigh, out,
-    k2, f2, va, vb, wxi, wxe, wyi, wye, wz2, diag2, inv2, sum2, e3,
+    place, gathered, v0, f0, f1, wx0, wy0, wz0, inv0, wx1, wy1, wz1, inv1, vlow, vmid, vhigh, out,
+    k2, f2, va, vb, wxi, wxe, wyi, wye, wz2, diag2, inv2, sumk, sumr, e3,
 ):
     gx, gy = place[0], place[1]
     lane = iota((16, 128), 1)
@@ -204,7 +216,7 @@
     for i in range(32):
         for c, ref in ((0, f2), (1, k2)):
             for core in range(2):
-                here = pl.ds(64 * core + 2 * i + c, 8, stride=128)
+                here = pl.ds(32 * i + 2 * core + c, 8, stride=4)
                 ref[i + PAD, 8 * core : 8 * core + 8] = gathered[here, :]
 
     def sides(c):
@@ -217,17 +229,11 @@
     zlast = z == 31
     zedge = zlast | (z == 0)
 
-    def each(field, body):
-        def steps(step, turned):
-            before, here = turned
-            for u in range(UNROLL):
-                i = PAD + UNROLL * step + u
-                after = lanes(field[i + 1], 64)
-                body(i, field[i], here, jnp.where(xl == 1, after, before))
-                before, here = here, after
-            return before, here
-
-        lax.fori_loop(0, 32 // UNROLL, steps, (zero, lanes(field[PAD], 64)))
+    def advance(i, field, turned, body):
+        before, here = turned
+        after = lanes(field[i + 1], 64)
+        body(i, field[i], here, jnp.where(xl == 1, after, before))
+        return here, after
 
     def summed(k):
         k = k + lanes(k, 64)
@@ -244,9 +250,7 @@
         inv = RELAX / diag
         wxi[i], wxe[i], wyi[i], wye[i], wz2[i], diag2[i], inv2[i] = a, b, c, e, w, diag, inv
         va[i] = inv * f2[i]
-        sum2[i] = summed(k)
-
-    each(k2, prepare)
+        sumk[i] = summed(k)
 
     def around2(i, c, inner, outer):
         yi, yo = sides(c)
@@ -261,20 +265,39 @@
     def first2(i, c, inner, outer):
         vb[i] = sweep2(i, c, inner, outer)
 
-    def four(q):
-        t = jnp.where(group == 0, sum2[4 * q + PAD], sum2[4 * q + PAD + 1])
-        t = jnp.where(group == 2, sum2[4 * q + PAD + 2], t)
-        t = jnp.where(group == 3, sum2[4 * q + PAD + 3], t)
+    def residual2(i, c, inner, outer):
+        sumr[i] = summed(f2[i] - diag2[i] * c + around2(i, c, inner, outer))
+
+    def three(i, state):
+        ofk, ofa, ofb = state
+        ofk = advance(i, k2, ofk, prepare)
+        ofa = advance(i - 1, va, ofa, first2)
+        return ofk, ofa, advance(i - 2, vb, ofb, residual2)
+
+    ofk = (zero, lanes(k2[PAD], 64))
+    ofk = advance(PAD, k2, ofk, prepare)
+    ofk = advance(PAD + 1, k2, ofk, prepare)
+    ofa = advance(PAD, va, (zero, lanes(va[PAD], 64)), first2)
+    ofb = (zero, lanes(vb[PAD], 64))
+
+    def steps(step, state):
+        for u in range(UNROLL):
+            state = three(PAD + 2 + UNROLL * step + u, state)
+        return state
+
+    _, ofa, ofb = lax.fori_loop(0, 30 // UNROLL, steps, (ofk, ofa, ofb))
+    advance(PAD + 31, va, ofa, first2)
+    ofb = advance(PAD + 30, vb, ofb, residual2)
+    advance(PAD + 31, vb, ofb, residual2)
+
+    def four(sums, q):
+        t = jnp.where(group == 0, sums[4 * q + PAD], sums[4 * q + PAD + 1])
+        t = jnp.where(group == 2, sums[4 * q + PAD + 2], t)
+        t = jnp.where(group == 3, sums[4 * q + PAD + 3], t)
         return t + lanes(t, 1)
 
-    c3 = [0.125 * four(q) for q in range(8)]
-    each(va, first2)
-
-    def residual2(i, c, inner, outer):
-        sum2[i] = summed(f2[i] - diag2[i] * c + around2(i, c, inner, outer))
-
-    each(vb, residual2)
-    f3 = [0.5 * four(q) for q in range(8)]
+    c3 = [0.125 * four(sumk, q) for q in range(8)]
+    f3 = [0.5 * four(sumr, q) for q in range(8)]
 
     def plus3(v):
         up = [lanes(c, 32) for c in v] + [zero]
@@ -361,33 +384,33 @@
     some(va, vb, -2, 3)
     some(vb, va, -1, 2)
 
-    window = jnp.concatenate([va[gx + t + PAD] for t in range(-1, 2)], axis=1)
-    shape = (ROWS, 16)
-    column = 2 * (iota(shape, 1) % 8) + iota(shape, 1) // 8
-    choose = jnp.where(column == gy - 1 + iota(shape, 0) // 8, 1.0, 0.0)
-    window = jnp.dot(choose, window, precision=EXACT, preferred_element_type=jnp.float32)
-    wide = jnp.concatenate([window[:, 128 * a : 128 * a + 128] for a in range(3)], axis=0)
-    shape = (3 * ROWS, 128)
-    wide = jnp.where((iota(shape, 1) // 32) % 2 == (iota(shape, 0) // 4) % 2, wide, 0.0)
-    source_lane, target = iota((128, 256), 0), iota((128, 256), 1)
-    place_it = (source_lane // 64 == target // 128) & (source_lane % 32 == (target % 128) // 4)
-    wide = jnp.dot(
-        wide, jnp.where(place_it, 1.0, 0.0), precision=EXACT, preferred_element_type=jnp.float32
-    )
+    lane8 = iota((8, 128), 1)
+    pick = 32 * (iota((8, 128), 0) // 4) + lane8 // 4
+    wide = {}
+    for t in range(-1, 2):
+        for x in range(2):
+            parts = []
+            for b in range(-1, 2):
+                y = gy + b
+                inside = (y >= 0) & (y < 16)
+                y = jnp.clip(y, 0, 15)
+                line = va[gx + t + PAD, pl.ds(8 * (y % 2) + y // 2, 1), :]
+                line = jnp.broadcast_to(jnp.where(inside, line, 0.0), (8, 128))
+                parts.append(jnp.take_along_axis(line, 64 * x + pick, axis=1))
+            wide[t, x] = jnp.concatenate(parts, axis=0)
 
     def correction(i):
-        a, x = (i + 4) // 4, ((i + 4) % 4) // 2
-        return wide[ROWS * a : ROWS * a + ROWS, 128 * x : 128 * x + 128]
+        return wide[i // 4, (i % 4) // 2]
 
     middle = Window(2, (-2, 6))
-    middle.weights(Stored(k1, -3))
+    middle.given(wx1, wy1, wz1, inv1)
     source = Stored(f1, -2)
     upper_half = iota((8, 128), 0) >= 4
     second = (iota((ROWS, 128), 0) & 2) != 0
 
     def received(i):
-        n = 2 * i + 8
-        c = [jnp.where(upper_half, r[n + 1 : n + 2], r[n : n + 1]) for r in (vlow, vmid, vhigh)]
+        r, n = (vlow, vmid, vhigh)[(i + 4) // 4], 2 * (i % 4)
+        c = [jnp.where(upper_half, r[b + 1 : b + 2], r[b : b + 1]) for b in (n, n + 8, n + 16)]
         c = jnp.concatenate(c, axis=0)
         return jnp.where(second, lanes(c, 1), c)
 
@@ -398,7 +421,7 @@
     odd_lane = iota((ROWS, 128), 1) % 2 == 1
     odd_row = iota((ROWS, 128), 0) % 2 == 1
     fine = Window(1, (-1, 9))
-    fine.weights(Stored(k0, -2))
+    fine.given(wx0, wy0, wz0, inv0)
     source = Stored(f0, -1)
     base = Stored(v0, -2)
     spread1 = {}
@@ -412,6 +435,9 @@
         out[i] = v[i][8:16]
 
 
+WINDOW_PLANES = (12, 10, 8, 11, 10, 10, 10, 9, 8, 8, 8)
+
+
 def f32(*shape):
     return jax.ShapeDtypeStruct(shape, jnp.float32)
 
@@ -438,36 +464,29 @@
     params = pltpu.CompilerParams(vmem_limit_bytes=VMEM)
     scalars = pl.BlockSpec(memory_space=pltpu.SMEM)
     array = pl.BlockSpec(memory_space=pltpu.VMEM)
-    packed, v0, k0, f0, k1, f1 = pl.pallas_call(
+    packed, *window = pl.pallas_call(
         down_kernel,
         in_specs=[array] * 3,
-        out_shape=(
-            f32(10, 128),
-            f32(12, ROWS, 128),
-            f32(12, ROWS, 128),
-            f32(10, ROWS, 128),
-            f32(10, ROWS, 128),
-            f32(8, ROWS, 128),
-        ),
+        out_shape=(f32(10, 128),) + tuple(f32(n, ROWS, 128) for n in WINDOW_PLANES),
         compiler_params=params,
         name="down",
     )(mid, low, high)
 
-    blocks = to_all(packed.reshape(1, 1280), "gx")
-    gathered = to_all(blocks[:, :, :256].reshape(64, 128), "gy").reshape(1024, 128)
+    blocks = to_all(packed.reshape(1, 1280), "gy")
+    gathered = to_all(blocks[:, :, :256].reshape(32, 128), "gx").reshape(1024, 128)
     v1 = jnp.pad(blocks[:, 0, 256:], ((1, 1), (0, 0)))
-    vmid = lax.dynamic_slice(v1, (gx, jnp.int32(0)), (3, 1024)).reshape(24, 128)
-    vlow, vhigh = shift(vmid, "gy", 1), shift(vmid, "gy", -1)
+    vmid = lax.dynamic_slice(v1, (gy, jnp.int32(0)), (3, 1024)).reshape(24, 128)
+    vlow, vhigh = shift(vmid, "gx", 1), shift(vmid, "gx", -1)
 
     plane = pltpu.VMEM((32 + 2 * PAD, 16, 128), jnp.float32)
     return pl.pallas_call(
         up_kernel,
-        in_specs=[scalars] + [array] * 9,
+        in_specs=[scalars] + [array] * (4 + len(WINDOW_PLANES)),
         out_shape=f32(8, 8, 128),
-        scratch_shapes=[plane] * 12 + [pltpu.VMEM((8, 16, 128), jnp.float32)],
+        scratch_shapes=[plane] * 13 + [pltpu.VMEM((8, 16, 128), jnp.float32)],
         compiler_params=params,
         name="up",
-    )(place, gathered, v0, k0, f0, k1, f1, vmid, vlow, vhigh)
+    )(place, gathered, *window, vlow, vmid, vhigh)
 
 
 def solution(mesh):

time: 83 us -> 79.2 us (0.954)
  the two profiles are of different devices: /device:TPU:1 before, /device:TPU:8 now
where the time goes in v2:
time: 79.2 us; the launch traced here: 78.7 us
  starting transfers between devices  29.6 us (37%)
  blocking collectives  22.5 us (28%)
  waiting for transfers between devices  15.6 us (20%)
  Pallas kernels  9.05 us (11%)
  local copies, waits for them, and re-layouts  1 us (1%)
  other arithmetic  0.89 us (1%)
    all_to_all x1, blocking collectives, to_all(): return lax.all_to_all(copies, axis, 0, 0)  22.5 us
    ppermute x6, starting transfers between devices, shift(): lax.ppermute(x, axis, [(i, i + by) for i in range(count) if 0 <= i + by <...  19.2 us
    all_to_all x1, starting transfers between devices, to_all(): return lax.all_to_all(copies, axis, 0, 0)  10.4 us
    ppermute x6, waiting for transfers between devices, shift(): lax.ppermute(x, axis, [(i, i + by) for i in range(count) if 0 <= i + by <...  10 us
    pallas_call x1, Pallas kernels, shards(): pl.pallas_call(up_kernel, in_specs=[scalars] + [array] * (4 + len(WINDOW_...  7.36 us
    all_to_all x1, waiting for transfers between devices, to_all(): return lax.all_to_all(copies, axis, 0, 0)  5.55 us
    pallas_call x1, Pallas kernels, shards(): pl.pallas_call(down_kernel, in_specs=[array] * 3, out_shape=(f32(10, 128)...  1.69 us
  transfers between devices with their start and end apart: 7, of which 5 were waited for; matrix products, arithmetic and copies ran while one was open for 0% of the time, Pallas kernels for 0%

profile of v2, /device:TPU:8, one launch (start us, length us, event | category | flops | bytes accessed | tf_op | source)
XLA Modules:
  0.0 78.7 jit_solution(14113593937910199720)
XLA Ops:
  0.0 0.8 %pad_maximum_fusion.1 = f32[3,8,8,128]{3,2,1,0:T(8,128)S(1)} fusion(f32[1,8,8,128]{3,2,1,0:T(8,128)} %bitcast.14, f32[1,8,8,128]{3,2,1,0:T(8,128)} %bitcast.16, f32[1,8,8,128]{3,2,1,0:T(8,128)} %bitcast.18), kind=kLoop, calls=%fused_computation.1 | loop fusion | flops 49152 | bytes 196608 | tf_op jit(solution)/shard_map/stack | solution.py:458
  0.8 0.0 copy-start.1
  0.8 0.0 copy-start.2
  0.8 3.5 %collective-permute-start = (f32[3,7,8,128]{3,2,1,0:T(8,128)S(1)}, f32[3,7,8,128]{3,2,1,0:T(8,128)S(1)}, u32[]{:S(2)}, u32[]{:S(2)}) collective-permute-start(f32[3,7,8,128]{3,2,1,0:T(8,128)S(1)} %get-tuple-element.29), channel_id=1, source_target_pairs={{0,16},{16,32},{32,48},{48,64},{64,80},{80,96},{96,112},{112,128},... | collective-permute-start | bytes 258056 | tf_op jit(solution)/shard_map/ppermute | solution.py:447
  4.3 5.5 %collective-permute-start.1 = (f32[3,7,8,128]{3,2,1,0:T(8,128)S(1)}, f32[3,7,8,128]{3,2,1,0:T(8,128)S(1)}, u32[]{:S(2)}, u32[]{:S(2)}) collective-permute-start(f32[3,7,8,128]{3,2,1,0:T(8,128)S(1)} %get-tuple-element.30), channel_id=1, source_target_pairs={{16,0},{32,16},{48,32},{64,48},{80,64},{96,80},{112,96},{128,112},... | collective-permute-start | bytes 258056 | tf_op jit(solution)/shard_map/ppermute | solution.py:447
  9.9 0.5 collective-permute-done
  10.4 1.6 %collective-permute-done.1 = f32[3,7,8,128]{3,2,1,0:T(8,128)S(1)} collective-permute-done((f32[3,7,8,128]{3,2,1,0:T(8,128)S(1)}, f32[3,7,8,128]{3,2,1,0:T(8,128)S(1)}, u32[]{:S(2)}, u32[]{:S(2)}) %collective-permute-start.1) | collective-permute-done | bytes 86048 | tf_op jit(solution)/shard_map/ppermute | solution.py:447
  12.0 0.0 copy-done
  12.0 0.0 copy-done.1
  12.0 1.3 %collective-permute-start.3 = (f32[3,22,8,128]{3,2,1,0:T(8,128)S(1)}, f32[3,22,8,128]{3,2,1,0:T(8,128)S(1)}, u32[]{:S(2)}, u32[]{:S(2)}) collective-permute-start(f32[3,22,8,128]{3,2,1,0:T(8,128)S(1)} %pad_maximum_fusion.mid), channel_id=1, source_target_pairs={{1,0},{2,1},{3,2},{4,3},{5,4},{6,5},{7,6},{8,7},{9,8},{10,9},{11,1... | collective-permute-start | bytes 811016 | tf_op jit(solution)/shard_map/ppermute | solution.py:447
  13.3 3.0 %collective-permute-start.2 = (f32[3,22,8,128]{3,2,1,0:T(8,128)S(1)}, f32[3,22,8,128]{3,2,1,0:T(8,128)S(1)}, u32[]{:S(2)}, u32[]{:S(2)}) collective-permute-start(f32[3,22,8,128]{3,2,1,0:T(8,128)S(1)} %pad_maximum_fusion.mid), channel_id=1, source_target_pairs={{0,1},{1,2},{2,3},{3,4},{4,5},{5,6},{6,7},{7,8},{8,9},{9,10},{10,1... | collective-permute-start | bytes 811016 | tf_op jit(solution)/shard_map/ppermute | solution.py:447
  16.4 0.0 collective-permute-done.3.high
  16.4 1.1 %collective-permute-done.2.low = f32[3,22,8,128]{3,2,1,0:T(8,128)S(1)} collective-permute-done((f32[3,22,8,128]{3,2,1,0:T(8,128)S(1)}, f32[3,22,8,128]{3,2,1,0:T(8,128)S(1)}, u32[]{:S(2)}, u32[]{:S(2)}) %collective-permute-start.2) | collective-permute-done | bytes 270368 | tf_op jit(solution)/shard_map/ppermute | solution.py:447
  17.5 1.7 %down.1 = (f32[10,128]{1,0:T(8,128)S(1)}, f32[12,24,128]{2,1,0:T(8,128)S(1)}, f32[10,24,128]{2,1,0:T(8,128)S(1)}, f32[8,24,128]{2,1,0:T(8,128)S(1)}, f32[11,24,1...) custom-call(f32[3,22,8,128]{3,2,1,0:T(8,128)S(1)} %pad_maximum_fusio, ...), custom_call_target="tpu_custom_call" | custom-call | tf_op jit(solution)/shard_map/down/pallas_call | solution.py:467
  19.2 22.5 %all_to_all.10 = f32[16,1,1280]{2,1,0:T(1,128)S(1)} all-to-all(f32[16,1,1280]{2,1,0:T(1,128)S(1)} %broadcast_in_dim.15), channel_id=1, replica_groups=mesh['gx'=32,'gy'=16] {'gy'}, dimensions={0} | all-to-all | bytes 163840 | tf_op jit(solution)/shard_map/all_to_all | solution.py:452
  41.7 0.9 %broadcast_in_dim.17 = f32[32,32,128]{2,1,0:T(8,128)} broadcast(f32[32,128]{1,0:T(8,128)S(1)} %bitcast.20), dimensions={1,2} | broadcast | bytes 540672 | tf_op jit(solution)/shard_map/broadcast_in_dim | solution.py:451
  42.6 10.4 %all-to-all-start.1 = ((f32[32,32,128]{2,1,0:T(8,128)}), f32[32,32,128]{2,1,0:T(8,128)S(1)}, u32[]{:S(2)}, u32[]{:S(2)}) async-start(f32[32,32,128]{2,1,0:T(8,128)} %broadcast_in_dim.17), calls=%async_computation.1 | async-start | bytes 1048576 | tf_op jit(solution)/shard_map/all_to_all | solution.py:452
  53.0 2.1 %collective-permute-start.5 = (f32[24,128]{1,0:T(8,128)S(1)}, f32[24,128]{1,0:T(8,128)S(1)}, u32[]{:S(2)}, u32[]{:S(2)}) collective-permute-start(f32[24,128]{1,0:T(8,128)S(1)} %reshape.11.vmid), channel_id=1, source_target_pairs={{16,0},{32,16},{48,32},{64,48},{80,64},{96,80},{112,96},{128,112},... | collective-permute-start | bytes 36872 | tf_op jit(solution)/shard_map/ppermute | solution.py:447
  55.2 3.7 %collective-permute-start.4 = (f32[24,128]{1,0:T(8,128)S(1)}, f32[24,128]{1,0:T(8,128)S(1)}, u32[]{:S(2)}, u32[]{:S(2)}) collective-permute-start(f32[24,128]{1,0:T(8,128)S(1)} %reshape.11.vmid), channel_id=1, source_target_pairs={{0,16},{16,32},{32,48},{48,64},{64,80},{80,96},{96,112},{112,128},... | collective-permute-start | bytes 36872 | tf_op jit(solution)/shard_map/ppermute | solution.py:447
  58.9 0.1 pad_add_fusion.place
  59.0 6.8 %collective-permute-done.5.vhigh = f32[24,128]{1,0:T(8,128)S(1)} collective-permute-done((f32[24,128]{1,0:T(8,128)S(1)}, f32[24,128]{1,0:T(8,128)S(1)}, u32[]{:S(2)}, u32[]{:S(2)}) %collective-permute-start.5) | collective-permute-done | bytes 12320 | tf_op jit(solution)/shard_map/ppermute | solution.py:447
  65.8 0.0 collective-permute-done.4.vlow
  65.8 5.6 %all-to-all-done.1 = f32[32,32,128]{2,1,0:T(8,128)S(1)} async-done(((f32[32,32,128]{2,1,0:T(8,128)}), f32[32,32,128]{2,1,0:T(8,128)S(1)}, u32[]{:S(2)}, u32[]{:S(2)}) %all-to-all-start.1) | async-done | bytes 524320 | tf_op jit(solution)/shard_map/all_to_all | solution.py:452
  71.3 7.4 %up.1 = f32[8,8,128]{2,1,0:T(8,128)} custom-call(s32[2]{0:T(128)S(1)} %pad_add_fusion.place, f32[1024,128]{1,0:T(8,128)S(1)} %bitcast.11, f32[12,24,128]{2,1,0:T(8,128)S(1)} %get-tuple-element.18.v0, f32[10,24,128]{2,1,0:T(8,128)S(1)} %get-tuple-element.19.f0, f32[8,24,128]{2,1,0:T(8,128)S(1)} %get-tuple-element.20.f1, ...), custom_call_target="tpu_custom_call" | custom-call | tf_op jit(solution)/shard_map/up/pallas_call | solution.py:482
  (10 shorter events, 0.1 us)
Async XLA Ops:
  0.8 11.2 %copy-start = (f32[8,8,128]{2,1,0:T(8,128)S(1)}, f32[8,8,128]{2,1,0:T(8,128)}, u32[]{:S(2)}) copy-start(f32[8,8,128]{2,1,0:T(8,128)} %param.5) | copy-start | bytes 98308
  0.8 11.2 %copy-start.1 = (f32[8,8,128]{2,1,0:T(8,128)S(1)}, f32[8,8,128]{2,1,0:T(8,128)}, u32[]{:S(2)}) copy-start(f32[8,8,128]{2,1,0:T(8,128)} %param.4) | copy-start | bytes 98308
  0.8 11.2 %copy-start.2 = (f32[8,8,128]{2,1,0:T(8,128)S(1)}, f32[8,8,128]{2,1,0:T(8,128)}, u32[]{:S(2)}) copy-start(f32[8,8,128]{2,1,0:T(8,128)} %param.3) | copy-start | bytes 98308
  0.8 9.6 %collective-permute-start = (f32[3,7,8,128]{3,2,1,0:T(8,128)S(1)}, f32[3,7,8,128]{3,2,1,0:T(8,128)S(1)}, u32[]{:S(2)}, u32[]{:S(2)}) collective-permute-start(f32[3,7,8,128]{3,2,1,0:T(8,128)S(1)} %get-tuple-element.29), channel_id=1, source_target_pairs={{0,16},{16,32},{32,48},{48,64},{64,80},{80,96},{96,112},{112,128},... | collective-permute-start | bytes 258056 | tf_op jit(solution)/shard_map/ppermute | solution.py:447
  4.3 7.6 %collective-permute-start.1 = (f32[3,7,8,128]{3,2,1,0:T(8,128)S(1)}, f32[3,7,8,128]{3,2,1,0:T(8,128)S(1)}, u32[]{:S(2)}, u32[]{:S(2)}) collective-permute-start(f32[3,7,8,128]{3,2,1,0:T(8,128)S(1)} %get-tuple-element.30), channel_id=1, source_target_pairs={{16,0},{32,16},{48,32},{64,48},{80,64},{96,80},{112,96},{128,112},... | collective-permute-start | bytes 258056 | tf_op jit(solution)/shard_map/ppermute | solution.py:447
  12.0 4.4 %collective-permute-start.3 = (f32[3,22,8,128]{3,2,1,0:T(8,128)S(1)}, f32[3,22,8,128]{3,2,1,0:T(8,128)S(1)}, u32[]{:S(2)}, u32[]{:S(2)}) collective-permute-start(f32[3,22,8,128]{3,2,1,0:T(8,128)S(1)} %pad_maximum_fusion.mid), channel_id=1, source_target_pairs={{1,0},{2,1},{3,2},{4,3},{5,4},{6,5},{7,6},{8,7},{9,8},{10,9},{11,1... | collective-permute-start | bytes 811016 | tf_op jit(solution)/shard_map/ppermute | solution.py:447
  13.3 4.2 %collective-permute-start.2 = (f32[3,22,8,128]{3,2,1,0:T(8,128)S(1)}, f32[3,22,8,128]{3,2,1,0:T(8,128)S(1)}, u32[]{:S(2)}, u32[]{:S(2)}) collective-permute-start(f32[3,22,8,128]{3,2,1,0:T(8,128)S(1)} %pad_maximum_fusion.mid), channel_id=1, source_target_pairs={{0,1},{1,2},{2,3},{3,4},{4,5},{5,6},{6,7},{7,8},{8,9},{9,10},{10,1... | collective-permute-start | bytes 811016 | tf_op jit(solution)/shard_map/ppermute | solution.py:447
  42.6 28.7 %all-to-all-start.1 = ((f32[32,32,128]{2,1,0:T(8,128)}), f32[32,32,128]{2,1,0:T(8,128)S(1)}, u32[]{:S(2)}, u32[]{:S(2)}) async-start(f32[32,32,128]{2,1,0:T(8,128)} %broadcast_in_dim.17), calls=%async_computation.1 | async-start | bytes 1048576 | tf_op jit(solution)/shard_map/all_to_all | solution.py:452
  53.0 12.7 %collective-permute-start.5 = (f32[24,128]{1,0:T(8,128)S(1)}, f32[24,128]{1,0:T(8,128)S(1)}, u32[]{:S(2)}, u32[]{:S(2)}) collective-permute-start(f32[24,128]{1,0:T(8,128)S(1)} %reshape.11.vmid), channel_id=1, source_target_pairs={{16,0},{32,16},{48,32},{64,48},{80,64},{96,80},{112,96},{128,112},... | collective-permute-start | bytes 36872 | tf_op jit(solution)/shard_map/ppermute | solution.py:447
  55.2 10.6 %collective-permute-start.4 = (f32[24,128]{1,0:T(8,128)S(1)}, f32[24,128]{1,0:T(8,128)S(1)}, u32[]{:S(2)}, u32[]{:S(2)}) collective-permute-start(f32[24,128]{1,0:T(8,128)S(1)} %reshape.11.vmid), channel_id=1, source_target_pairs={{0,16},{16,32},{32,48},{48,64},{64,80},{80,96},{96,112},{112,128},... | collective-permute-start | bytes 36872 | tf_op jit(solution)/shard_map/ppermute | solution.py:447

commit v3 on v2

--- a/solution.py
+++ b/solution.py
@@ -92,12 +92,23 @@
     return s + lanes(s, step)
 
 
+def core_mask(rows_of):
+    core = lax.rem(lax.axis_index("gy"), 2)
+    return jnp.broadcast_to(core, (rows_of, 128)) == 0
+
+
+def joined(first, mid, near, far):
+    return jnp.concatenate([jnp.where(first, far, near), mid, jnp.where(first, near, far)], axis=0)
+
+
 def down_kernel(
-    mid, low, high, packed, v0_out, f0_out, f1_out, wx0, wy0, wz0, inv0, wx1, wy1, wz1, inv1
+    mid, near, far, packed, v0_out, f0_out, f1_out, wx0, wy0, wz0, inv0, wx1, wy1, wz1, inv1
 ):
+    first = core_mask(8)
+
     def field(which):
         return {
-            i - HALO: jnp.concatenate([low[which, i], mid[which, i], high[which, i]], axis=0)
+            i - HALO: joined(first, mid[which, i], near[which, i], far[which, i])
             for i in range(mid.shape[1])
         }
 
@@ -199,10 +210,11 @@
 
 
 def up_kernel(
-    place, gathered, v0, f0, f1, wx0, wy0, wz0, inv0, wx1, wy1, wz1, inv1, vlow, vmid, vhigh, out,
+    mine, other, v0, f0, f1, wx0, wy0, wz0, inv0, wx1, wy1, wz1, inv1, vmid, vnear, vfar, out,
     k2, f2, va, vb, wxi, wxe, wyi, wye, wz2, diag2, inv2, sumk, sumr, e3,
 ):
-    gx, gy = place[0], place[1]
+    gx, gy = lax.axis_index("gx"), lax.axis_index("gy")
+    first = core_mask(8)
     lane = iota((16, 128), 1)
     row = iota((16, 128), 0)
     group, z = lane // 32, lane % 32
@@ -215,9 +227,10 @@
             ref[32 + PAD + i] = zero
     for i in range(32):
         for c, ref in ((0, f2), (1, k2)):
-            for core in range(2):
-                here = pl.ds(32 * i + 2 * core + c, 8, stride=4)
-                ref[i + PAD, 8 * core : 8 * core + 8] = gathered[here, :]
+            here = pl.ds(2 * i + c, 8, stride=64)
+            a, b = mine[here, :], other[here, :]
+            ref[i + PAD, :8] = jnp.where(first, a, b)
+            ref[i + PAD, 8:] = jnp.where(first, b, a)
 
     def sides(c):
         up, down = lanes(c, 32), lanes(c, -32)
@@ -409,9 +422,9 @@
     second = (iota((ROWS, 128), 0) & 2) != 0
 
     def received(i):
-        r, n = (vlow, vmid, vhigh)[(i + 4) // 4], 2 * (i % 4)
-        c = [jnp.where(upper_half, r[b + 1 : b + 2], r[b : b + 1]) for b in (n, n + 8, n + 16)]
-        c = jnp.concatenate(c, axis=0)
+        n = 2 * i + 8
+        c = [jnp.where(upper_half, r[n + 1 : n + 2], r[n : n + 1]) for r in (vmid, vnear, vfar)]
+        c = joined(first, *c)
         return jnp.where(second, lanes(c, 1), c)
 
     v = {i: received(i) + correction(i) for i in range(-3, 7)}
@@ -442,27 +455,27 @@
     return jax.ShapeDtypeStruct(shape, jnp.float32)
 
 
-def shift(x, axis, by):
-    count = lax.axis_size(axis)
-    return lax.ppermute(x, axis, [(i, i + by) for i in range(count) if 0 <= i + by < count])
-
-
-def to_all(x, axis):
-    copies = jnp.broadcast_to(x[None], (lax.axis_size(axis),) + x.shape)
-    return lax.all_to_all(copies, axis, 0, 0)
+def shift(x, by):
+    count = lax.axis_size("gx")
+    return lax.ppermute(x, "gx", [(i, i + by) for i in range(count) if 0 <= i + by < count])
+
+
+def swap(x, first):
+    pairs = [(i, i + 1) for i in range(first, lax.axis_size("gy") - 1, 2)]
+    return lax.ppermute(x, "gy", pairs + [(b, a) for a, b in pairs])
+
+
+def to_all(x, axis, count, groups=None):
+    copies = jnp.broadcast_to(x[None], (count,) + x.shape)
+    return lax.all_to_all(copies, axis, 0, 0, axis_index_groups=groups)
 
 
 def shards(right_side, coefficient, previous):
-    gx, gy = lax.axis_index("gx"), lax.axis_index("gy")
-    place = jnp.stack([gx, gy]).astype(jnp.int32)
     own = jnp.stack([right_side, coefficient, previous])
-    mid = jnp.concatenate(
-        [shift(own[:, -HALO:], "gx", 1), own, shift(own[:, :HALO], "gx", -1)], axis=1
-    )
-    low, high = shift(mid, "gy", 1), shift(mid, "gy", -1)
+    mid = jnp.concatenate([shift(own[:, -HALO:], 1), own, shift(own[:, :HALO], -1)], axis=1)
+    near, far = swap(mid, 0), swap(mid, 1)
 
     params = pltpu.CompilerParams(vmem_limit_bytes=VMEM)
-    scalars = pl.BlockSpec(memory_space=pltpu.SMEM)
     array = pl.BlockSpec(memory_space=pltpu.VMEM)
     packed, *window = pl.pallas_call(
         down_kernel,
@@ -470,23 +483,27 @@
         out_shape=(f32(10, 128),) + tuple(f32(n, ROWS, 128) for n in WINDOW_PLANES),
         compiler_params=params,
         name="down",
-    )(mid, low, high)
-
-    blocks = to_all(packed.reshape(1, 1280), "gy")
-    gathered = to_all(blocks[:, :, :256].reshape(32, 128), "gx").reshape(1024, 128)
+    )(mid, near, far)
+
+    blocks = to_all(packed.reshape(1, 1280), "gx", 32)
+    mine = to_all(
+        blocks[:, :, :256].reshape(64, 128), "gy", 8, [[2 * z + c for z in range(8)] for c in range(2)]
+    ).reshape(512, 128)
+    other = swap(mine, 0)
     v1 = jnp.pad(blocks[:, 0, 256:], ((1, 1), (0, 0)))
-    vmid = lax.dynamic_slice(v1, (gy, jnp.int32(0)), (3, 1024)).reshape(24, 128)
-    vlow, vhigh = shift(vmid, "gx", 1), shift(vmid, "gx", -1)
+    start = (lax.axis_index("gx"), jnp.int32(0))
+    vmid = lax.dynamic_slice(v1, start, (3, 1024)).reshape(24, 128)
+    vnear, vfar = swap(vmid, 0), swap(vmid, 1)
 
     plane = pltpu.VMEM((32 + 2 * PAD, 16, 128), jnp.float32)
     return pl.pallas_call(
         up_kernel,
-        in_specs=[scalars] + [array] * (4 + len(WINDOW_PLANES)),
+        in_specs=[array] * (5 + len(WINDOW_PLANES)),
         out_shape=f32(8, 8, 128),
         scratch_shapes=[plane] * 13 + [pltpu.VMEM((8, 16, 128), jnp.float32)],
         compiler_params=params,
         name="up",
-    )(place, gathered, *window, vlow, vmid, vhigh)
+    )(mine, other, *window, vmid, vnear, vfar)
 
 
 def solution(mesh):

time: 79.2 us -> 82.5 us (1.042)
  the two profiles are of different devices: /device:TPU:8 before, /device:TPU:1 now
where the time goes in v3:
time: 82.5 us; the launch traced here: 82.1 us
  blocking collectives  35.2 us (43%)
  starting transfers between devices  24.7 us (30%)
  waiting for transfers between devices  12.2 us (15%)
  Pallas kernels  8.72 us (11%)
    all_to_all x2, blocking collectives, to_all(): return lax.all_to_all(copies, axis, 0, 0, axis_index_groups=groups)  35.2 us
    ppermute x5, starting transfers between devices, swap(): return lax.ppermute(x, 'gy', pairs + [(b, a) for a, b in pairs])  19.4 us
    ppermute x5, waiting for transfers between devices, swap(): return lax.ppermute(x, 'gy', pairs + [(b, a) for a, b in pairs])  8.27 us
    pallas_call x1, Pallas kernels, shards(): pl.pallas_call(up_kernel, in_specs=[array] * (5 + len(WINDOW_PLANES)), ou...  7.08 us
    ppermute x2, starting transfers between devices, shift(): lax.ppermute(x, 'gx', [(i, i + by) for i in range(count) if 0 <= i + by <...  5.33 us
    ppermute x2, waiting for transfers between devices, shift(): lax.ppermute(x, 'gx', [(i, i + by) for i in range(count) if 0 <= i + by <...  3.93 us
  transfers between devices with their start and end apart: 7, of which 4 were waited for; matrix products, arithmetic and copies ran while one was open for 0% of the time, Pallas kernels for 0%

profile of v3, /device:TPU:1, one launch (start us, length us, event | category | flops | bytes accessed | tf_op | source)
XLA Modules:
  0.0 82.1 jit_solution(8251846272702811760)
XLA Ops:
  0.0 0.8 pad_maximum_fusion.1
  0.8 0.0 copy-start.1
  0.8 0.0 copy-start.2
  0.8 4.0 %collective-permute-start = (f32[3,7,8,128]{3,2,1,0:T(8,128)S(1)}, f32[3,7,8,128]{3,2,1,0:T(8,128)S(1)}, u32[]{:S(2)}, u32[]{:S(2)}) collective-permute-start(f32[3,7,8,128]{3,2,1,0:T(8,128)S(1)} %get-tuple-element.29), channel_id=1, source_target_pairs={{0,16},{16,32},{32,48},{48,64},{64,80},{80,96},{96,112},{112,128},... | collective-permute-start | bytes 258056 | tf_op jit(solution)/shard_map/ppermute | solution.py:460
  4.9 1.3 %collective-permute-start.1 = (f32[3,7,8,128]{3,2,1,0:T(8,128)S(1)}, f32[3,7,8,128]{3,2,1,0:T(8,128)S(1)}, u32[]{:S(2)}, u32[]{:S(2)}) collective-permute-start(f32[3,7,8,128]{3,2,1,0:T(8,128)S(1)} %get-tuple-element.30), channel_id=1, source_target_pairs={{16,0},{32,16},{48,32},{64,48},{80,64},{96,80},{112,96},{128,112},... | collective-permute-start | bytes 258056 | tf_op jit(solution)/shard_map/ppermute | solution.py:460
  6.2 0.3 collective-permute-done
  6.5 3.6 %collective-permute-done.1 = f32[3,7,8,128]{3,2,1,0:T(8,128)S(1)} collective-permute-done((f32[3,7,8,128]{3,2,1,0:T(8,128)S(1)}, f32[3,7,8,128]{3,2,1,0:T(8,128)S(1)}, u32[]{:S(2)}, u32[]{:S(2)}) %collective-permute-start.1) | collective-permute-done | bytes 86048 | tf_op jit(solution)/shard_map/ppermute | solution.py:460
  10.1 0.0 copy-done
  10.1 0.0 copy-done.1
  10.2 7.2 %collective-permute-start.2 = (f32[3,22,8,128]{3,2,1,0:T(8,128)S(1)}, f32[3,22,8,128]{3,2,1,0:T(8,128)S(1)}, u32[]{:S(2)}, u32[]{:S(2)}) collective-permute-start(f32[3,22,8,128]{3,2,1,0:T(8,128)S(1)} %pad_maximum_fusion.mid), channel_id=1, source_target_pairs={{0,1},{2,3},{4,5},{6,7},{8,9},{10,11},{12,13},{14,15},{1,0},{3,2},... | collective-permute-start | bytes 811016 | tf_op jit(solution)/shard_map/ppermute | solution.py:465
  17.4 1.9 %collective-permute-start.3 = (f32[3,22,8,128]{3,2,1,0:T(8,128)S(1)}, f32[3,22,8,128]{3,2,1,0:T(8,128)S(1)}, u32[]{:S(2)}, u32[]{:S(2)}) collective-permute-start(f32[3,22,8,128]{3,2,1,0:T(8,128)S(1)} %pad_maximum_fusion.mid), channel_id=1, source_target_pairs={{1,2},{3,4},{5,6},{7,8},{9,10},{11,12},{13,14},{2,1},{4,3},{6,5},{... | collective-permute-start | bytes 811016 | tf_op jit(solution)/shard_map/ppermute | solution.py:465
  19.3 0.0 collective-permute-done.2.near
  19.3 5.8 %collective-permute-done.3.far = f32[3,22,8,128]{3,2,1,0:T(8,128)S(1)} collective-permute-done((f32[3,22,8,128]{3,2,1,0:T(8,128)S(1)}, f32[3,22,8,128]{3,2,1,0:T(8,128)S(1)}, u32[]{:S(2)}, u32[]{:S(2)}) %collective-permute-start.3) | collective-permute-done | bytes 270368 | tf_op jit(solution)/shard_map/ppermute | solution.py:465
  25.1 1.6 %down.1 = (f32[10,128]{1,0:T(8,128)S(1)}, f32[12,24,128]{2,1,0:T(8,128)S(1)}, f32[10,24,128]{2,1,0:T(8,128)S(1)}, f32[8,24,128]{2,1,0:T(8,128)S(1)}, f32[11,24,1...) custom-call(f32[3,22,8,128]{3,2,1,0:T(8,128)S(1)} %pad_maximum_fusio, ...), custom_call_target="tpu_custom_call" | custom-call | tf_op jit(solution)/shard_map/down/pallas_call | solution.py:480
  26.8 0.1 broadcast_in_dim.15
  26.9 16.0 %all_to_all.10 = f32[32,1,1280]{2,1,0:T(1,128)S(1)} all-to-all(f32[32,1,1280]{2,1,0:T(1,128)S(1)} %broadcast_in_dim.15), channel_id=1, replica_groups=mesh['gx'=32,'gy'=16] {'gx'}, dimensions={0} | all-to-all | bytes 327680 | tf_op jit(solution)/shard_map/all_to_all | solution.py:470
  42.9 19.2 %all_to_all.11 = f32[8,64,128]{2,1,0:T(8,128)S(1)} all-to-all(f32[8,64,128]{2,1,0:T(8,128)S(1)} %broadcast_in_dim.17), channel_id=1, replica_groups={{0,2,4,6,8,10,12,14},{1,3,5,7,9,11,13,15},{16,18,20,22,24,26,28,30},{17..., dimensions={0} | all-to-all | bytes 524288 | tf_op jit(solution)/shard_map/all_to_all | solution.py:470
  62.2 5.8 %collective-permute-start.4 = (f32[512,128]{1,0:T(8,128)S(1)}, f32[512,128]{1,0:T(8,128)S(1)}, u32[]{:S(2)}, u32[]{:S(2)}) collective-permute-start(f32[512,128]{1,0:T(8,128)S(1)} %bitcast.9), channel_id=1, source_target_pairs={{0,1},{2,3},{4,5},{6,7},{8,9},{10,11},{12,13},{14,15},{1,0},{3,2},... | collective-permute-start | bytes 786440 | tf_op jit(solution)/shard_map/ppermute | solution.py:465
  68.1 1.9 %collective-permute-start.5 = (f32[24,128]{1,0:T(8,128)S(1)}, f32[24,128]{1,0:T(8,128)S(1)}, u32[]{:S(2)}, u32[]{:S(2)}) collective-permute-start(f32[24,128]{1,0:T(8,128)S(1)} %reshape.11.vmid), channel_id=1, source_target_pairs={{0,1},{2,3},{4,5},{6,7},{8,9},{10,11},{12,13},{14,15},{1,0},{3,2},... | collective-permute-start | bytes 36872 | tf_op jit(solution)/shard_map/ppermute | solution.py:465
  70.0 2.6 %collective-permute-start.6 = (f32[24,128]{1,0:T(8,128)S(1)}, f32[24,128]{1,0:T(8,128)S(1)}, u32[]{:S(2)}, u32[]{:S(2)}) collective-permute-start(f32[24,128]{1,0:T(8,128)S(1)} %reshape.11.vmid), channel_id=1, source_target_pairs={{1,2},{3,4},{5,6},{7,8},{9,10},{11,12},{13,14},{2,1},{4,3},{6,5},{... | collective-permute-start | bytes 36872 | tf_op jit(solution)/shard_map/ppermute | solution.py:465
  72.6 0.0 collective-permute-done.5.vnear
  72.6 2.4 %collective-permute-done.6.vfar = f32[24,128]{1,0:T(8,128)S(1)} collective-permute-done((f32[24,128]{1,0:T(8,128)S(1)}, f32[24,128]{1,0:T(8,128)S(1)}, u32[]{:S(2)}, u32[]{:S(2)}) %collective-permute-start.6) | collective-permute-done | bytes 12320 | tf_op jit(solution)/shard_map/ppermute | solution.py:465
  75.0 0.0 collective-permute-done.4.other
  75.0 7.1 %up.1 = f32[8,8,128]{2,1,0:T(8,128)} custom-call(f32[512,128]{1,0:T(8,128)S(1)} %bitcast.10, f32[512,128]{1,0:T(8,128)S(1)} %collective-permute-done.4.other, f32[12,24,128]{2,1,0:T(8,128)S(1)} %get-tuple-element.18.v0, f32[10,24,128]{2,1,0:T(8,128)S(1)} %get-tuple-element.19.f0, f32[8,24,128]{2,1,0:T(8,128)S(1)} %get-tuple-element.20.f1, ...), custom_call_target="tpu_custom_call" | custom-call | tf_op jit(solution)/shard_map/up/pallas_call | solution.py:499
  (10 shorter events, 0.1 us)
Async XLA Ops:
  0.8 9.3 %copy-start = (f32[8,8,128]{2,1,0:T(8,128)S(1)}, f32[8,8,128]{2,1,0:T(8,128)}, u32[]{:S(2)}) copy-start(f32[8,8,128]{2,1,0:T(8,128)} %param.5) | copy-start | bytes 98308
  0.8 9.3 %copy-start.1 = (f32[8,8,128]{2,1,0:T(8,128)S(1)}, f32[8,8,128]{2,1,0:T(8,128)}, u32[]{:S(2)}) copy-start(f32[8,8,128]{2,1,0:T(8,128)} %param.4) | copy-start | bytes 98308
  0.8 9.3 %copy-start.2 = (f32[8,8,128]{2,1,0:T(8,128)S(1)}, f32[8,8,128]{2,1,0:T(8,128)}, u32[]{:S(2)}) copy-start(f32[8,8,128]{2,1,0:T(8,128)} %param.3) | copy-start | bytes 98308
  0.8 5.6 %collective-permute-start = (f32[3,7,8,128]{3,2,1,0:T(8,128)S(1)}, f32[3,7,8,128]{3,2,1,0:T(8,128)S(1)}, u32[]{:S(2)}, u32[]{:S(2)}) collective-permute-start(f32[3,7,8,128]{3,2,1,0:T(8,128)S(1)} %get-tuple-element.29), channel_id=1, source_target_pairs={{0,16},{16,32},{32,48},{48,64},{64,80},{80,96},{96,112},{112,128},... | collective-permute-start | bytes 258056 | tf_op jit(solution)/shard_map/ppermute | solution.py:460
  4.9 5.2 %collective-permute-start.1 = (f32[3,7,8,128]{3,2,1,0:T(8,128)S(1)}, f32[3,7,8,128]{3,2,1,0:T(8,128)S(1)}, u32[]{:S(2)}, u32[]{:S(2)}) collective-permute-start(f32[3,7,8,128]{3,2,1,0:T(8,128)S(1)} %get-tuple-element.30), channel_id=1, source_target_pairs={{16,0},{32,16},{48,32},{64,48},{80,64},{96,80},{112,96},{128,112},... | collective-permute-start | bytes 258056 | tf_op jit(solution)/shard_map/ppermute | solution.py:460
  10.2 9.1 %collective-permute-start.2 = (f32[3,22,8,128]{3,2,1,0:T(8,128)S(1)}, f32[3,22,8,128]{3,2,1,0:T(8,128)S(1)}, u32[]{:S(2)}, u32[]{:S(2)}) collective-permute-start(f32[3,22,8,128]{3,2,1,0:T(8,128)S(1)} %pad_maximum_fusion.mid), channel_id=1, source_target_pairs={{0,1},{2,3},{4,5},{6,7},{8,9},{10,11},{12,13},{14,15},{1,0},{3,2},... | collective-permute-start | bytes 811016 | tf_op jit(solution)/shard_map/ppermute | solution.py:465
  17.4 7.8 %collective-permute-start.3 = (f32[3,22,8,128]{3,2,1,0:T(8,128)S(1)}, f32[3,22,8,128]{3,2,1,0:T(8,128)S(1)}, u32[]{:S(2)}, u32[]{:S(2)}) collective-permute-start(f32[3,22,8,128]{3,2,1,0:T(8,128)S(1)} %pad_maximum_fusion.mid), channel_id=1, source_target_pairs={{1,2},{3,4},{5,6},{7,8},{9,10},{11,12},{13,14},{2,1},{4,3},{6,5},{... | collective-permute-start | bytes 811016 | tf_op jit(solution)/shard_map/ppermute | solution.py:465
  62.2 12.8 %collective-permute-start.4 = (f32[512,128]{1,0:T(8,128)S(1)}, f32[512,128]{1,0:T(8,128)S(1)}, u32[]{:S(2)}, u32[]{:S(2)}) collective-permute-start(f32[512,128]{1,0:T(8,128)S(1)} %bitcast.9), channel_id=1, source_target_pairs={{0,1},{2,3},{4,5},{6,7},{8,9},{10,11},{12,13},{14,15},{1,0},{3,2},... | collective-permute-start | bytes 786440 | tf_op jit(solution)/shard_map/ppermute | solution.py:465
  68.1 4.5 %collective-permute-start.5 = (f32[24,128]{1,0:T(8,128)S(1)}, f32[24,128]{1,0:T(8,128)S(1)}, u32[]{:S(2)}, u32[]{:S(2)}) collective-permute-start(f32[24,128]{1,0:T(8,128)S(1)} %reshape.11.vmid), channel_id=1, source_target_pairs={{0,1},{2,3},{4,5},{6,7},{8,9},{10,11},{12,13},{14,15},{1,0},{3,2},... | collective-permute-start | bytes 36872 | tf_op jit(solution)/shard_map/ppermute | solution.py:465
  70.0 5.0 %collective-permute-start.6 = (f32[24,128]{1,0:T(8,128)S(1)}, f32[24,128]{1,0:T(8,128)S(1)}, u32[]{:S(2)}, u32[]{:S(2)}) collective-permute-start(f32[24,128]{1,0:T(8,128)S(1)} %reshape.11.vmid), channel_id=1, source_target_pairs={{1,2},{3,4},{5,6},{7,8},{9,10},{11,12},{13,14},{2,1},{4,3},{6,5},{... | collective-permute-start | bytes 36872 | tf_op jit(solution)/shard_map/ppermute | solution.py:465

commit v4 on v3

--- a/solution.py
+++ b/solution.py
@@ -210,7 +210,7 @@
 
 
 def up_kernel(
-    mine, other, v0, f0, f1, wx0, wy0, wz0, inv0, wx1, wy1, wz1, inv1, vmid, vnear, vfar, out,
+    gathered, v0, f0, f1, wx0, wy0, wz0, inv0, wx1, wy1, wz1, inv1, vmid, vnear, vfar, out,
     k2, f2, va, vb, wxi, wxe, wyi, wye, wz2, diag2, inv2, sumk, sumr, e3,
 ):
     gx, gy = lax.axis_index("gx"), lax.axis_index("gy")
@@ -227,10 +227,9 @@
             ref[32 + PAD + i] = zero
     for i in range(32):
         for c, ref in ((0, f2), (1, k2)):
-            here = pl.ds(2 * i + c, 8, stride=64)
-            a, b = mine[here, :], other[here, :]
-            ref[i + PAD, :8] = jnp.where(first, a, b)
-            ref[i + PAD, 8:] = jnp.where(first, b, a)
+            for core in range(2):
+                here = pl.ds(64 * core + 2 * i + c, 8, stride=128)
+                ref[i + PAD, 8 * core : 8 * core + 8] = gathered[here, :]
 
     def sides(c):
         up, down = lanes(c, 32), lanes(c, -32)
@@ -455,25 +454,24 @@
     return jax.ShapeDtypeStruct(shape, jnp.float32)
 
 
-def shift(x, by):
-    count = lax.axis_size("gx")
-    return lax.ppermute(x, "gx", [(i, i + by) for i in range(count) if 0 <= i + by < count])
-
-
-def swap(x, first):
-    pairs = [(i, i + 1) for i in range(first, lax.axis_size("gy") - 1, 2)]
-    return lax.ppermute(x, "gy", pairs + [(b, a) for a, b in pairs])
-
-
-def to_all(x, axis, count, groups=None):
-    copies = jnp.broadcast_to(x[None], (count,) + x.shape)
-    return lax.all_to_all(copies, axis, 0, 0, axis_index_groups=groups)
+def swap(x, axis, first):
+    pairs = [(i, i + 1) for i in range(first, lax.axis_size(axis) - 1, 2)]
+    return lax.ppermute(x, axis, pairs + [(b, a) for a, b in pairs])
+
+
+def to_all(x, axis):
+    copies = jnp.broadcast_to(x[None], (lax.axis_size(axis),) + x.shape)
+    return lax.all_to_all(copies, axis, 0, 0)
 
 
 def shards(right_side, coefficient, previous):
     own = jnp.stack([right_side, coefficient, previous])
-    mid = jnp.concatenate([shift(own[:, -HALO:], 1), own, shift(own[:, :HALO], -1)], axis=1)
-    near, far = swap(mid, 0), swap(mid, 1)
+    even = lax.axis_index("gx") % 2 == 0
+    start, end = own[:, :HALO], own[:, -HALO:]
+    near = swap(jnp.where(even, end, start), "gx", 0)
+    far = swap(jnp.where(even, start, end), "gx", 1)
+    mid = jnp.concatenate([jnp.where(even, far, near), own, jnp.where(even, near, far)], axis=1)
+    near, far = swap(mid, "gy", 0), swap(mid, "gy", 1)
 
     params = pltpu.CompilerParams(vmem_limit_bytes=VMEM)
     array = pl.BlockSpec(memory_space=pltpu.VMEM)
@@ -485,25 +483,22 @@
         name="down",
     )(mid, near, far)
 
-    blocks = to_all(packed.reshape(1, 1280), "gx", 32)
-    mine = to_all(
-        blocks[:, :, :256].reshape(64, 128), "gy", 8, [[2 * z + c for z in range(8)] for c in range(2)]
-    ).reshape(512, 128)
-    other = swap(mine, 0)
+    blocks = to_all(packed.reshape(1, 1280), "gx")
+    gathered = to_all(blocks[:, :, :256].reshape(64, 128), "gy").reshape(1024, 128)
     v1 = jnp.pad(blocks[:, 0, 256:], ((1, 1), (0, 0)))
-    start = (lax.axis_index("gx"), jnp.int32(0))
-    vmid = lax.dynamic_slice(v1, start, (3, 1024)).reshape(24, 128)
-    vnear, vfar = swap(vmid, 0), swap(vmid, 1)
+    place = (lax.axis_index("gx"), jnp.int32(0))
+    vmid = lax.dynamic_slice(v1, place, (3, 1024)).reshape(24, 128)
+    vnear, vfar = swap(vmid, "gy", 0), swap(vmid, "gy", 1)
 
     plane = pltpu.VMEM((32 + 2 * PAD, 16, 128), jnp.float32)
     return pl.pallas_call(
         up_kernel,
-        in_specs=[array] * (5 + len(WINDOW_PLANES)),
+        in_specs=[array] * (4 + len(WINDOW_PLANES)),
         out_shape=f32(8, 8, 128),
         scratch_shapes=[plane] * 13 + [pltpu.VMEM((8, 16, 128), jnp.float32)],
         compiler_params=params,
         name="up",
-    )(mine, other, *window, vmid, vnear, vfar)
+    )(gathered, *window, vmid, vnear, vfar)
 
 
 def solution(mesh):

time: 82.5 us -> 79.2 us (0.960)
  blocking collectives: 35.2 us -> 18.8 us
  starting transfers between devices: 24.7 us -> 32.5 us
  waiting for transfers between devices: 12.2 us -> 15.8 us
  local copies, waits for them, and re-layouts: 0.22 us -> 1.78 us
    all_to_all x2 -> x1, blocking collectives: 35.2 us -> 18.8 us  [to_all(): return lax.all_to_all(copies, axis, 0, 0)]
    all_to_all x0 -> x1, starting transfers between devices: none -> 12.2 us  [to_all(): return lax.all_to_all(copies, axis, 0, 0)]
    ppermute x7 -> x6, starting transfers between devices: 24.7 us -> 20.3 us  [swap(): return lax.ppermute(x, axis, pairs + [(b, a) for a, b in pairs])]
    all_to_all x0 -> x1, waiting for transfers between devices: none -> 3.08 us  [to_all(): return lax.all_to_all(copies, axis, 0, 0)]
    broadcast_in_dim x2, local copies, waits for them, and re-layouts: 0.11 us -> 0.93 us  [to_all(): copies = jnp.broadcast_to(x[None], (lax.axis_size(axis),) + x.shape)]
    ppermute x7 -> x6, waiting for transfers between devices: 12.2 us -> 12.7 us  [swap(): return lax.ppermute(x, axis, pairs + [(b, a) for a, b in pairs])]
where the time goes in v4:
time: 79.2 us; the launch traced here: 78.6 us
  starting transfers between devices  32.5 us (41%)
  blocking collectives  18.8 us (24%)
  waiting for transfers between devices  15.8 us (20%)
  Pallas kernels  8.68 us (11%)
  local copies, waits for them, and re-layouts  1.78 us (2%)
  other arithmetic  0.83 us (1%)
    ppermute x6, starting transfers between devices, swap(): return lax.ppermute(x, axis, pairs + [(b, a) for a, b in pairs])  20.3 us
    all_to_all x1, blocking collectives, to_all(): return lax.all_to_all(copies, axis, 0, 0)  18.8 us
    ppermute x6, waiting for transfers between devices, swap(): return lax.ppermute(x, axis, pairs + [(b, a) for a, b in pairs])  12.7 us
    all_to_all x1, starting transfers between devices, to_all(): return lax.all_to_all(copies, axis, 0, 0)  12.2 us
    pallas_call x1, Pallas kernels, shards(): pl.pallas_call(up_kernel, in_specs=[array] * (4 + len(WINDOW_PLANES)), ou...  7.05 us
    all_to_all x1, waiting for transfers between devices, to_all(): return lax.all_to_all(copies, axis, 0, 0)  3.08 us
    pallas_call x1, Pallas kernels, shards(): pl.pallas_call(down_kernel, in_specs=[array] * 3, out_shape=(f32(10, 128)...  1.63 us
  transfers between devices with their start and end apart: 7, of which 4 were waited for; matrix products, arithmetic and copies ran while one was open for 0% of the time, Pallas kernels for 0%

profile of v4, /device:TPU:1, one launch (start us, length us, event | category | flops | bytes accessed | tf_op | source)
XLA Modules:
  0.0 78.6 jit_solution(2438780426506981886)
XLA Ops:
  0.0 0.8 copy-done
  0.8 0.8 pad_maximum_fusion.1
  1.6 0.7 collective-permute-start
  2.2 0.0 copy-start.1
  2.2 0.0 copy-start.2
  2.3 6.6 %collective-permute-start.1 = (f32[3,7,8,128]{3,2,1,0:T(8,128)S(1)}, f32[3,7,8,128]{3,2,1,0:T(8,128)S(1)}, u32[]{:S(2)}, u32[]{:S(2)}) collective-permute-start(f32[3,7,8,128]{3,2,1,0:T(8,128)S(1)} %get-tuple-element.32), channel_id=1, source_target_pairs={{0,16},{32,48},{64,80},{96,112},{128,144},{160,176},{192,208},{224... | collective-permute-start | bytes 258056 | tf_op jit(solution)/shard_map/ppermute | solution.py:459
  8.8 0.0 collective-permute-done
  8.8 1.8 %collective-permute-done.1 = f32[3,7,8,128]{3,2,1,0:T(8,128)S(1)} collective-permute-done((f32[3,7,8,128]{3,2,1,0:T(8,128)S(1)}, f32[3,7,8,128]{3,2,1,0:T(8,128)S(1)}, u32[]{:S(2)}, u32[]{:S(2)}) %collective-permute-start.1) | collective-permute-done | bytes 86048 | tf_op jit(solution)/shard_map/ppermute | solution.py:459
  10.7 0.0 copy-done.1
  10.8 5.7 %collective-permute-start.3 = (f32[3,22,8,128]{3,2,1,0:T(8,128)S(1)}, f32[3,22,8,128]{3,2,1,0:T(8,128)S(1)}, u32[]{:S(2)}, u32[]{:S(2)}) collective-permute-start(f32[3,22,8,128]{3,2,1,0:T(8,128)S(1)} %pad_maximum_fusion.mid), channel_id=1, source_target_pairs={{1,2},{3,4},{5,6},{7,8},{9,10},{11,12},{13,14},{2,1},{4,3},{6,5},{... | collective-permute-start | bytes 811016 | tf_op jit(solution)/shard_map/ppermute | solution.py:459
  16.5 1.9 %collective-permute-start.2 = (f32[3,22,8,128]{3,2,1,0:T(8,128)S(1)}, f32[3,22,8,128]{3,2,1,0:T(8,128)S(1)}, u32[]{:S(2)}, u32[]{:S(2)}) collective-permute-start(f32[3,22,8,128]{3,2,1,0:T(8,128)S(1)} %pad_maximum_fusion.mid), channel_id=1, source_target_pairs={{0,1},{2,3},{4,5},{6,7},{8,9},{10,11},{12,13},{14,15},{1,0},{3,2},... | collective-permute-start | bytes 811016 | tf_op jit(solution)/shard_map/ppermute | solution.py:459
  18.4 2.2 %collective-permute-done.3.far = f32[3,22,8,128]{3,2,1,0:T(8,128)S(1)} collective-permute-done((f32[3,22,8,128]{3,2,1,0:T(8,128)S(1)}, f32[3,22,8,128]{3,2,1,0:T(8,128)S(1)}, u32[]{:S(2)}, u32[]{:S(2)}) %collective-permute-start.3) | collective-permute-done | bytes 270368 | tf_op jit(solution)/shard_map/ppermute | solution.py:459
  20.6 0.0 collective-permute-done.2.near
  20.6 1.6 %down.1 = (f32[10,128]{1,0:T(8,128)S(1)}, f32[12,24,128]{2,1,0:T(8,128)S(1)}, f32[10,24,128]{2,1,0:T(8,128)S(1)}, f32[8,24,128]{2,1,0:T(8,128)S(1)}, f32[11,24,1...) custom-call(f32[3,22,8,128]{3,2,1,0:T(8,128)S(1)} %pad_maximum_fusio, ...), custom_call_target="tpu_custom_call" | custom-call | tf_op jit(solution)/shard_map/down/pallas_call | solution.py:478
  22.3 0.1 broadcast_in_dim.15
  22.3 18.8 %all_to_all.10 = f32[32,1,1280]{2,1,0:T(1,128)S(1)} all-to-all(f32[32,1,1280]{2,1,0:T(1,128)S(1)} %broadcast_in_dim.15), channel_id=1, replica_groups=mesh['gx'=32,'gy'=16] {'gx'}, dimensions={0} | all-to-all | bytes 327680 | tf_op jit(solution)/shard_map/all_to_all | solution.py:464
  41.2 0.8 %broadcast_in_dim.17 = f32[16,64,128]{2,1,0:T(8,128)} broadcast(f32[64,128]{1,0:T(8,128)S(1)} %bitcast.12), dimensions={1,2} | broadcast | bytes 557056 | tf_op jit(solution)/shard_map/broadcast_in_dim | solution.py:463
  42.0 12.2 %all-to-all-start.1 = ((f32[16,64,128]{2,1,0:T(8,128)}), f32[16,64,128]{2,1,0:T(8,128)S(1)}, u32[]{:S(2)}, u32[]{:S(2)}) async-start(f32[16,64,128]{2,1,0:T(8,128)} %broadcast_in_dim.17), calls=%async_computation.1 | async-start | bytes 1048576 | tf_op jit(solution)/shard_map/all_to_all | solution.py:464
  54.3 3.5 %collective-permute-start.5 = (f32[24,128]{1,0:T(8,128)S(1)}, f32[24,128]{1,0:T(8,128)S(1)}, u32[]{:S(2)}, u32[]{:S(2)}) collective-permute-start(f32[24,128]{1,0:T(8,128)S(1)} %reshape.11.vmid), channel_id=1, source_target_pairs={{1,2},{3,4},{5,6},{7,8},{9,10},{11,12},{13,14},{2,1},{4,3},{6,5},{... | collective-permute-start | bytes 36872 | tf_op jit(solution)/shard_map/ppermute | solution.py:459
  57.9 1.9 %collective-permute-start.4 = (f32[24,128]{1,0:T(8,128)S(1)}, f32[24,128]{1,0:T(8,128)S(1)}, u32[]{:S(2)}, u32[]{:S(2)}) collective-permute-start(f32[24,128]{1,0:T(8,128)S(1)} %reshape.11.vmid), channel_id=1, source_target_pairs={{0,1},{2,3},{4,5},{6,7},{8,9},{10,11},{12,13},{14,15},{1,0},{3,2},... | collective-permute-start | bytes 36872 | tf_op jit(solution)/shard_map/ppermute | solution.py:459
  59.8 8.7 %collective-permute-done.5.vfar = f32[24,128]{1,0:T(8,128)S(1)} collective-permute-done((f32[24,128]{1,0:T(8,128)S(1)}, f32[24,128]{1,0:T(8,128)S(1)}, u32[]{:S(2)}, u32[]{:S(2)}) %collective-permute-start.5) | collective-permute-done | bytes 12320 | tf_op jit(solution)/shard_map/ppermute | solution.py:459
  68.5 0.0 collective-permute-done.4.vnear
  68.5 3.1 %all-to-all-done.1 = f32[16,64,128]{2,1,0:T(8,128)S(1)} async-done(((f32[16,64,128]{2,1,0:T(8,128)}), f32[16,64,128]{2,1,0:T(8,128)S(1)}, u32[]{:S(2)}, u32[]{:S(2)}) %all-to-all-start.1) | async-done | bytes 524320 | tf_op jit(solution)/shard_map/all_to_all | solution.py:464
  71.5 7.1 %up.1 = f32[8,8,128]{2,1,0:T(8,128)} custom-call(f32[1024,128]{1,0:T(8,128)S(1)} %bitcast.9, f32[12,24,128]{2,1,0:T(8,128)S(1)} %get-tuple-element.18.v0, f32[10,24,128]{2,1,0:T(8,128)S(1)} %get-tuple-element.19.f0, f32[8,24,128]{2,1,0:T(8,128)S(1)} %get-tuple-element.20.f1, f32[11,24,128]{2,1,0:T(8,128)S(1)} %get-tuple-element.21.wx0, ...), custom_call_target="tpu_custom_call" | custom-call | tf_op jit(solution)/shard_map/up/pallas_call | solution.py:494
  (10 shorter events, 0.1 us)
Async XLA Ops:
  0.0 0.8 copy-start
  1.6 7.3 %collective-permute-start = (f32[3,7,8,128]{3,2,1,0:T(8,128)S(1)}, f32[3,7,8,128]{3,2,1,0:T(8,128)S(1)}, u32[]{:S(2)}, u32[]{:S(2)}) collective-permute-start(f32[3,7,8,128]{3,2,1,0:T(8,128)S(1)} %get-tuple-element.31), channel_id=1, source_target_pairs={{16,32},{48,64},{80,96},{112,128},{144,160},{176,192},{208,224},{2... | collective-permute-start | bytes 258056 | tf_op jit(solution)/shard_map/ppermute | solution.py:459
  2.2 8.5 %copy-start.1 = (f32[8,8,128]{2,1,0:T(8,128)S(1)}, f32[8,8,128]{2,1,0:T(8,128)}, u32[]{:S(2)}) copy-start(f32[8,8,128]{2,1,0:T(8,128)} %param.4) | copy-start | bytes 98308
  2.2 8.5 %copy-start.2 = (f32[8,8,128]{2,1,0:T(8,128)S(1)}, f32[8,8,128]{2,1,0:T(8,128)}, u32[]{:S(2)}) copy-start(f32[8,8,128]{2,1,0:T(8,128)} %param.3) | copy-start | bytes 98308
  2.3 8.4 %collective-permute-start.1 = (f32[3,7,8,128]{3,2,1,0:T(8,128)S(1)}, f32[3,7,8,128]{3,2,1,0:T(8,128)S(1)}, u32[]{:S(2)}, u32[]{:S(2)}) collective-permute-start(f32[3,7,8,128]{3,2,1,0:T(8,128)S(1)} %get-tuple-element.32), channel_id=1, source_target_pairs={{0,16},{32,48},{64,80},{96,112},{128,144},{160,176},{192,208},{224... | collective-permute-start | bytes 258056 | tf_op jit(solution)/shard_map/ppermute | solution.py:459
  10.8 9.8 %collective-permute-start.3 = (f32[3,22,8,128]{3,2,1,0:T(8,128)S(1)}, f32[3,22,8,128]{3,2,1,0:T(8,128)S(1)}, u32[]{:S(2)}, u32[]{:S(2)}) collective-permute-start(f32[3,22,8,128]{3,2,1,0:T(8,128)S(1)} %pad_maximum_fusion.mid), channel_id=1, source_target_pairs={{1,2},{3,4},{5,6},{7,8},{9,10},{11,12},{13,14},{2,1},{4,3},{6,5},{... | collective-permute-start | bytes 811016 | tf_op jit(solution)/shard_map/ppermute | solution.py:459
  16.5 4.1 %collective-permute-start.2 = (f32[3,22,8,128]{3,2,1,0:T(8,128)S(1)}, f32[3,22,8,128]{3,2,1,0:T(8,128)S(1)}, u32[]{:S(2)}, u32[]{:S(2)}) collective-permute-start(f32[3,22,8,128]{3,2,1,0:T(8,128)S(1)} %pad_maximum_fusion.mid), channel_id=1, source_target_pairs={{0,1},{2,3},{4,5},{6,7},{8,9},{10,11},{12,13},{14,15},{1,0},{3,2},... | collective-permute-start | bytes 811016 | tf_op jit(solution)/shard_map/ppermute | solution.py:459
  42.0 29.5 %all-to-all-start.1 = ((f32[16,64,128]{2,1,0:T(8,128)}), f32[16,64,128]{2,1,0:T(8,128)S(1)}, u32[]{:S(2)}, u32[]{:S(2)}) async-start(f32[16,64,128]{2,1,0:T(8,128)} %broadcast_in_dim.17), calls=%async_computation.1 | async-start | bytes 1048576 | tf_op jit(solution)/shard_map/all_to_all | solution.py:464
  54.3 14.2 %collective-permute-start.5 = (f32[24,128]{1,0:T(8,128)S(1)}, f32[24,128]{1,0:T(8,128)S(1)}, u32[]{:S(2)}, u32[]{:S(2)}) collective-permute-start(f32[24,128]{1,0:T(8,128)S(1)} %reshape.11.vmid), channel_id=1, source_target_pairs={{1,2},{3,4},{5,6},{7,8},{9,10},{11,12},{13,14},{2,1},{4,3},{6,5},{... | collective-permute-start | bytes 36872 | tf_op jit(solution)/shard_map/ppermute | solution.py:459
  57.9 10.6 %collective-permute-start.4 = (f32[24,128]{1,0:T(8,128)S(1)}, f32[24,128]{1,0:T(8,128)S(1)}, u32[]{:S(2)}, u32[]{:S(2)}) collective-permute-start(f32[24,128]{1,0:T(8,128)S(1)} %reshape.11.vmid), channel_id=1, source_target_pairs={{0,1},{2,3},{4,5},{6,7},{8,9},{10,11},{12,13},{14,15},{1,0},{3,2},... | collective-permute-start | bytes 36872 | tf_op jit(solution)/shard_map/ppermute | solution.py:459

commit v5 on v4

--- a/solution.py
+++ b/solution.py
@@ -102,7 +102,7 @@
 
 
 def down_kernel(
-    mid, near, far, packed, v0_out, f0_out, f1_out, wx0, wy0, wz0, inv0, wx1, wy1, wz1, inv1
+    mid, near, far, packed, v1_out, v0_out, f0_out, f1_out, wx0, wy0, wz0, inv0, wx1, wy1, wz1, inv1
 ):
     first = core_mask(8)
 
@@ -139,8 +139,8 @@
     for i in range(4):
         c = v[i][8:16]
         c = jnp.where(even, c, lanes(rows(c, 2), -1))
-        packed[2 * i + 2 : 2 * i + 3, :] = c[0:1]
-        packed[2 * i + 3 : 2 * i + 4, :] = c[4:5]
+        v1_out[2 * i : 2 * i + 1, :] = c[0:1]
+        v1_out[2 * i + 1 : 2 * i + 2, :] = c[4:5]
     r = middle.residual(v, source, 0, 4)
 
     source = [0.5 * block_sum(r[2 * i], r[2 * i + 1], 2)[8:16] for i in range(2)]
@@ -190,7 +190,7 @@
 
     def sweeps(self, v, source, count):
         step = lambda _, v: tuple(self.sweep(list(v), source))
-        return list(lax.fori_loop(0, count, step, tuple(v)))
+        return list(lax.fori_loop(0, count, step, tuple(v), unroll=True))
 
     def residual(self, v, source):
         around = self.around(v)
@@ -465,29 +465,30 @@
 
 
 def shards(right_side, coefficient, previous):
-    own = jnp.stack([right_side, coefficient, previous])
     even = lax.axis_index("gx") % 2 == 0
+    own = lax.optimization_barrier(jnp.stack([right_side, coefficient, previous]))
     start, end = own[:, :HALO], own[:, -HALO:]
     near = swap(jnp.where(even, end, start), "gx", 0)
     far = swap(jnp.where(even, start, end), "gx", 1)
-    mid = jnp.concatenate([jnp.where(even, far, near), own, jnp.where(even, near, far)], axis=1)
+
+    def around(near, own, far, axis):
+        return jnp.concatenate([jnp.where(even, far, near), own, jnp.where(even, near, far)], axis=axis)
+
+    mid = around(near, own, far, 1)
     near, far = swap(mid, "gy", 0), swap(mid, "gy", 1)
 
     params = pltpu.CompilerParams(vmem_limit_bytes=VMEM)
     array = pl.BlockSpec(memory_space=pltpu.VMEM)
-    packed, *window = pl.pallas_call(
+    packed, v1, *window = pl.pallas_call(
         down_kernel,
         in_specs=[array] * 3,
-        out_shape=(f32(10, 128),) + tuple(f32(n, ROWS, 128) for n in WINDOW_PLANES),
+        out_shape=(f32(2, 128), f32(8, 128)) + tuple(f32(n, ROWS, 128) for n in WINDOW_PLANES),
         compiler_params=params,
         name="down",
     )(mid, near, far)
 
-    blocks = to_all(packed.reshape(1, 1280), "gx")
-    gathered = to_all(blocks[:, :, :256].reshape(64, 128), "gy").reshape(1024, 128)
-    v1 = jnp.pad(blocks[:, 0, 256:], ((1, 1), (0, 0)))
-    place = (lax.axis_index("gx"), jnp.int32(0))
-    vmid = lax.dynamic_slice(v1, place, (3, 1024)).reshape(24, 128)
+    gathered = to_all(to_all(packed, "gx").reshape(64, 128), "gy").reshape(1024, 128)
+    vmid = around(swap(v1, "gx", 0), v1, swap(v1, "gx", 1), 0)
     vnear, vfar = swap(vmid, "gy", 0), swap(vmid, "gy", 1)
 
     plane = pltpu.VMEM((32 + 2 * PAD, 16, 128), jnp.float32)

time: 79.2 us -> 79.4 us (level)
  starting transfers between devices: 32.5 us -> 39.4 us
  blocking collectives: 18.8 us -> 14.9 us
  waiting for transfers between devices: 15.8 us -> 14.1 us
  local copies, waits for them, and re-layouts: 1.78 us -> 0.86 us
    ppermute x6 -> x8, starting transfers between devices: 20.3 us -> 26.7 us  [swap(): return lax.ppermute(x, axis, pairs + [(b, a) for a, b in pairs])]
    all_to_all x1, blocking collectives: 18.8 us -> 14.9 us  [to_all(): return lax.all_to_all(copies, axis, 0, 0)]
    ppermute x6 -> x8, waiting for transfers between devices: 12.7 us -> 11 us  [swap(): return lax.ppermute(x, axis, pairs + [(b, a) for a, b in pairs])]
    unnamed x7 -> x0, local copies, waits for them, and re-layouts: 0.8 us -> none
  transfers between devices with their start and end apart: 7 -> 9, of which waited for: 4 -> 5; matrix products, arithmetic and copies ran while one was open for 0% -> 0% of each run, Pallas kernels for 0% -> 0%
where the time goes in v5:
time: 79.4 us; the launch traced here: 78.9 us
  starting transfers between devices  39.4 us (50%)
  blocking collectives  14.9 us (19%)
  waiting for transfers between devices  14.1 us (18%)
  Pallas kernels  8.56 us (11%)
  other arithmetic  0.86 us (1%)
  local copies, waits for them, and re-layouts  0.86 us (1%)
    ppermute x8, starting transfers between devices, swap(): return lax.ppermute(x, axis, pairs + [(b, a) for a, b in pairs])  26.7 us
    all_to_all x1, blocking collectives, to_all(): return lax.all_to_all(copies, axis, 0, 0)  14.9 us
    all_to_all x1, starting transfers between devices, to_all(): return lax.all_to_all(copies, axis, 0, 0)  12.7 us
    ppermute x8, waiting for transfers between devices, swap(): return lax.ppermute(x, axis, pairs + [(b, a) for a, b in pairs])  11 us
    pallas_call x1, Pallas kernels, shards(): pl.pallas_call(up_kernel, in_specs=[array] * (4 + len(WINDOW_PLANES)), ou...  6.93 us
    all_to_all x1, waiting for transfers between devices, to_all(): return lax.all_to_all(copies, axis, 0, 0)  3.09 us
    pallas_call x1, Pallas kernels, shards(): pl.pallas_call(down_kernel, in_specs=[array] * 3, out_shape=(f32(2, 128),...  1.63 us
  transfers between devices with their start and end apart: 9, of which 5 were waited for; matrix products, arithmetic and copies ran while one was open for 0% of the time, Pallas kernels for 0%

profile of v5, /device:TPU:1, one launch (start us, length us, event | category | flops | bytes accessed | tf_op | source)
XLA Modules:
  0.0 78.9 jit_solution(18313535690853969512)
XLA Ops:
  0.0 0.8 %pad_maximum_fusion.1 = f32[3,8,8,128]{3,2,1,0:T(8,128)S(1)} fusion(f32[1,8,8,128]{3,2,1,0:T(8,128)} %bitcast.7, f32[1,8,8,128]{3,2,1,0:T(8,128)} %bitcast.8, f32[1,8,8,128]{3,2,1,0:T(8,128)} %bitcast.9), kind=kLoop, calls=%fused_computation.1 | loop fusion | flops 49152 | bytes 196608 | tf_op jit(solution)/shard_map/stack | solution.py:469
  0.8 0.7 collective-permute-start
  1.5 6.6 %collective-permute-start.1 = (f32[3,7,8,128]{3,2,1,0:T(8,128)S(1)}, f32[3,7,8,128]{3,2,1,0:T(8,128)S(1)}, u32[]{:S(2)}, u32[]{:S(2)}) collective-permute-start(f32[3,7,8,128]{3,2,1,0:T(8,128)S(1)} %get-tuple-element.34), channel_id=1, source_target_pairs={{0,16},{32,48},{64,80},{96,112},{128,144},{160,176},{192,208},{224... | collective-permute-start | bytes 258056 | tf_op jit(solution)/shard_map/ppermute | solution.py:459
  8.1 0.0 collective-permute-done
  8.1 1.8 %collective-permute-done.1 = f32[3,7,8,128]{3,2,1,0:T(8,128)S(1)} collective-permute-done((f32[3,7,8,128]{3,2,1,0:T(8,128)S(1)}, f32[3,7,8,128]{3,2,1,0:T(8,128)S(1)}, u32[]{:S(2)}, u32[]{:S(2)}) %collective-permute-start.1) | collective-permute-done | bytes 86048 | tf_op jit(solution)/shard_map/ppermute | solution.py:459
  10.0 6.7 %collective-permute-start.2 = (f32[3,22,8,128]{3,2,1,0:T(8,128)S(1)}, f32[3,22,8,128]{3,2,1,0:T(8,128)S(1)}, u32[]{:S(2)}, u32[]{:S(2)}) collective-permute-start(f32[3,22,8,128]{3,2,1,0:T(8,128)S(1)} %pad_maximum_fusion.mid), channel_id=1, source_target_pairs={{0,1},{2,3},{4,5},{6,7},{8,9},{10,11},{12,13},{14,15},{1,0},{3,2},... | collective-permute-start | bytes 811016 | tf_op jit(solution)/shard_map/ppermute | solution.py:459
  16.7 1.9 %collective-permute-start.3 = (f32[3,22,8,128]{3,2,1,0:T(8,128)S(1)}, f32[3,22,8,128]{3,2,1,0:T(8,128)S(1)}, u32[]{:S(2)}, u32[]{:S(2)}) collective-permute-start(f32[3,22,8,128]{3,2,1,0:T(8,128)S(1)} %pad_maximum_fusion.mid), channel_id=1, source_target_pairs={{1,2},{3,4},{5,6},{7,8},{9,10},{11,12},{13,14},{2,1},{4,3},{6,5},{... | collective-permute-start | bytes 811016 | tf_op jit(solution)/shard_map/ppermute | solution.py:459
  18.6 0.0 collective-permute-done.2.near
  18.6 5.8 %collective-permute-done.3.far = f32[3,22,8,128]{3,2,1,0:T(8,128)S(1)} collective-permute-done((f32[3,22,8,128]{3,2,1,0:T(8,128)S(1)}, f32[3,22,8,128]{3,2,1,0:T(8,128)S(1)}, u32[]{:S(2)}, u32[]{:S(2)}) %collective-permute-start.3) | collective-permute-done | bytes 270368 | tf_op jit(solution)/shard_map/ppermute | solution.py:459
  24.5 1.6 %down.1 = (f32[2,128]{1,0:T(2,128)S(1)}, f32[8,128]{1,0:T(8,128)S(1)}, f32[12,24,128]{2,1,0:T(8,128)S(1)}, f32[10,24,128]{2,1,0:T(8,128)S(1)}, f32[8,24,128]{2,1...) custom-call(f32[3,22,8,128]{3,2,1,0:T(8,128)S(1)} %pad_maximum_fusio, ...), custom_call_target="tpu_custom_call" | custom-call | tf_op jit(solution)/shard_map/down/pallas_call | solution.py:482
  26.1 14.9 %all_to_all.10 = f32[32,2,128]{2,1,0:T(2,128)S(1)} all-to-all(f32[32,2,128]{2,1,0:T(2,128)S(1)} %broadcast_in_dim.6), channel_id=1, replica_groups=mesh['gx'=32,'gy'=16] {'gx'}, dimensions={0} | all-to-all | bytes 65536 | tf_op jit(solution)/shard_map/all_to_all | solution.py:464
  41.1 0.8 %broadcast_in_dim.15 = f32[16,64,128]{2,1,0:T(8,128)} broadcast(f32[64,128]{1,0:T(8,128)S(1)} %bitcast.6), dimensions={1,2} | broadcast | bytes 557056 | tf_op jit(solution)/shard_map/broadcast_in_dim | solution.py:463
  41.9 12.7 %all-to-all-start.1 = ((f32[16,64,128]{2,1,0:T(8,128)}), f32[16,64,128]{2,1,0:T(8,128)S(1)}, u32[]{:S(2)}, u32[]{:S(2)}) async-start(f32[16,64,128]{2,1,0:T(8,128)} %broadcast_in_dim.15), calls=%async_computation.1 | async-start | bytes 1048576 | tf_op jit(solution)/shard_map/all_to_all | solution.py:464
  54.6 0.6 collective-permute-start.4
  55.3 3.9 %collective-permute-start.5 = (f32[8,128]{1,0:T(8,128)S(1)}, f32[8,128]{1,0:T(8,128)S(1)}, u32[]{:S(2)}, u32[]{:S(2)}) collective-permute-start(f32[8,128]{1,0:T(8,128)S(1)} %get-tuple-element.30), channel_id=1, source_target_pairs={{0,16},{32,48},{64,80},{96,112},{128,144},{160,176},{192,208},{224... | collective-permute-start | bytes 12296 | tf_op jit(solution)/shard_map/ppermute | solution.py:459
  59.2 0.0 collective-permute-done.4
  59.2 1.3 %collective-permute-done.5 = f32[8,128]{1,0:T(8,128)S(1)} collective-permute-done((f32[8,128]{1,0:T(8,128)S(1)}, f32[8,128]{1,0:T(8,128)S(1)}, u32[]{:S(2)}, u32[]{:S(2)}) %collective-permute-start.5) | collective-permute-done | bytes 4128 | tf_op jit(solution)/shard_map/ppermute | solution.py:459
  60.5 2.8 %collective-permute-start.6 = (f32[24,128]{1,0:T(8,128)S(1)}, f32[24,128]{1,0:T(8,128)S(1)}, u32[]{:S(2)}, u32[]{:S(2)}) collective-permute-start(f32[24,128]{1,0:T(8,128)S(1)} %pad_maximum_fusion.2.vmid), channel_id=1, source_target_pairs={{0,1},{2,3},{4,5},{6,7},{8,9},{10,11},{12,13},{14,15},{1,0},{3,2},... | collective-permute-start | bytes 36872 | tf_op jit(solution)/shard_map/ppermute | solution.py:459
  63.3 3.4 %collective-permute-start.7 = (f32[24,128]{1,0:T(8,128)S(1)}, f32[24,128]{1,0:T(8,128)S(1)}, u32[]{:S(2)}, u32[]{:S(2)}) collective-permute-start(f32[24,128]{1,0:T(8,128)S(1)} %pad_maximum_fusion.2.vmid), channel_id=1, source_target_pairs={{1,2},{3,4},{5,6},{7,8},{9,10},{11,12},{13,14},{2,1},{4,3},{6,5},{... | collective-permute-start | bytes 36872 | tf_op jit(solution)/shard_map/ppermute | solution.py:459
  66.8 0.0 collective-permute-done.6.vnear
  66.8 2.1 %collective-permute-done.7.vfar = f32[24,128]{1,0:T(8,128)S(1)} collective-permute-done((f32[24,128]{1,0:T(8,128)S(1)}, f32[24,128]{1,0:T(8,128)S(1)}, u32[]{:S(2)}, u32[]{:S(2)}) %collective-permute-start.7) | collective-permute-done | bytes 12320 | tf_op jit(solution)/shard_map/ppermute | solution.py:459
  68.9 3.1 %all-to-all-done.1 = f32[16,64,128]{2,1,0:T(8,128)S(1)} async-done(((f32[16,64,128]{2,1,0:T(8,128)}), f32[16,64,128]{2,1,0:T(8,128)S(1)}, u32[]{:S(2)}, u32[]{:S(2)}) %all-to-all-start.1) | async-done | bytes 524320 | tf_op jit(solution)/shard_map/all_to_all | solution.py:464
  72.0 6.9 %up.1 = f32[8,8,128]{2,1,0:T(8,128)} custom-call(f32[1024,128]{1,0:T(8,128)S(1)} %bitcast.5, f32[12,24,128]{2,1,0:T(8,128)S(1)} %get-tuple-element.19.v0, f32[10,24,128]{2,1,0:T(8,128)S(1)} %get-tuple-element.20.f0, f32[8,24,128]{2,1,0:T(8,128)S(1)} %get-tuple-element.21.f1, f32[11,24,128]{2,1,0:T(8,128)S(1)} %get-tuple-element.22.wx0, ...), custom_call_target="tpu_custom_call" | custom-call | tf_op jit(solution)/shard_map/up/pallas_call | solution.py:495
  (6 shorter events, 0.1 us)
Async XLA Ops:
  0.8 7.3 %collective-permute-start = (f32[3,7,8,128]{3,2,1,0:T(8,128)S(1)}, f32[3,7,8,128]{3,2,1,0:T(8,128)S(1)}, u32[]{:S(2)}, u32[]{:S(2)}) collective-permute-start(f32[3,7,8,128]{3,2,1,0:T(8,128)S(1)} %get-tuple-element.33), channel_id=1, source_target_pairs={{16,32},{48,64},{80,96},{112,128},{144,160},{176,192},{208,224},{2... | collective-permute-start | bytes 258056 | tf_op jit(solution)/shard_map/ppermute | solution.py:459
  1.5 8.4 %collective-permute-start.1 = (f32[3,7,8,128]{3,2,1,0:T(8,128)S(1)}, f32[3,7,8,128]{3,2,1,0:T(8,128)S(1)}, u32[]{:S(2)}, u32[]{:S(2)}) collective-permute-start(f32[3,7,8,128]{3,2,1,0:T(8,128)S(1)} %get-tuple-element.34), channel_id=1, source_target_pairs={{0,16},{32,48},{64,80},{96,112},{128,144},{160,176},{192,208},{224... | collective-permute-start | bytes 258056 | tf_op jit(solution)/shard_map/ppermute | solution.py:459
  10.0 8.7 %collective-permute-start.2 = (f32[3,22,8,128]{3,2,1,0:T(8,128)S(1)}, f32[3,22,8,128]{3,2,1,0:T(8,128)S(1)}, u32[]{:S(2)}, u32[]{:S(2)}) collective-permute-start(f32[3,22,8,128]{3,2,1,0:T(8,128)S(1)} %pad_maximum_fusion.mid), channel_id=1, source_target_pairs={{0,1},{2,3},{4,5},{6,7},{8,9},{10,11},{12,13},{14,15},{1,0},{3,2},... | collective-permute-start | bytes 811016 | tf_op jit(solution)/shard_map/ppermute | solution.py:459
  16.7 7.8 %collective-permute-start.3 = (f32[3,22,8,128]{3,2,1,0:T(8,128)S(1)}, f32[3,22,8,128]{3,2,1,0:T(8,128)S(1)}, u32[]{:S(2)}, u32[]{:S(2)}) collective-permute-start(f32[3,22,8,128]{3,2,1,0:T(8,128)S(1)} %pad_maximum_fusion.mid), channel_id=1, source_target_pairs={{1,2},{3,4},{5,6},{7,8},{9,10},{11,12},{13,14},{2,1},{4,3},{6,5},{... | collective-permute-start | bytes 811016 | tf_op jit(solution)/shard_map/ppermute | solution.py:459
  41.9 30.0 %all-to-all-start.1 = ((f32[16,64,128]{2,1,0:T(8,128)}), f32[16,64,128]{2,1,0:T(8,128)S(1)}, u32[]{:S(2)}, u32[]{:S(2)}) async-start(f32[16,64,128]{2,1,0:T(8,128)} %broadcast_in_dim.15), calls=%async_computation.1 | async-start | bytes 1048576 | tf_op jit(solution)/shard_map/all_to_all | solution.py:464
  54.6 4.6 %collective-permute-start.4 = (f32[8,128]{1,0:T(8,128)S(1)}, f32[8,128]{1,0:T(8,128)S(1)}, u32[]{:S(2)}, u32[]{:S(2)}) collective-permute-start(f32[8,128]{1,0:T(8,128)S(1)} %get-tuple-element.30), channel_id=1, source_target_pairs={{16,32},{48,64},{80,96},{112,128},{144,160},{176,192},{208,224},{2... | collective-permute-start | bytes 12296 | tf_op jit(solution)/shard_map/ppermute | solution.py:459
  55.3 5.2 %collective-permute-start.5 = (f32[8,128]{1,0:T(8,128)S(1)}, f32[8,128]{1,0:T(8,128)S(1)}, u32[]{:S(2)}, u32[]{:S(2)}) collective-permute-start(f32[8,128]{1,0:T(8,128)S(1)} %get-tuple-element.30), channel_id=1, source_target_pairs={{0,16},{32,48},{64,80},{96,112},{128,144},{160,176},{192,208},{224... | collective-permute-start | bytes 12296 | tf_op jit(solution)/shard_map/ppermute | solution.py:459
  60.5 6.3 %collective-permute-start.6 = (f32[24,128]{1,0:T(8,128)S(1)}, f32[24,128]{1,0:T(8,128)S(1)}, u32[]{:S(2)}, u32[]{:S(2)}) collective-permute-start(f32[24,128]{1,0:T(8,128)S(1)} %pad_maximum_fusion.2.vmid), channel_id=1, source_target_pairs={{0,1},{2,3},{4,5},{6,7},{8,9},{10,11},{12,13},{14,15},{1,0},{3,2},... | collective-permute-start | bytes 36872 | tf_op jit(solution)/shard_map/ppermute | solution.py:459
  63.3 5.5 %collective-permute-start.7 = (f32[24,128]{1,0:T(8,128)S(1)}, f32[24,128]{1,0:T(8,128)S(1)}, u32[]{:S(2)}, u32[]{:S(2)}) collective-permute-start(f32[24,128]{1,0:T(8,128)S(1)} %pad_maximum_fusion.2.vmid), channel_id=1, source_target_pairs={{1,2},{3,4},{5,6},{7,8},{9,10},{11,12},{13,14},{2,1},{4,3},{6,5},{... | collective-permute-start | bytes 36872 | tf_op jit(solution)/shard_map/ppermute | solution.py:459

commit v6 on v4

--- a/solution.py
+++ b/solution.py
@@ -190,7 +190,7 @@
 
     def sweeps(self, v, source, count):
         step = lambda _, v: tuple(self.sweep(list(v), source))
-        return list(lax.fori_loop(0, count, step, tuple(v)))
+        return list(lax.fori_loop(0, count, step, tuple(v), unroll=True))
 
     def residual(self, v, source):
         around = self.around(v)
@@ -210,7 +210,7 @@
 
 
 def up_kernel(
-    gathered, v0, f0, f1, wx0, wy0, wz0, inv0, wx1, wy1, wz1, inv1, vmid, vnear, vfar, out,
+    mine, other, v0, f0, f1, wx0, wy0, wz0, inv0, wx1, wy1, wz1, inv1, vmid, vnear, vfar, out,
     k2, f2, va, vb, wxi, wxe, wyi, wye, wz2, diag2, inv2, sumk, sumr, e3,
 ):
     gx, gy = lax.axis_index("gx"), lax.axis_index("gy")
@@ -227,9 +227,10 @@
             ref[32 + PAD + i] = zero
     for i in range(32):
         for c, ref in ((0, f2), (1, k2)):
-            for core in range(2):
-                here = pl.ds(64 * core + 2 * i + c, 8, stride=128)
-                ref[i + PAD, 8 * core : 8 * core + 8] = gathered[here, :]
+            here = pl.ds(2 * i + c, 8, stride=64)
+            a, b = mine[here, :], other[here, :]
+            ref[i + PAD, :8] = jnp.where(first, a, b)
+            ref[i + PAD, 8:] = jnp.where(first, b, a)
 
     def sides(c):
         up, down = lanes(c, 32), lanes(c, -32)
@@ -459,17 +460,18 @@
     return lax.ppermute(x, axis, pairs + [(b, a) for a, b in pairs])
 
 
-def to_all(x, axis):
-    copies = jnp.broadcast_to(x[None], (lax.axis_size(axis),) + x.shape)
-    return lax.all_to_all(copies, axis, 0, 0)
+def to_all(x, axis, count, groups=None):
+    copies = jnp.broadcast_to(x[None], (count,) + x.shape)
+    return lax.all_to_all(copies, axis, 0, 0, axis_index_groups=groups)
 
 
 def shards(right_side, coefficient, previous):
-    own = jnp.stack([right_side, coefficient, previous])
     even = lax.axis_index("gx") % 2 == 0
+    own = lax.optimization_barrier(jnp.stack([right_side, coefficient, previous]))
     start, end = own[:, :HALO], own[:, -HALO:]
     near = swap(jnp.where(even, end, start), "gx", 0)
     far = swap(jnp.where(even, start, end), "gx", 1)
+
     mid = jnp.concatenate([jnp.where(even, far, near), own, jnp.where(even, near, far)], axis=1)
     near, far = swap(mid, "gy", 0), swap(mid, "gy", 1)
 
@@ -483,22 +485,25 @@
         name="down",
     )(mid, near, far)
 
-    blocks = to_all(packed.reshape(1, 1280), "gx")
-    gathered = to_all(blocks[:, :, :256].reshape(64, 128), "gy").reshape(1024, 128)
+    blocks = to_all(packed.reshape(1, 1280), "gx", 32)
+    same_core = [[2 * z + c for z in range(8)] for c in range(2)]
+    mine = to_all(blocks[:, :, :256].reshape(64, 128), "gy", 8, same_core).reshape(512, 128)
     v1 = jnp.pad(blocks[:, 0, 256:], ((1, 1), (0, 0)))
     place = (lax.axis_index("gx"), jnp.int32(0))
     vmid = lax.dynamic_slice(v1, place, (3, 1024)).reshape(24, 128)
     vnear, vfar = swap(vmid, "gy", 0), swap(vmid, "gy", 1)
+    mine, vnear, vfar = lax.optimization_barrier((mine, vnear, vfar))
+    other = swap(mine, "gy", 0)
 
     plane = pltpu.VMEM((32 + 2 * PAD, 16, 128), jnp.float32)
     return pl.pallas_call(
         up_kernel,
-        in_specs=[array] * (4 + len(WINDOW_PLANES)),
+        in_specs=[array] * (5 + len(WINDOW_PLANES)),
         out_shape=f32(8, 8, 128),
         scratch_shapes=[plane] * 13 + [pltpu.VMEM((8, 16, 128), jnp.float32)],
         compiler_params=params,
         name="up",
-    )(gathered, *window, vmid, vnear, vfar)
+    )(mine, other, *window, vmid, vnear, vfar)
 
 
 def solution(mesh):

time: 79.2 us -> 75.2 us (0.949)
  waiting for transfers between devices: 15.8 us -> 6.33 us
  starting transfers between devices: 32.5 us -> 38.3 us
    ppermute x6 -> x7, starting transfers between devices: 20.3 us -> 29.5 us  [swap(): return lax.ppermute(x, axis, pairs + [(b, a) for a, b in pairs])]
    ppermute x6 -> x7, waiting for transfers between devices: 12.7 us -> 6.33 us  [swap(): return lax.ppermute(x, axis, pairs + [(b, a) for a, b in pairs])]
    all_to_all x1, starting transfers between devices: 12.2 us -> 8.86 us  [to_all(): return lax.all_to_all(copies, axis, 0, 0, axis_index_groups=groups)]
    all_to_all x1, waiting for transfers between devices: 3.08 us -> 0.01 us  [to_all(): return lax.all_to_all(copies, axis, 0, 0, axis_index_groups=groups)]
  transfers between devices with their start and end apart: 7 -> 8, of which waited for: 4 -> 4; matrix products, arithmetic and copies ran while one was open for 0% -> 0% of each run, Pallas kernels for 0% -> 0%
where the time goes in v6:
time: 75.2 us; the launch traced here: 74.6 us
  starting transfers between devices  38.3 us (51%)
  blocking collectives  18.8 us (25%)
  Pallas kernels  8.59 us (11%)
  waiting for transfers between devices  6.33 us (8%)
  local copies, waits for them, and re-layouts  1.65 us (2%)
  other arithmetic  0.83 us (1%)
    ppermute x7, starting transfers between devices, swap(): return lax.ppermute(x, axis, pairs + [(b, a) for a, b in pairs])  29.5 us
    all_to_all x1, blocking collectives, to_all(): return lax.all_to_all(copies, axis, 0, 0, axis_index_groups=groups)  18.8 us
    all_to_all x1, starting transfers between devices, to_all(): return lax.all_to_all(copies, axis, 0, 0, axis_index_groups=groups)  8.86 us
    pallas_call x1, Pallas kernels, shards(): pl.pallas_call(up_kernel, in_specs=[array] * (5 + len(WINDOW_PLANES)), ou...  6.96 us
    ppermute x7, waiting for transfers between devices, swap(): return lax.ppermute(x, axis, pairs + [(b, a) for a, b in pairs])  6.33 us
    pallas_call x1, Pallas kernels, shards(): pl.pallas_call(down_kernel, in_specs=[array] * 3, out_shape=(f32(10, 128)...  1.63 us
  transfers between devices with their start and end apart: 8, of which 4 were waited for; matrix products, arithmetic and copies ran while one was open for 0% of the time, Pallas kernels for 0%

profile of v6, /device:TPU:1, one launch (start us, length us, event | category | flops | bytes accessed | tf_op | source)
XLA Modules:
  0.0 74.6 jit_solution(1072659168788539462)
XLA Ops:
  0.0 0.0 copy-start
  0.0 0.8 %copy-done = f32[8,8,128]{2,1,0:T(8,128)S(1)} copy-done((f32[8,8,128]{2,1,0:T(8,128)S(1)}, f32[8,8,128]{2,1,0:T(8,128)}, u32[]{:S(2)}) %copy-start) | copy-done | bytes 32792
  0.8 0.8 %pad_maximum_fusion.1 = f32[3,8,8,128]{3,2,1,0:T(8,128)S(1)} fusion(f32[1,8,8,128]{3,2,1,0:T(8,128)S(1)} %bitcast.14, f32[1,8,8,128]{3,2,1,0:T(8,128)} %bitcast.15, f32[1,8,8,128]{3,2,1,0:T(8,128)} %bitcast.16), kind=kLoop, calls=%fused_computation.3 | loop fusion | flops 49152 | bytes 196608 | tf_op jit(solution)/shard_map/stack | solution.py:470
  1.6 0.7 collective-permute-start
  2.2 6.6 %collective-permute-start.1 = (f32[3,7,8,128]{3,2,1,0:T(8,128)S(1)}, f32[3,7,8,128]{3,2,1,0:T(8,128)S(1)}, u32[]{:S(2)}, u32[]{:S(2)}) collective-permute-start(f32[3,7,8,128]{3,2,1,0:T(8,128)S(1)} %get-tuple-element.38), channel_id=1, source_target_pairs={{0,16},{32,48},{64,80},{96,112},{128,144},{160,176},{192,208},{224... | collective-permute-start | bytes 258056 | tf_op jit(solution)/shard_map/ppermute | solution.py:460
  8.8 0.0 collective-permute-done
  8.8 1.8 %collective-permute-done.1 = f32[3,7,8,128]{3,2,1,0:T(8,128)S(1)} collective-permute-done((f32[3,7,8,128]{3,2,1,0:T(8,128)S(1)}, f32[3,7,8,128]{3,2,1,0:T(8,128)S(1)}, u32[]{:S(2)}, u32[]{:S(2)}) %collective-permute-start.1) | collective-permute-done | bytes 86048 | tf_op jit(solution)/shard_map/ppermute | solution.py:460
  10.7 5.7 %collective-permute-start.3 = (f32[3,22,8,128]{3,2,1,0:T(8,128)S(1)}, f32[3,22,8,128]{3,2,1,0:T(8,128)S(1)}, u32[]{:S(2)}, u32[]{:S(2)}) collective-permute-start(f32[3,22,8,128]{3,2,1,0:T(8,128)S(1)} %pad_maximum_fusion.mid), channel_id=1, source_target_pairs={{1,2},{3,4},{5,6},{7,8},{9,10},{11,12},{13,14},{2,1},{4,3},{6,5},{... | collective-permute-start | bytes 811016 | tf_op jit(solution)/shard_map/ppermute | solution.py:460
  16.4 1.9 %collective-permute-start.2 = (f32[3,22,8,128]{3,2,1,0:T(8,128)S(1)}, f32[3,22,8,128]{3,2,1,0:T(8,128)S(1)}, u32[]{:S(2)}, u32[]{:S(2)}) collective-permute-start(f32[3,22,8,128]{3,2,1,0:T(8,128)S(1)} %pad_maximum_fusion.mid), channel_id=1, source_target_pairs={{0,1},{2,3},{4,5},{6,7},{8,9},{10,11},{12,13},{14,15},{1,0},{3,2},... | collective-permute-start | bytes 811016 | tf_op jit(solution)/shard_map/ppermute | solution.py:460
  18.4 2.2 %collective-permute-done.3.far = f32[3,22,8,128]{3,2,1,0:T(8,128)S(1)} collective-permute-done((f32[3,22,8,128]{3,2,1,0:T(8,128)S(1)}, f32[3,22,8,128]{3,2,1,0:T(8,128)S(1)}, u32[]{:S(2)}, u32[]{:S(2)}) %collective-permute-start.3) | collective-permute-done | bytes 270368 | tf_op jit(solution)/shard_map/ppermute | solution.py:460
  20.6 0.0 collective-permute-done.2.near
  20.6 1.6 %down.1 = (f32[10,128]{1,0:T(8,128)S(1)}, f32[12,24,128]{2,1,0:T(8,128)S(1)}, f32[10,24,128]{2,1,0:T(8,128)S(1)}, f32[8,24,128]{2,1,0:T(8,128)S(1)}, f32[11,24,1...) custom-call(f32[3,22,8,128]{3,2,1,0:T(8,128)S(1)} %pad_maximum_fusio, ...), custom_call_target="tpu_custom_call" | custom-call | tf_op jit(solution)/shard_map/down/pallas_call | solution.py:480
  22.2 0.1 broadcast_in_dim.15
  22.3 18.8 %all_to_all.10 = f32[32,1,1280]{2,1,0:T(1,128)S(1)} all-to-all(f32[32,1,1280]{2,1,0:T(1,128)S(1)} %broadcast_in_dim.15), channel_id=1, replica_groups=mesh['gx'=32,'gy'=16] {'gx'}, dimensions={0} | all-to-all | bytes 327680 | tf_op jit(solution)/shard_map/all_to_all | solution.py:465
  41.1 0.7 broadcast_in_dim.17
  41.8 8.9 %all-to-all-start.1 = ((f32[8,64,128]{2,1,0:T(8,128)}), f32[8,64,128]{2,1,0:T(8,128)S(1)}, u32[]{:S(2)}, u32[]{:S(2)}) async-start(f32[8,64,128]{2,1,0:T(8,128)} %broadcast_in_dim.17), calls=%async_computation.1 | async-start | bytes 524288 | tf_op jit(solution)/shard_map/all_to_all | solution.py:465
  50.8 6.9 %collective-permute-start.5 = (f32[24,128]{1,0:T(8,128)S(1)}, f32[24,128]{1,0:T(8,128)S(1)}, u32[]{:S(2)}, u32[]{:S(2)}) collective-permute-start(f32[24,128]{1,0:T(8,128)S(1)} %reshape.11.vmid), channel_id=1, source_target_pairs={{1,2},{3,4},{5,6},{7,8},{9,10},{11,12},{13,14},{2,1},{4,3},{6,5},{... | collective-permute-start | bytes 36872 | tf_op jit(solution)/shard_map/ppermute | solution.py:460
  57.7 1.9 %collective-permute-start.4 = (f32[24,128]{1,0:T(8,128)S(1)}, f32[24,128]{1,0:T(8,128)S(1)}, u32[]{:S(2)}, u32[]{:S(2)}) collective-permute-start(f32[24,128]{1,0:T(8,128)S(1)} %reshape.11.vmid), channel_id=1, source_target_pairs={{0,1},{2,3},{4,5},{6,7},{8,9},{10,11},{12,13},{14,15},{1,0},{3,2},... | collective-permute-start | bytes 36872 | tf_op jit(solution)/shard_map/ppermute | solution.py:460
  59.6 0.0 collective-permute-done.5.vfar
  59.6 1.1 %collective-permute-done.4.vnear = f32[24,128]{1,0:T(8,128)S(1)} collective-permute-done((f32[24,128]{1,0:T(8,128)S(1)}, f32[24,128]{1,0:T(8,128)S(1)}, u32[]{:S(2)}, u32[]{:S(2)}) %collective-permute-start.4) | collective-permute-done | bytes 12320 | tf_op jit(solution)/shard_map/ppermute | solution.py:460
  60.7 0.0 all-to-all-done.1
  60.7 5.8 %collective-permute-start.6 = (f32[512,128]{1,0:T(8,128)S(1)}, f32[512,128]{1,0:T(8,128)S(1)}, u32[]{:S(2)}, u32[]{:S(2)}) collective-permute-start(f32[512,128]{1,0:T(8,128)S(1)} %bitcast.9), channel_id=1, source_target_pairs={{0,1},{2,3},{4,5},{6,7},{8,9},{10,11},{12,13},{14,15},{1,0},{3,2},... | collective-permute-start | bytes 786440 | tf_op jit(solution)/shard_map/ppermute | solution.py:460
  66.5 1.1 %collective-permute-done.6.other = f32[512,128]{1,0:T(8,128)S(1)} collective-permute-done((f32[512,128]{1,0:T(8,128)S(1)}, f32[512,128]{1,0:T(8,128)S(1)}, u32[]{:S(2)}, u32[]{:S(2)}) %collective-permute-start.6) | collective-permute-done | bytes 262176 | tf_op jit(solution)/shard_map/ppermute | solution.py:460
  67.7 7.0 %up.1 = f32[8,8,128]{2,1,0:T(8,128)} custom-call(f32[512,128]{1,0:T(8,128)S(1)} %bitcast.10, f32[512,128]{1,0:T(8,128)S(1)} %collective-permute-done.6.other, f32[12,24,128]{2,1,0:T(8,128)S(1)} %get-tuple-element.22.v0, f32[10,24,128]{2,1,0:T(8,128)S(1)} %get-tuple-element.23.f0, f32[8,24,128]{2,1,0:T(8,128)S(1)} %get-tuple-element.24.f1, ...), custom_call_target="tpu_custom_call" | custom-call | tf_op jit(solution)/shard_map/up/pallas_call | solution.py:499
  (8 shorter events, 0.1 us)
Async XLA Ops:
  0.0 0.8 %copy-start = (f32[8,8,128]{2,1,0:T(8,128)S(1)}, f32[8,8,128]{2,1,0:T(8,128)}, u32[]{:S(2)}) copy-start(f32[8,8,128]{2,1,0:T(8,128)} %param.5) | copy-start | bytes 98308
  1.6 7.3 %collective-permute-start = (f32[3,7,8,128]{3,2,1,0:T(8,128)S(1)}, f32[3,7,8,128]{3,2,1,0:T(8,128)S(1)}, u32[]{:S(2)}, u32[]{:S(2)}) collective-permute-start(f32[3,7,8,128]{3,2,1,0:T(8,128)S(1)} %get-tuple-element.37), channel_id=1, source_target_pairs={{16,32},{48,64},{80,96},{112,128},{144,160},{176,192},{208,224},{2... | collective-permute-start | bytes 258056 | tf_op jit(solution)/shard_map/ppermute | solution.py:460
  2.2 8.4 %collective-permute-start.1 = (f32[3,7,8,128]{3,2,1,0:T(8,128)S(1)}, f32[3,7,8,128]{3,2,1,0:T(8,128)S(1)}, u32[]{:S(2)}, u32[]{:S(2)}) collective-permute-start(f32[3,7,8,128]{3,2,1,0:T(8,128)S(1)} %get-tuple-element.38), channel_id=1, source_target_pairs={{0,16},{32,48},{64,80},{96,112},{128,144},{160,176},{192,208},{224... | collective-permute-start | bytes 258056 | tf_op jit(solution)/shard_map/ppermute | solution.py:460
  10.7 9.8 %collective-permute-start.3 = (f32[3,22,8,128]{3,2,1,0:T(8,128)S(1)}, f32[3,22,8,128]{3,2,1,0:T(8,128)S(1)}, u32[]{:S(2)}, u32[]{:S(2)}) collective-permute-start(f32[3,22,8,128]{3,2,1,0:T(8,128)S(1)} %pad_maximum_fusion.mid), channel_id=1, source_target_pairs={{1,2},{3,4},{5,6},{7,8},{9,10},{11,12},{13,14},{2,1},{4,3},{6,5},{... | collective-permute-start | bytes 811016 | tf_op jit(solution)/shard_map/ppermute | solution.py:460
  16.4 4.1 %collective-permute-start.2 = (f32[3,22,8,128]{3,2,1,0:T(8,128)S(1)}, f32[3,22,8,128]{3,2,1,0:T(8,128)S(1)}, u32[]{:S(2)}, u32[]{:S(2)}) collective-permute-start(f32[3,22,8,128]{3,2,1,0:T(8,128)S(1)} %pad_maximum_fusion.mid), channel_id=1, source_target_pairs={{0,1},{2,3},{4,5},{6,7},{8,9},{10,11},{12,13},{14,15},{1,0},{3,2},... | collective-permute-start | bytes 811016 | tf_op jit(solution)/shard_map/ppermute | solution.py:460
  41.8 18.9 %all-to-all-start.1 = ((f32[8,64,128]{2,1,0:T(8,128)}), f32[8,64,128]{2,1,0:T(8,128)S(1)}, u32[]{:S(2)}, u32[]{:S(2)}) async-start(f32[8,64,128]{2,1,0:T(8,128)} %broadcast_in_dim.17), calls=%async_computation.1 | async-start | bytes 524288 | tf_op jit(solution)/shard_map/all_to_all | solution.py:465
  50.8 8.8 %collective-permute-start.5 = (f32[24,128]{1,0:T(8,128)S(1)}, f32[24,128]{1,0:T(8,128)S(1)}, u32[]{:S(2)}, u32[]{:S(2)}) collective-permute-start(f32[24,128]{1,0:T(8,128)S(1)} %reshape.11.vmid), channel_id=1, source_target_pairs={{1,2},{3,4},{5,6},{7,8},{9,10},{11,12},{13,14},{2,1},{4,3},{6,5},{... | collective-permute-start | bytes 36872 | tf_op jit(solution)/shard_map/ppermute | solution.py:460
  57.7 3.1 %collective-permute-start.4 = (f32[24,128]{1,0:T(8,128)S(1)}, f32[24,128]{1,0:T(8,128)S(1)}, u32[]{:S(2)}, u32[]{:S(2)}) collective-permute-start(f32[24,128]{1,0:T(8,128)S(1)} %reshape.11.vmid), channel_id=1, source_target_pairs={{0,1},{2,3},{4,5},{6,7},{8,9},{10,11},{12,13},{14,15},{1,0},{3,2},... | collective-permute-start | bytes 36872 | tf_op jit(solution)/shard_map/ppermute | solution.py:460
  60.7 7.0 %collective-permute-start.6 = (f32[512,128]{1,0:T(8,128)S(1)}, f32[512,128]{1,0:T(8,128)S(1)}, u32[]{:S(2)}, u32[]{:S(2)}) collective-permute-start(f32[512,128]{1,0:T(8,128)S(1)} %bitcast.9), channel_id=1, source_target_pairs={{0,1},{2,3},{4,5},{6,7},{8,9},{10,11},{12,13},{14,15},{1,0},{3,2},... | collective-permute-start | bytes 786440 | tf_op jit(solution)/shard_map/ppermute | solution.py:460

commit v7 on v6

--- a/solution.py
+++ b/solution.py
@@ -92,6 +92,43 @@
     return s + lanes(s, step)
 
 
+def alone(*planes):
+    return [(i, 8, None) for i in planes]
+
+
+INNER = range(8)
+NARROW = [(0, 6, -6), (7, 6, 13)] + alone(1, 2, 3, 4, 5, 6, -1, -2, 8, 9)
+NARROW += [(-3, 5, -5), (10, 5, 12), (-4, 4, 11)]
+WIDE = alone(*INNER, -1, -2, 8, 9)
+WIDE += [(-3, 6, -7), (10, 6, 14), (-4, 5, -6), (11, 5, 13), (-5, 4, 12)]
+TILES = (NARROW, WIDE, WIDE)
+
+
+def planes_of(which, own, near, far):
+    even = jnp.broadcast_to(lax.rem(lax.axis_index("gx"), 2), (8, 128)) == 0
+    planes = {i: own[which, i] for i in INNER}
+    for i in range(HALO):
+        a, b = near[which, i], far[which, i]
+        planes[i - HALO], planes[i + 8] = jnp.where(even, b, a), jnp.where(even, a, b)
+    return planes
+
+
+def pack_kernel(own, near, far, to_near, to_far):
+    first = core_mask(8)
+    row = iota((8, 128), 0)
+    at = 0
+    for which, tiles in enumerate(TILES):
+        planes = planes_of(which, own, near, far)
+        for a, n, b in tiles:
+            upward = downward = planes[a]
+            if b is not None:
+                upward = jnp.where(row >= 8 - n, planes[a], rows(planes[b], n))
+                downward = jnp.where(row < n, planes[a], rows(planes[b], -n))
+            to_near[at] = jnp.where(first, upward, downward)
+            to_far[at] = jnp.where(first, downward, upward)
+            at += 1
+
+
 def core_mask(rows_of):
     core = lax.rem(lax.axis_index("gy"), 2)
     return jnp.broadcast_to(core, (rows_of, 128)) == 0
@@ -102,17 +139,22 @@
 
 
 def down_kernel(
-    mid, near, far, packed, v0_out, f0_out, f1_out, wx0, wy0, wz0, inv0, wx1, wy1, wz1, inv1
+    own, xnear, xfar, near, far, packed, v0_out, f0_out, f1_out, wx0, wy0, wz0, inv0, wx1, wy1, wz1, inv1
 ):
     first = core_mask(8)
 
-    def field(which):
-        return {
-            i - HALO: joined(first, mid[which, i], near[which, i], far[which, i])
-            for i in range(mid.shape[1])
-        }
-
-    source, coeff, v = field(0), field(1), field(2)
+    fields, at = [], 0
+    for which, tiles in enumerate(TILES):
+        mid = planes_of(which, own, xnear, xfar)
+        low, high = {}, {}
+        for i, n, other in tiles:
+            below_it, above_it = jnp.where(first, far[at], near[at]), jnp.where(first, near[at], far[at])
+            low[i], high[i] = below_it, above_it
+            if other is not None:
+                low[other], high[other] = rows(below_it, -n), rows(above_it, n)
+            at += 1
+        fields.append({i: jnp.concatenate([low[i], mid[i], high[i]], axis=0) for i in low})
+    source, coeff, v = fields
     source = {i: 2.0 * source[i] for i in range(-6, 14)}
 
     fine = Window(1, (-6, 14))
@@ -467,23 +509,30 @@
 
 def shards(right_side, coefficient, previous):
     even = lax.axis_index("gx") % 2 == 0
-    own = lax.optimization_barrier(jnp.stack([right_side, coefficient, previous]))
+    own = lax.optimization_barrier(jnp.concatenate([right_side, coefficient, previous])).reshape(3, 8, 8, 128)
     start, end = own[:, :HALO], own[:, -HALO:]
     near = swap(jnp.where(even, end, start), "gx", 0)
     far = swap(jnp.where(even, start, end), "gx", 1)
 
-    mid = jnp.concatenate([jnp.where(even, far, near), own, jnp.where(even, near, far)], axis=1)
-    near, far = swap(mid, "gy", 0), swap(mid, "gy", 1)
-
     params = pltpu.CompilerParams(vmem_limit_bytes=VMEM)
     array = pl.BlockSpec(memory_space=pltpu.VMEM)
+    count = sum(len(tiles) for tiles in TILES)
+    to_near, to_far = pl.pallas_call(
+        pack_kernel,
+        in_specs=[array] * 3,
+        out_shape=(f32(count, 8, 128),) * 2,
+        compiler_params=params,
+        name="pack",
+    )(own, near, far)
+    from_near, from_far = swap(to_near, "gy", 0), swap(to_far, "gy", 1)
+
     packed, *window = pl.pallas_call(
         down_kernel,
-        in_specs=[array] * 3,
+        in_specs=[array] * 5,
         out_shape=(f32(10, 128),) + tuple(f32(n, ROWS, 128) for n in WINDOW_PLANES),
         compiler_params=params,
         name="down",
-    )(mid, near, far)
+    )(own, near, far, from_near, from_far)
 
     blocks = to_all(packed.reshape(1, 1280), "gx", 32)
     same_core = [[2 * z + c for z in range(8)] for c in range(2)]

time: 75.2 us -> 75.5 us (level)
  blocking collectives: 18.8 us -> 15.4 us
  waiting for transfers between devices: 6.33 us -> 9.23 us
  starting transfers between devices: 38.3 us -> 40 us
  local copies, waits for them, and re-layouts: 1.65 us -> 0.89 us
    all_to_all x1, blocking collectives: 18.8 us -> 15.4 us  [to_all(): return lax.all_to_all(copies, axis, 0, 0, axis_index_groups=groups)]
    ppermute x7, waiting for transfers between devices: 6.33 us -> 9.23 us  [swap(): return lax.ppermute(x, axis, pairs + [(b, a) for a, b in pairs])]
    all_to_all x1, starting transfers between devices: 8.86 us -> 10 us  [to_all(): return lax.all_to_all(copies, axis, 0, 0, axis_index_groups=groups)]
    another operation x1 -> x0, other arithmetic: 0.78 us -> none  [shards(): jnp.stack([right_side, coefficient, previous])]
    concatenate x1, other arithmetic: 0.02 us -> 0.8 us  [shards(): jnp.concatenate([right_side, coefficient, previous])]
    unnamed x3 -> x1, local copies, waits for them, and re-layouts: 0.78 us -> 0.03 us
    pallas_call x1 -> x2, Pallas kernels: 1.63 us -> 1.62 us  [the longest x1 1.58 us: shards(): pl.pallas_call(down_kernel, in_specs=[array] * 5, out_shape=(f32(10, 128)...]
where the time goes in v7:
time: 75.5 us; the launch traced here: 75 us
  starting transfers between devices  40 us (53%)
  blocking collectives  15.4 us (20%)
  waiting for transfers between devices  9.23 us (12%)
  Pallas kernels  8.57 us (11%)
  local copies, waits for them, and re-layouts  0.89 us (1%)
  other arithmetic  0.81 us (1%)
    ppermute x7, starting transfers between devices, swap(): return lax.ppermute(x, axis, pairs + [(b, a) for a, b in pairs])  29.9 us
    all_to_all x1, blocking collectives, to_all(): return lax.all_to_all(copies, axis, 0, 0, axis_index_groups=groups)  15.4 us
    all_to_all x1, starting transfers between devices, to_all(): return lax.all_to_all(copies, axis, 0, 0, axis_index_groups=groups)  10 us
    ppermute x7, waiting for transfers between devices, swap(): return lax.ppermute(x, axis, pairs + [(b, a) for a, b in pairs])  9.23 us
    pallas_call x1, Pallas kernels, shards(): pl.pallas_call(up_kernel, in_specs=[array] * (5 + len(WINDOW_PLANES)), ou...  6.96 us
    pallas_call x1, Pallas kernels, shards(): pl.pallas_call(down_kernel, in_specs=[array] * 5, out_shape=(f32(10, 128)...  1.58 us
  transfers between devices with their start and end apart: 8, of which 4 were waited for; matrix products, arithmetic and copies ran while one was open for 0% of the time, Pallas kernels for 0%

profile of v7, /device:TPU:1, one launch (start us, length us, event | category | flops | bytes accessed | tf_op | source)
XLA Modules:
  0.0 75.0 jit_solution(11936874744741160940)
XLA Ops:
  0.0 0.8 %pad_maximum_fusion = f32[24,8,128]{2,1,0:T(8,128)S(1)} fusion(f32[8,8,128]{2,1,0:T(8,128)} %param.5, f32[8,8,128]{2,1,0:T(8,128)} %param.4, f32[8,8,128]{2,1,0:T(8,128)} %param.3), kind=kLoop, calls=%fused_computation.2 | loop fusion | flops 49152 | bytes 196608 | tf_op jit(solution)/shard_map/concatenate | solution.py:512
  0.8 0.7 collective-permute-start.1
  1.5 6.6 %collective-permute-start = (f32[3,7,8,128]{3,2,1,0:T(8,128)S(1)}, f32[3,7,8,128]{3,2,1,0:T(8,128)S(1)}, u32[]{:S(2)}, u32[]{:S(2)}) collective-permute-start(f32[3,7,8,128]{3,2,1,0:T(8,128)S(1)} %get-tuple-element.40), channel_id=1, source_target_pairs={{0,16},{32,48},{64,80},{96,112},{128,144},{160,176},{192,208},{224... | collective-permute-start | bytes 258056 | tf_op jit(solution)/shard_map/ppermute | solution.py:502
  8.1 0.0 collective-permute-done.1.far.xfar
  8.1 1.8 %collective-permute-done.near.xnear = f32[3,7,8,128]{3,2,1,0:T(8,128)S(1)} collective-permute-done((f32[3,7,8,128]{3,2,1,0:T(8,128)S(1)}, f32[3,7,8,128]{3,2,1,0:T(8,128)S(1)}, u32[]{:S(2)}, u32[]{:S(2)}) %collective-permute-start) | collective-permute-done | bytes 86048 | tf_op jit(solution)/shard_map/ppermute | solution.py:502
  10.0 6.7 %collective-permute-start.2 = (f32[49,8,128]{2,1,0:T(8,128)S(1)}, f32[49,8,128]{2,1,0:T(8,128)S(1)}, u32[]{:S(2)}, u32[]{:S(2)}) collective-permute-start(f32[49,8,128]{2,1,0:T(8,128)S(1)} %get-tuple-element.22), channel_id=1, source_target_pairs={{0,1},{2,3},{4,5},{6,7},{8,9},{10,11},{12,13},{14,15},{1,0},{3,2},... | collective-permute-start | bytes 602120 | tf_op jit(solution)/shard_map/ppermute | solution.py:502
  16.7 1.9 %collective-permute-start.3 = (f32[49,8,128]{2,1,0:T(8,128)S(1)}, f32[49,8,128]{2,1,0:T(8,128)S(1)}, u32[]{:S(2)}, u32[]{:S(2)}) collective-permute-start(f32[49,8,128]{2,1,0:T(8,128)S(1)} %get-tuple-element.23), channel_id=1, source_target_pairs={{1,2},{3,4},{5,6},{7,8},{9,10},{11,12},{13,14},{2,1},{4,3},{6,5},{... | collective-permute-start | bytes 602120 | tf_op jit(solution)/shard_map/ppermute | solution.py:502
  18.6 0.0 collective-permute-done.2.near
  18.6 5.1 %collective-permute-done.3.far = f32[49,8,128]{2,1,0:T(8,128)S(1)} collective-permute-done((f32[49,8,128]{2,1,0:T(8,128)S(1)}, f32[49,8,128]{2,1,0:T(8,128)S(1)}, u32[]{:S(2)}, u32[]{:S(2)}) %collective-permute-start.3) | collective-permute-done | bytes 200736 | tf_op jit(solution)/shard_map/ppermute | solution.py:502
  23.7 1.6 %down.1 = (f32[10,128]{1,0:T(8,128)S(1)}, f32[12,24,128]{2,1,0:T(8,128)S(1)}, f32[10,24,128]{2,1,0:T(8,128)S(1)}, f32[8,24,128]{2,1,0:T(8,128)S(1)}, f32[11,24,1...) custom-call(f32[3,8,8,128]{3,2,1,0:T(8,128)S(1)} %bitcast.9, ...), custom_call_target="tpu_custom_call" | custom-call | tf_op jit(solution)/shard_map/down/pallas_call | solution.py:529
  25.3 0.1 broadcast_in_dim.15
  25.4 15.4 %all_to_all.10 = f32[32,1,1280]{2,1,0:T(1,128)S(1)} all-to-all(f32[32,1,1280]{2,1,0:T(1,128)S(1)} %broadcast_in_dim.15), channel_id=1, replica_groups=mesh['gx'=32,'gy'=16] {'gx'}, dimensions={0} | all-to-all | bytes 327680 | tf_op jit(solution)/shard_map/all_to_all | solution.py:507
  40.9 0.7 broadcast_in_dim.17
  41.6 10.0 %all-to-all-start.1 = ((f32[8,64,128]{2,1,0:T(8,128)}), f32[8,64,128]{2,1,0:T(8,128)S(1)}, u32[]{:S(2)}, u32[]{:S(2)}) async-start(f32[8,64,128]{2,1,0:T(8,128)} %broadcast_in_dim.17), calls=%async_computation.1 | async-start | bytes 524288 | tf_op jit(solution)/shard_map/all_to_all | solution.py:507
  51.7 6.3 %collective-permute-start.5 = (f32[24,128]{1,0:T(8,128)S(1)}, f32[24,128]{1,0:T(8,128)S(1)}, u32[]{:S(2)}, u32[]{:S(2)}) collective-permute-start(f32[24,128]{1,0:T(8,128)S(1)} %reshape.15.vmid), channel_id=1, source_target_pairs={{1,2},{3,4},{5,6},{7,8},{9,10},{11,12},{13,14},{2,1},{4,3},{6,5},{... | collective-permute-start | bytes 36872 | tf_op jit(solution)/shard_map/ppermute | solution.py:502
  58.1 1.9 %collective-permute-start.4 = (f32[24,128]{1,0:T(8,128)S(1)}, f32[24,128]{1,0:T(8,128)S(1)}, u32[]{:S(2)}, u32[]{:S(2)}) collective-permute-start(f32[24,128]{1,0:T(8,128)S(1)} %reshape.15.vmid), channel_id=1, source_target_pairs={{0,1},{2,3},{4,5},{6,7},{8,9},{10,11},{12,13},{14,15},{1,0},{3,2},... | collective-permute-start | bytes 36872 | tf_op jit(solution)/shard_map/ppermute | solution.py:502
  60.0 0.0 collective-permute-done.5.vfar
  60.0 1.1 %collective-permute-done.4.vnear = f32[24,128]{1,0:T(8,128)S(1)} collective-permute-done((f32[24,128]{1,0:T(8,128)S(1)}, f32[24,128]{1,0:T(8,128)S(1)}, u32[]{:S(2)}, u32[]{:S(2)}) %collective-permute-start.4) | collective-permute-done | bytes 12320 | tf_op jit(solution)/shard_map/ppermute | solution.py:502
  61.1 0.0 all-to-all-done.1
  61.1 5.8 %collective-permute-start.6 = (f32[512,128]{1,0:T(8,128)S(1)}, f32[512,128]{1,0:T(8,128)S(1)}, u32[]{:S(2)}, u32[]{:S(2)}) collective-permute-start(f32[512,128]{1,0:T(8,128)S(1)} %bitcast.10), channel_id=1, source_target_pairs={{0,1},{2,3},{4,5},{6,7},{8,9},{10,11},{12,13},{14,15},{1,0},{3,2},... | collective-permute-start | bytes 786440 | tf_op jit(solution)/shard_map/ppermute | solution.py:502
  67.0 1.1 %collective-permute-done.6.other = f32[512,128]{1,0:T(8,128)S(1)} collective-permute-done((f32[512,128]{1,0:T(8,128)S(1)}, f32[512,128]{1,0:T(8,128)S(1)}, u32[]{:S(2)}, u32[]{:S(2)}) %collective-permute-start.6) | collective-permute-done | bytes 262176 | tf_op jit(solution)/shard_map/ppermute | solution.py:502
  68.1 7.0 %up.1 = f32[8,8,128]{2,1,0:T(8,128)} custom-call(f32[512,128]{1,0:T(8,128)S(1)} %bitcast.11, f32[512,128]{1,0:T(8,128)S(1)} %collective-permute-done.6.other, f32[12,24,128]{2,1,0:T(8,128)S(1)} %get-tuple-element.26.v0, f32[10,24,128]{2,1,0:T(8,128)S(1)} %get-tuple-element.27.f0, f32[8,24,128]{2,1,0:T(8,128)S(1)} %get-tuple-element.28.f1, ...), custom_call_target="tpu_custom_call" | custom-call | tf_op jit(solution)/shard_map/up/pallas_call | solution.py:548
  (7 shorter events, 0.1 us)
Async XLA Ops:
  0.8 7.3 %collective-permute-start.1 = (f32[3,7,8,128]{3,2,1,0:T(8,128)S(1)}, f32[3,7,8,128]{3,2,1,0:T(8,128)S(1)}, u32[]{:S(2)}, u32[]{:S(2)}) collective-permute-start(f32[3,7,8,128]{3,2,1,0:T(8,128)S(1)} %get-tuple-element.39), channel_id=1, source_target_pairs={{16,32},{48,64},{80,96},{112,128},{144,160},{176,192},{208,224},{2... | collective-permute-start | bytes 258056 | tf_op jit(solution)/shard_map/ppermute | solution.py:502
  1.5 8.4 %collective-permute-start = (f32[3,7,8,128]{3,2,1,0:T(8,128)S(1)}, f32[3,7,8,128]{3,2,1,0:T(8,128)S(1)}, u32[]{:S(2)}, u32[]{:S(2)}) collective-permute-start(f32[3,7,8,128]{3,2,1,0:T(8,128)S(1)} %get-tuple-element.40), channel_id=1, source_target_pairs={{0,16},{32,48},{64,80},{96,112},{128,144},{160,176},{192,208},{224... | collective-permute-start | bytes 258056 | tf_op jit(solution)/shard_map/ppermute | solution.py:502
  10.0 8.7 %collective-permute-start.2 = (f32[49,8,128]{2,1,0:T(8,128)S(1)}, f32[49,8,128]{2,1,0:T(8,128)S(1)}, u32[]{:S(2)}, u32[]{:S(2)}) collective-permute-start(f32[49,8,128]{2,1,0:T(8,128)S(1)} %get-tuple-element.22), channel_id=1, source_target_pairs={{0,1},{2,3},{4,5},{6,7},{8,9},{10,11},{12,13},{14,15},{1,0},{3,2},... | collective-permute-start | bytes 602120 | tf_op jit(solution)/shard_map/ppermute | solution.py:502
  16.7 7.0 %collective-permute-start.3 = (f32[49,8,128]{2,1,0:T(8,128)S(1)}, f32[49,8,128]{2,1,0:T(8,128)S(1)}, u32[]{:S(2)}, u32[]{:S(2)}) collective-permute-start(f32[49,8,128]{2,1,0:T(8,128)S(1)} %get-tuple-element.23), channel_id=1, source_target_pairs={{1,2},{3,4},{5,6},{7,8},{9,10},{11,12},{13,14},{2,1},{4,3},{6,5},{... | collective-permute-start | bytes 602120 | tf_op jit(solution)/shard_map/ppermute | solution.py:502
  41.6 19.6 %all-to-all-start.1 = ((f32[8,64,128]{2,1,0:T(8,128)}), f32[8,64,128]{2,1,0:T(8,128)S(1)}, u32[]{:S(2)}, u32[]{:S(2)}) async-start(f32[8,64,128]{2,1,0:T(8,128)} %broadcast_in_dim.17), calls=%async_computation.1 | async-start | bytes 524288 | tf_op jit(solution)/shard_map/all_to_all | solution.py:507
  51.7 8.3 %collective-permute-start.5 = (f32[24,128]{1,0:T(8,128)S(1)}, f32[24,128]{1,0:T(8,128)S(1)}, u32[]{:S(2)}, u32[]{:S(2)}) collective-permute-start(f32[24,128]{1,0:T(8,128)S(1)} %reshape.15.vmid), channel_id=1, source_target_pairs={{1,2},{3,4},{5,6},{7,8},{9,10},{11,12},{13,14},{2,1},{4,3},{6,5},{... | collective-permute-start | bytes 36872 | tf_op jit(solution)/shard_map/ppermute | solution.py:502
  58.1 3.1 %collective-permute-start.4 = (f32[24,128]{1,0:T(8,128)S(1)}, f32[24,128]{1,0:T(8,128)S(1)}, u32[]{:S(2)}, u32[]{:S(2)}) collective-permute-start(f32[24,128]{1,0:T(8,128)S(1)} %reshape.15.vmid), channel_id=1, source_target_pairs={{0,1},{2,3},{4,5},{6,7},{8,9},{10,11},{12,13},{14,15},{1,0},{3,2},... | collective-permute-start | bytes 36872 | tf_op jit(solution)/shard_map/ppermute | solution.py:502
  61.1 7.0 %collective-permute-start.6 = (f32[512,128]{1,0:T(8,128)S(1)}, f32[512,128]{1,0:T(8,128)S(1)}, u32[]{:S(2)}, u32[]{:S(2)}) collective-permute-start(f32[512,128]{1,0:T(8,128)S(1)} %bitcast.10), channel_id=1, source_target_pairs={{0,1},{2,3},{4,5},{6,7},{8,9},{10,11},{12,13},{14,15},{1,0},{3,2},... | collective-permute-start | bytes 786440 | tf_op jit(solution)/shard_map/ppermute | solution.py:502

commit v8 on v7

--- a/solution.py
+++ b/solution.py
@@ -139,7 +139,7 @@
 
 
 def down_kernel(
-    own, xnear, xfar, near, far, packed, v0_out, f0_out, f1_out, wx0, wy0, wz0, inv0, wx1, wy1, wz1, inv1
+    own, xnear, xfar, far, near, packed, v0_out, f0_out, f1_out, wx0, wy0, wz0, inv0, wx1, wy1, wz1, inv1
 ):
     first = core_mask(8)
 
@@ -247,7 +247,7 @@
     return jnp.concatenate([rows(c[8:], -1), c[:8]], axis=0)
 
 
-UNROLL = 10
+UNROLL = 15
 PAD = 3
 
 
@@ -524,7 +524,8 @@
         compiler_params=params,
         name="pack",
     )(own, near, far)
-    from_near, from_far = swap(to_near, "gy", 0), swap(to_far, "gy", 1)
+    from_far = swap(to_far, "gy", 1)
+    from_near = swap(to_near, "gy", 0)
 
     packed, *window = pl.pallas_call(
         down_kernel,
@@ -532,7 +533,7 @@
         out_shape=(f32(10, 128),) + tuple(f32(n, ROWS, 128) for n in WINDOW_PLANES),
         compiler_params=params,
         name="down",
-    )(own, near, far, from_near, from_far)
+    )(own, near, far, from_far, from_near)
 
     blocks = to_all(packed.reshape(1, 1280), "gx", 32)
     same_core = [[2 * z + c for z in range(8)] for c in range(2)]

time: 75.5 us -> 75.1 us (level)
  waiting for transfers between devices: 9.23 us -> 5.59 us
  blocking collectives: 15.4 us -> 18.2 us
  Pallas kernels: 8.57 us -> 10.1 us
  starting transfers between devices: 40 us -> 38.9 us
    ppermute x7, waiting for transfers between devices: 9.23 us -> 5.58 us  [swap(): return lax.ppermute(x, axis, pairs + [(b, a) for a, b in pairs])]
    all_to_all x1, blocking collectives: 15.4 us -> 18.2 us  [to_all(): return lax.all_to_all(copies, axis, 0, 0, axis_index_groups=groups)]
    pallas_call x1, Pallas kernels: 6.96 us -> 8.45 us  [shards(): pl.pallas_call(up_kernel, in_specs=[array] * (5 + len(WINDOW_PLANES)), ou...]
where the time goes in v8:
time: 75.1 us; the launch traced here: 74.6 us
  starting transfers between devices  38.9 us (52%)
  blocking collectives  18.2 us (24%)
  Pallas kernels  10.1 us (13%)
  waiting for transfers between devices  5.59 us (7%)
  local copies, waits for them, and re-layouts  0.89 us (1%)
  other arithmetic  0.81 us (1%)
    ppermute x7, starting transfers between devices, swap(): return lax.ppermute(x, axis, pairs + [(b, a) for a, b in pairs])  29.5 us
    all_to_all x1, blocking collectives, to_all(): return lax.all_to_all(copies, axis, 0, 0, axis_index_groups=groups)  18.2 us
    all_to_all x1, starting transfers between devices, to_all(): return lax.all_to_all(copies, axis, 0, 0, axis_index_groups=groups)  9.48 us
    pallas_call x1, Pallas kernels, shards(): pl.pallas_call(up_kernel, in_specs=[array] * (5 + len(WINDOW_PLANES)), ou...  8.45 us
    ppermute x7, waiting for transfers between devices, swap(): return lax.ppermute(x, axis, pairs + [(b, a) for a, b in pairs])  5.58 us
    pallas_call x1, Pallas kernels, shards(): pl.pallas_call(down_kernel, in_specs=[array] * 5, out_shape=(f32(10, 128)...  1.58 us
  transfers between devices with their start and end apart: 8, of which 4 were waited for; matrix products, arithmetic and copies ran while one was open for 0% of the time, Pallas kernels for 0%

profile of v8, /device:TPU:1, one launch (start us, length us, event | category | flops | bytes accessed | tf_op | source)
XLA Modules:
  0.0 74.6 jit_solution(13429921736284618085)
XLA Ops:
  0.0 0.8 %pad_maximum_fusion = f32[24,8,128]{2,1,0:T(8,128)S(1)} fusion(f32[8,8,128]{2,1,0:T(8,128)} %param.5, f32[8,8,128]{2,1,0:T(8,128)} %param.4, f32[8,8,128]{2,1,0:T(8,128)} %param.3), kind=kLoop, calls=%fused_computation.2 | loop fusion | flops 49152 | bytes 196608 | tf_op jit(solution)/shard_map/concatenate | solution.py:512
  0.8 0.7 collective-permute-start.1
  1.5 6.6 %collective-permute-start = (f32[3,7,8,128]{3,2,1,0:T(8,128)S(1)}, f32[3,7,8,128]{3,2,1,0:T(8,128)S(1)}, u32[]{:S(2)}, u32[]{:S(2)}) collective-permute-start(f32[3,7,8,128]{3,2,1,0:T(8,128)S(1)} %get-tuple-element.40), channel_id=1, source_target_pairs={{0,16},{32,48},{64,80},{96,112},{128,144},{160,176},{192,208},{224... | collective-permute-start | bytes 258056 | tf_op jit(solution)/shard_map/ppermute | solution.py:502
  8.1 0.0 collective-permute-done.1.far.xfar
  8.1 1.8 %collective-permute-done.near.xnear = f32[3,7,8,128]{3,2,1,0:T(8,128)S(1)} collective-permute-done((f32[3,7,8,128]{3,2,1,0:T(8,128)S(1)}, f32[3,7,8,128]{3,2,1,0:T(8,128)S(1)}, u32[]{:S(2)}, u32[]{:S(2)}) %collective-permute-start) | collective-permute-done | bytes 86048 | tf_op jit(solution)/shard_map/ppermute | solution.py:502
  10.0 5.7 %collective-permute-start.2 = (f32[49,8,128]{2,1,0:T(8,128)S(1)}, f32[49,8,128]{2,1,0:T(8,128)S(1)}, u32[]{:S(2)}, u32[]{:S(2)}) collective-permute-start(f32[49,8,128]{2,1,0:T(8,128)S(1)} %get-tuple-element.22), channel_id=1, source_target_pairs={{1,2},{3,4},{5,6},{7,8},{9,10},{11,12},{13,14},{2,1},{4,3},{6,5},{... | collective-permute-start | bytes 602120 | tf_op jit(solution)/shard_map/ppermute | solution.py:502
  15.7 1.9 %collective-permute-start.3 = (f32[49,8,128]{2,1,0:T(8,128)S(1)}, f32[49,8,128]{2,1,0:T(8,128)S(1)}, u32[]{:S(2)}, u32[]{:S(2)}) collective-permute-start(f32[49,8,128]{2,1,0:T(8,128)S(1)} %get-tuple-element.23), channel_id=1, source_target_pairs={{0,1},{2,3},{4,5},{6,7},{8,9},{10,11},{12,13},{14,15},{1,0},{3,2},... | collective-permute-start | bytes 602120 | tf_op jit(solution)/shard_map/ppermute | solution.py:502
  17.6 1.5 %collective-permute-done.2.far = f32[49,8,128]{2,1,0:T(8,128)S(1)} collective-permute-done((f32[49,8,128]{2,1,0:T(8,128)S(1)}, f32[49,8,128]{2,1,0:T(8,128)S(1)}, u32[]{:S(2)}, u32[]{:S(2)}) %collective-permute-start.2) | collective-permute-done | bytes 200736 | tf_op jit(solution)/shard_map/ppermute | solution.py:502
  19.1 0.0 collective-permute-done.3.near
  19.1 1.6 %down.1 = (f32[10,128]{1,0:T(8,128)S(1)}, f32[12,24,128]{2,1,0:T(8,128)S(1)}, f32[10,24,128]{2,1,0:T(8,128)S(1)}, f32[8,24,128]{2,1,0:T(8,128)S(1)}, f32[11,24,1...) custom-call(f32[3,8,8,128]{3,2,1,0:T(8,128)S(1)} %bitcast.9, ...), custom_call_target="tpu_custom_call" | custom-call | tf_op jit(solution)/shard_map/down/pallas_call | solution.py:530
  20.7 0.1 broadcast_in_dim.15
  20.8 18.2 %all_to_all.10 = f32[32,1,1280]{2,1,0:T(1,128)S(1)} all-to-all(f32[32,1,1280]{2,1,0:T(1,128)S(1)} %broadcast_in_dim.15), channel_id=1, replica_groups=mesh['gx'=32,'gy'=16] {'gx'}, dimensions={0} | all-to-all | bytes 327680 | tf_op jit(solution)/shard_map/all_to_all | solution.py:507
  39.0 0.7 broadcast_in_dim.17
  39.7 9.5 %all-to-all-start.1 = ((f32[8,64,128]{2,1,0:T(8,128)}), f32[8,64,128]{2,1,0:T(8,128)S(1)}, u32[]{:S(2)}, u32[]{:S(2)}) async-start(f32[8,64,128]{2,1,0:T(8,128)} %broadcast_in_dim.17), calls=%async_computation.1 | async-start | bytes 524288 | tf_op jit(solution)/shard_map/all_to_all | solution.py:507
  49.2 6.9 %collective-permute-start.5 = (f32[24,128]{1,0:T(8,128)S(1)}, f32[24,128]{1,0:T(8,128)S(1)}, u32[]{:S(2)}, u32[]{:S(2)}) collective-permute-start(f32[24,128]{1,0:T(8,128)S(1)} %reshape.15.vmid), channel_id=1, source_target_pairs={{1,2},{3,4},{5,6},{7,8},{9,10},{11,12},{13,14},{2,1},{4,3},{6,5},{... | collective-permute-start | bytes 36872 | tf_op jit(solution)/shard_map/ppermute | solution.py:502
  56.1 1.9 %collective-permute-start.4 = (f32[24,128]{1,0:T(8,128)S(1)}, f32[24,128]{1,0:T(8,128)S(1)}, u32[]{:S(2)}, u32[]{:S(2)}) collective-permute-start(f32[24,128]{1,0:T(8,128)S(1)} %reshape.15.vmid), channel_id=1, source_target_pairs={{0,1},{2,3},{4,5},{6,7},{8,9},{10,11},{12,13},{14,15},{1,0},{3,2},... | collective-permute-start | bytes 36872 | tf_op jit(solution)/shard_map/ppermute | solution.py:502
  58.1 0.0 collective-permute-done.5.vfar
  58.1 1.1 %collective-permute-done.4.vnear = f32[24,128]{1,0:T(8,128)S(1)} collective-permute-done((f32[24,128]{1,0:T(8,128)S(1)}, f32[24,128]{1,0:T(8,128)S(1)}, u32[]{:S(2)}, u32[]{:S(2)}) %collective-permute-start.4) | collective-permute-done | bytes 12320 | tf_op jit(solution)/shard_map/ppermute | solution.py:502
  59.2 0.0 all-to-all-done.1
  59.2 5.8 %collective-permute-start.6 = (f32[512,128]{1,0:T(8,128)S(1)}, f32[512,128]{1,0:T(8,128)S(1)}, u32[]{:S(2)}, u32[]{:S(2)}) collective-permute-start(f32[512,128]{1,0:T(8,128)S(1)} %bitcast.10), channel_id=1, source_target_pairs={{0,1},{2,3},{4,5},{6,7},{8,9},{10,11},{12,13},{14,15},{1,0},{3,2},... | collective-permute-start | bytes 786440 | tf_op jit(solution)/shard_map/ppermute | solution.py:502
  65.0 1.1 %collective-permute-done.6.other = f32[512,128]{1,0:T(8,128)S(1)} collective-permute-done((f32[512,128]{1,0:T(8,128)S(1)}, f32[512,128]{1,0:T(8,128)S(1)}, u32[]{:S(2)}, u32[]{:S(2)}) %collective-permute-start.6) | collective-permute-done | bytes 262176 | tf_op jit(solution)/shard_map/ppermute | solution.py:502
  66.2 8.4 %up.1 = f32[8,8,128]{2,1,0:T(8,128)} custom-call(f32[512,128]{1,0:T(8,128)S(1)} %bitcast.11, f32[512,128]{1,0:T(8,128)S(1)} %collective-permute-done.6.other, f32[12,24,128]{2,1,0:T(8,128)S(1)} %get-tuple-element.26.v0, f32[10,24,128]{2,1,0:T(8,128)S(1)} %get-tuple-element.27.f0, f32[8,24,128]{2,1,0:T(8,128)S(1)} %get-tuple-element.28.f1, ...), custom_call_target="tpu_custom_call" | custom-call | tf_op jit(solution)/shard_map/up/pallas_call | solution.py:549
  (7 shorter events, 0.1 us)
Async XLA Ops:
  0.8 7.3 %collective-permute-start.1 = (f32[3,7,8,128]{3,2,1,0:T(8,128)S(1)}, f32[3,7,8,128]{3,2,1,0:T(8,128)S(1)}, u32[]{:S(2)}, u32[]{:S(2)}) collective-permute-start(f32[3,7,8,128]{3,2,1,0:T(8,128)S(1)} %get-tuple-element.39), channel_id=1, source_target_pairs={{16,32},{48,64},{80,96},{112,128},{144,160},{176,192},{208,224},{2... | collective-permute-start | bytes 258056 | tf_op jit(solution)/shard_map/ppermute | solution.py:502
  1.5 8.4 %collective-permute-start = (f32[3,7,8,128]{3,2,1,0:T(8,128)S(1)}, f32[3,7,8,128]{3,2,1,0:T(8,128)S(1)}, u32[]{:S(2)}, u32[]{:S(2)}) collective-permute-start(f32[3,7,8,128]{3,2,1,0:T(8,128)S(1)} %get-tuple-element.40), channel_id=1, source_target_pairs={{0,16},{32,48},{64,80},{96,112},{128,144},{160,176},{192,208},{224... | collective-permute-start | bytes 258056 | tf_op jit(solution)/shard_map/ppermute | solution.py:502
  10.0 9.1 %collective-permute-start.2 = (f32[49,8,128]{2,1,0:T(8,128)S(1)}, f32[49,8,128]{2,1,0:T(8,128)S(1)}, u32[]{:S(2)}, u32[]{:S(2)}) collective-permute-start(f32[49,8,128]{2,1,0:T(8,128)S(1)} %get-tuple-element.22), channel_id=1, source_target_pairs={{1,2},{3,4},{5,6},{7,8},{9,10},{11,12},{13,14},{2,1},{4,3},{6,5},{... | collective-permute-start | bytes 602120 | tf_op jit(solution)/shard_map/ppermute | solution.py:502
  15.7 3.4 %collective-permute-start.3 = (f32[49,8,128]{2,1,0:T(8,128)S(1)}, f32[49,8,128]{2,1,0:T(8,128)S(1)}, u32[]{:S(2)}, u32[]{:S(2)}) collective-permute-start(f32[49,8,128]{2,1,0:T(8,128)S(1)} %get-tuple-element.23), channel_id=1, source_target_pairs={{0,1},{2,3},{4,5},{6,7},{8,9},{10,11},{12,13},{14,15},{1,0},{3,2},... | collective-permute-start | bytes 602120 | tf_op jit(solution)/shard_map/ppermute | solution.py:502
  39.7 19.5 %all-to-all-start.1 = ((f32[8,64,128]{2,1,0:T(8,128)}), f32[8,64,128]{2,1,0:T(8,128)S(1)}, u32[]{:S(2)}, u32[]{:S(2)}) async-start(f32[8,64,128]{2,1,0:T(8,128)} %broadcast_in_dim.17), calls=%async_computation.1 | async-start | bytes 524288 | tf_op jit(solution)/shard_map/all_to_all | solution.py:507
  49.2 8.8 %collective-permute-start.5 = (f32[24,128]{1,0:T(8,128)S(1)}, f32[24,128]{1,0:T(8,128)S(1)}, u32[]{:S(2)}, u32[]{:S(2)}) collective-permute-start(f32[24,128]{1,0:T(8,128)S(1)} %reshape.15.vmid), channel_id=1, source_target_pairs={{1,2},{3,4},{5,6},{7,8},{9,10},{11,12},{13,14},{2,1},{4,3},{6,5},{... | collective-permute-start | bytes 36872 | tf_op jit(solution)/shard_map/ppermute | solution.py:502
  56.1 3.1 %collective-permute-start.4 = (f32[24,128]{1,0:T(8,128)S(1)}, f32[24,128]{1,0:T(8,128)S(1)}, u32[]{:S(2)}, u32[]{:S(2)}) collective-permute-start(f32[24,128]{1,0:T(8,128)S(1)} %reshape.15.vmid), channel_id=1, source_target_pairs={{0,1},{2,3},{4,5},{6,7},{8,9},{10,11},{12,13},{14,15},{1,0},{3,2},... | collective-permute-start | bytes 36872 | tf_op jit(solution)/shard_map/ppermute | solution.py:502
  59.2 7.0 %collective-permute-start.6 = (f32[512,128]{1,0:T(8,128)S(1)}, f32[512,128]{1,0:T(8,128)S(1)}, u32[]{:S(2)}, u32[]{:S(2)}) collective-permute-start(f32[512,128]{1,0:T(8,128)S(1)} %bitcast.10), channel_id=1, source_target_pairs={{0,1},{2,3},{4,5},{6,7},{8,9},{10,11},{12,13},{14,15},{1,0},{3,2},... | collective-permute-start | bytes 786440 | tf_op jit(solution)/shard_map/ppermute | solution.py:502

commit v9 on v8

--- a/solution.py
+++ b/solution.py
@@ -71,8 +71,22 @@
             i: KEEP * v[i] + self.inv[i] * (source[i] + self.around(v, i)) for i in range(first, end)
         }
 
+    def sweep_into(self, out, v, source, first, end):
+        def body(i):
+            out[i] = KEEP * v[i] + self.inv[i] * (source[i] + self.around(v, i))
+
+        over(first, end, body)
+
     def residual(self, v, source, first, end):
         return {i: source[i] - self.diag[i] * v[i] + self.around(v, i) for i in range(first, end)}
+
+
+def over(first, end, body, step=2):
+    def some(s, _):
+        for u in range(step):
+            body(first + step * s + u)
+
+    lax.fori_loop(0, (end - first) // step, some, None)
 
 
 class Stored:
@@ -232,7 +246,7 @@
 
     def sweeps(self, v, source, count):
         step = lambda _, v: tuple(self.sweep(list(v), source))
-        return list(lax.fori_loop(0, count, step, tuple(v), unroll=True))
+        return list(lax.fori_loop(0, count, step, tuple(v)))
 
     def residual(self, v, source):
         around = self.around(v)
@@ -247,13 +261,13 @@
     return jnp.concatenate([rows(c[8:], -1), c[:8]], axis=0)
 
 
-UNROLL = 15
+UNROLL = 5
 PAD = 3
 
 
 def up_kernel(
     mine, other, v0, f0, f1, wx0, wy0, wz0, inv0, wx1, wy1, wz1, inv1, vmid, vnear, vfar, out,
-    k2, f2, va, vb, wxi, wxe, wyi, wye, wz2, diag2, inv2, sumk, sumr, e3,
+    k2, f2, va, vb, wxi, wxe, wyi, wye, wz2, diag2, inv2, sumk, sumr, e3, v1a, v1b, v0a, v0b,
 ):
     gx, gy = lax.axis_index("gx"), lax.axis_index("gy")
     first = core_mask(8)
@@ -267,12 +281,14 @@
         for i in range(PAD):
             ref[i] = zero
             ref[32 + PAD + i] = zero
-    for i in range(32):
+    def unpack(i):
         for c, ref in ((0, f2), (1, k2)):
             here = pl.ds(2 * i + c, 8, stride=64)
             a, b = mine[here, :], other[here, :]
             ref[i + PAD, :8] = jnp.where(first, a, b)
             ref[i + PAD, 8:] = jnp.where(first, b, a)
+
+    over(0, 32, unpack, 8)
 
     def sides(c):
         up, down = lanes(c, 32), lanes(c, -32)
@@ -469,25 +485,32 @@
         c = joined(first, *c)
         return jnp.where(second, lanes(c, 1), c)
 
-    v = {i: received(i) + correction(i) for i in range(-3, 7)}
-    v = middle.sweep(v, source, -2, 6)
-    v = middle.sweep(v, source, -1, 5)
+    v, w = Stored(v1a, -3), Stored(v1b, -2)
+    for i in range(-3, 7):
+        v[i] = received(i) + correction(i)
+    middle.sweep_into(w, v, source, -2, 6)
+    middle.sweep_into(v, w, source, -1, 5)
 
     odd_lane = iota((ROWS, 128), 1) % 2 == 1
     odd_row = iota((ROWS, 128), 0) % 2 == 1
     fine = Window(1, (-1, 9))
     fine.given(wx0, wy0, wz0, inv0)
-    source = Stored(f0, -1)
-    base = Stored(v0, -2)
-    spread1 = {}
-    for i in range(-1, 5):
+    source, base, post, half = Stored(f0, -1), Stored(v0, -2), Stored(v0a, -2), Stored(v0b, -1)
+
+    def prolong(i):
         c = jnp.where(odd_lane, lanes(v[i], -1), v[i])
-        spread1[i] = jnp.where(odd_row, rows(c, -1), c)
-    v = {i: base[i] + spread1[i // 2] for i in range(-2, 10)}
-    v = fine.sweep(v, source, -1, 9)
-    v = fine.sweep(v, source, 0, 8)
-    for i in range(8):
-        out[i] = v[i][8:16]
+        c = jnp.where(odd_row, rows(c, -1), c)
+        post[2 * i] = base[2 * i] + c
+        post[2 * i + 1] = base[2 * i + 1] + c
+
+    over(-1, 5, prolong)
+    fine.sweep_into(half, post, source, -1, 9)
+
+    def last(i):
+        c = KEEP * half[i] + fine.inv[i] * (source[i] + fine.around(half, i))
+        out[i] = c[8:16]
+
+    over(0, 8, last)
 
 
 WINDOW_PLANES = (12, 10, 8, 11, 10, 10, 10, 9, 8, 8, 8)
@@ -550,7 +573,9 @@
         up_kernel,
         in_specs=[array] * (5 + len(WINDOW_PLANES)),
         out_shape=f32(8, 8, 128),
-        scratch_shapes=[plane] * 13 + [pltpu.VMEM((8, 16, 128), jnp.float32)],
+        scratch_shapes=[plane] * 13
+        + [pltpu.VMEM((8, 16, 128), jnp.float32)]
+        + [pltpu.VMEM((n, ROWS, 128), jnp.float32) for n in (10, 8, 12, 10)],
         compiler_params=params,
         name="up",
     )(mine, other, *window, vmid, vnear, vfar)

time: 75.1 us -> 75.4 us (level)
  no operation moved by 1% of the time
where the time goes in v9:
time: 75.4 us; the launch traced here: 74.9 us
  starting transfers between devices  38.9 us (52%)
  blocking collectives  18.2 us (24%)
  Pallas kernels  10.4 us (14%)
  waiting for transfers between devices  5.59 us (7%)
  local copies, waits for them, and re-layouts  0.89 us (1%)
  other arithmetic  0.81 us (1%)
    ppermute x7, starting transfers between devices, swap(): return lax.ppermute(x, axis, pairs + [(b, a) for a, b in pairs])  29.5 us
    all_to_all x1, blocking collectives, to_all(): return lax.all_to_all(copies, axis, 0, 0, axis_index_groups=groups)  18.2 us
    all_to_all x1, starting transfers between devices, to_all(): return lax.all_to_all(copies, axis, 0, 0, axis_index_groups=groups)  9.48 us
    pallas_call x1, Pallas kernels, shards(): pl.pallas_call(up_kernel, in_specs=[array] * (5 + len(WINDOW_PLANES)), ou...  8.79 us
    ppermute x7, waiting for transfers between devices, swap(): return lax.ppermute(x, axis, pairs + [(b, a) for a, b in pairs])  5.58 us
    pallas_call x1, Pallas kernels, shards(): pl.pallas_call(down_kernel, in_specs=[array] * 5, out_shape=(f32(10, 128)...  1.58 us
  transfers between devices with their start and end apart: 8, of which 4 were waited for; matrix products, arithmetic and copies ran while one was open for 0% of the time, Pallas kernels for 0%

profile of v9, /device:TPU:1, one launch (start us, length us, event | category | flops | bytes accessed | tf_op | source)
XLA Modules:
  0.0 74.9 jit_solution(907425830199116517)
XLA Ops:
  0.0 0.8 %pad_maximum_fusion = f32[24,8,128]{2,1,0:T(8,128)S(1)} fusion(f32[8,8,128]{2,1,0:T(8,128)} %param.5, f32[8,8,128]{2,1,0:T(8,128)} %param.4, f32[8,8,128]{2,1,0:T(8,128)} %param.3), kind=kLoop, calls=%fused_computation.2 | loop fusion | flops 49152 | bytes 196608 | tf_op jit(solution)/shard_map/concatenate | solution.py:535
  0.8 0.7 collective-permute-start.1
  1.5 6.6 %collective-permute-start = (f32[3,7,8,128]{3,2,1,0:T(8,128)S(1)}, f32[3,7,8,128]{3,2,1,0:T(8,128)S(1)}, u32[]{:S(2)}, u32[]{:S(2)}) collective-permute-start(f32[3,7,8,128]{3,2,1,0:T(8,128)S(1)} %get-tuple-element.40), channel_id=1, source_target_pairs={{0,16},{32,48},{64,80},{96,112},{128,144},{160,176},{192,208},{224... | collective-permute-start | bytes 258056 | tf_op jit(solution)/shard_map/ppermute | solution.py:525
  8.1 0.0 collective-permute-done.1.far.xfar
  8.1 1.8 %collective-permute-done.near.xnear = f32[3,7,8,128]{3,2,1,0:T(8,128)S(1)} collective-permute-done((f32[3,7,8,128]{3,2,1,0:T(8,128)S(1)}, f32[3,7,8,128]{3,2,1,0:T(8,128)S(1)}, u32[]{:S(2)}, u32[]{:S(2)}) %collective-permute-start) | collective-permute-done | bytes 86048 | tf_op jit(solution)/shard_map/ppermute | solution.py:525
  10.0 5.7 %collective-permute-start.2 = (f32[49,8,128]{2,1,0:T(8,128)S(1)}, f32[49,8,128]{2,1,0:T(8,128)S(1)}, u32[]{:S(2)}, u32[]{:S(2)}) collective-permute-start(f32[49,8,128]{2,1,0:T(8,128)S(1)} %get-tuple-element.22), channel_id=1, source_target_pairs={{1,2},{3,4},{5,6},{7,8},{9,10},{11,12},{13,14},{2,1},{4,3},{6,5},{... | collective-permute-start | bytes 602120 | tf_op jit(solution)/shard_map/ppermute | solution.py:525
  15.7 1.9 %collective-permute-start.3 = (f32[49,8,128]{2,1,0:T(8,128)S(1)}, f32[49,8,128]{2,1,0:T(8,128)S(1)}, u32[]{:S(2)}, u32[]{:S(2)}) collective-permute-start(f32[49,8,128]{2,1,0:T(8,128)S(1)} %get-tuple-element.23), channel_id=1, source_target_pairs={{0,1},{2,3},{4,5},{6,7},{8,9},{10,11},{12,13},{14,15},{1,0},{3,2},... | collective-permute-start | bytes 602120 | tf_op jit(solution)/shard_map/ppermute | solution.py:525
  17.6 1.5 %collective-permute-done.2.far = f32[49,8,128]{2,1,0:T(8,128)S(1)} collective-permute-done((f32[49,8,128]{2,1,0:T(8,128)S(1)}, f32[49,8,128]{2,1,0:T(8,128)S(1)}, u32[]{:S(2)}, u32[]{:S(2)}) %collective-permute-start.2) | collective-permute-done | bytes 200736 | tf_op jit(solution)/shard_map/ppermute | solution.py:525
  19.1 0.0 collective-permute-done.3.near
  19.1 1.6 %down.1 = (f32[10,128]{1,0:T(8,128)S(1)}, f32[12,24,128]{2,1,0:T(8,128)S(1)}, f32[10,24,128]{2,1,0:T(8,128)S(1)}, f32[8,24,128]{2,1,0:T(8,128)S(1)}, f32[11,24,1...) custom-call(f32[3,8,8,128]{3,2,1,0:T(8,128)S(1)} %bitcast.9, ...), custom_call_target="tpu_custom_call" | custom-call | tf_op jit(solution)/shard_map/down/pallas_call | solution.py:553
  20.7 0.1 broadcast_in_dim.15
  20.8 18.2 %all_to_all.10 = f32[32,1,1280]{2,1,0:T(1,128)S(1)} all-to-all(f32[32,1,1280]{2,1,0:T(1,128)S(1)} %broadcast_in_dim.15), channel_id=1, replica_groups=mesh['gx'=32,'gy'=16] {'gx'}, dimensions={0} | all-to-all | bytes 327680 | tf_op jit(solution)/shard_map/all_to_all | solution.py:530
  39.0 0.7 broadcast_in_dim.17
  39.7 9.5 %all-to-all-start.1 = ((f32[8,64,128]{2,1,0:T(8,128)}), f32[8,64,128]{2,1,0:T(8,128)S(1)}, u32[]{:S(2)}, u32[]{:S(2)}) async-start(f32[8,64,128]{2,1,0:T(8,128)} %broadcast_in_dim.17), calls=%async_computation.1 | async-start | bytes 524288 | tf_op jit(solution)/shard_map/all_to_all | solution.py:530
  49.2 6.9 %collective-permute-start.5 = (f32[24,128]{1,0:T(8,128)S(1)}, f32[24,128]{1,0:T(8,128)S(1)}, u32[]{:S(2)}, u32[]{:S(2)}) collective-permute-start(f32[24,128]{1,0:T(8,128)S(1)} %reshape.15.vmid), channel_id=1, source_target_pairs={{1,2},{3,4},{5,6},{7,8},{9,10},{11,12},{13,14},{2,1},{4,3},{6,5},{... | collective-permute-start | bytes 36872 | tf_op jit(solution)/shard_map/ppermute | solution.py:525
  56.1 1.9 %collective-permute-start.4 = (f32[24,128]{1,0:T(8,128)S(1)}, f32[24,128]{1,0:T(8,128)S(1)}, u32[]{:S(2)}, u32[]{:S(2)}) collective-permute-start(f32[24,128]{1,0:T(8,128)S(1)} %reshape.15.vmid), channel_id=1, source_target_pairs={{0,1},{2,3},{4,5},{6,7},{8,9},{10,11},{12,13},{14,15},{1,0},{3,2},... | collective-permute-start | bytes 36872 | tf_op jit(solution)/shard_map/ppermute | solution.py:525
  58.1 0.0 collective-permute-done.5.vfar
  58.1 1.1 %collective-permute-done.4.vnear = f32[24,128]{1,0:T(8,128)S(1)} collective-permute-done((f32[24,128]{1,0:T(8,128)S(1)}, f32[24,128]{1,0:T(8,128)S(1)}, u32[]{:S(2)}, u32[]{:S(2)}) %collective-permute-start.4) | collective-permute-done | bytes 12320 | tf_op jit(solution)/shard_map/ppermute | solution.py:525
  59.2 0.0 all-to-all-done.1
  59.2 5.8 %collective-permute-start.6 = (f32[512,128]{1,0:T(8,128)S(1)}, f32[512,128]{1,0:T(8,128)S(1)}, u32[]{:S(2)}, u32[]{:S(2)}) collective-permute-start(f32[512,128]{1,0:T(8,128)S(1)} %bitcast.10), channel_id=1, source_target_pairs={{0,1},{2,3},{4,5},{6,7},{8,9},{10,11},{12,13},{14,15},{1,0},{3,2},... | collective-permute-start | bytes 786440 | tf_op jit(solution)/shard_map/ppermute | solution.py:525
  65.0 1.1 %collective-permute-done.6.other = f32[512,128]{1,0:T(8,128)S(1)} collective-permute-done((f32[512,128]{1,0:T(8,128)S(1)}, f32[512,128]{1,0:T(8,128)S(1)}, u32[]{:S(2)}, u32[]{:S(2)}) %collective-permute-start.6) | collective-permute-done | bytes 262176 | tf_op jit(solution)/shard_map/ppermute | solution.py:525
  66.2 8.8 %up.1 = f32[8,8,128]{2,1,0:T(8,128)} custom-call(f32[512,128]{1,0:T(8,128)S(1)} %bitcast.11, f32[512,128]{1,0:T(8,128)S(1)} %collective-permute-done.6.other, f32[12,24,128]{2,1,0:T(8,128)S(1)} %get-tuple-element.26.v0, f32[10,24,128]{2,1,0:T(8,128)S(1)} %get-tuple-element.27.f0, f32[8,24,128]{2,1,0:T(8,128)S(1)} %get-tuple-element.28.f1, ...), custom_call_target="tpu_custom_call" | custom-call | tf_op jit(solution)/shard_map/up/pallas_call | solution.py:572
  (7 shorter events, 0.1 us)
Async XLA Ops:
  0.8 7.3 %collective-permute-start.1 = (f32[3,7,8,128]{3,2,1,0:T(8,128)S(1)}, f32[3,7,8,128]{3,2,1,0:T(8,128)S(1)}, u32[]{:S(2)}, u32[]{:S(2)}) collective-permute-start(f32[3,7,8,128]{3,2,1,0:T(8,128)S(1)} %get-tuple-element.39), channel_id=1, source_target_pairs={{16,32},{48,64},{80,96},{112,128},{144,160},{176,192},{208,224},{2... | collective-permute-start | bytes 258056 | tf_op jit(solution)/shard_map/ppermute | solution.py:525
  1.5 8.4 %collective-permute-start = (f32[3,7,8,128]{3,2,1,0:T(8,128)S(1)}, f32[3,7,8,128]{3,2,1,0:T(8,128)S(1)}, u32[]{:S(2)}, u32[]{:S(2)}) collective-permute-start(f32[3,7,8,128]{3,2,1,0:T(8,128)S(1)} %get-tuple-element.40), channel_id=1, source_target_pairs={{0,16},{32,48},{64,80},{96,112},{128,144},{160,176},{192,208},{224... | collective-permute-start | bytes 258056 | tf_op jit(solution)/shard_map/ppermute | solution.py:525
  10.0 9.1 %collective-permute-start.2 = (f32[49,8,128]{2,1,0:T(8,128)S(1)}, f32[49,8,128]{2,1,0:T(8,128)S(1)}, u32[]{:S(2)}, u32[]{:S(2)}) collective-permute-start(f32[49,8,128]{2,1,0:T(8,128)S(1)} %get-tuple-element.22), channel_id=1, source_target_pairs={{1,2},{3,4},{5,6},{7,8},{9,10},{11,12},{13,14},{2,1},{4,3},{6,5},{... | collective-permute-start | bytes 602120 | tf_op jit(solution)/shard_map/ppermute | solution.py:525
  15.7 3.4 %collective-permute-start.3 = (f32[49,8,128]{2,1,0:T(8,128)S(1)}, f32[49,8,128]{2,1,0:T(8,128)S(1)}, u32[]{:S(2)}, u32[]{:S(2)}) collective-permute-start(f32[49,8,128]{2,1,0:T(8,128)S(1)} %get-tuple-element.23), channel_id=1, source_target_pairs={{0,1},{2,3},{4,5},{6,7},{8,9},{10,11},{12,13},{14,15},{1,0},{3,2},... | collective-permute-start | bytes 602120 | tf_op jit(solution)/shard_map/ppermute | solution.py:525
  39.7 19.5 %all-to-all-start.1 = ((f32[8,64,128]{2,1,0:T(8,128)}), f32[8,64,128]{2,1,0:T(8,128)S(1)}, u32[]{:S(2)}, u32[]{:S(2)}) async-start(f32[8,64,128]{2,1,0:T(8,128)} %broadcast_in_dim.17), calls=%async_computation.1 | async-start | bytes 524288 | tf_op jit(solution)/shard_map/all_to_all | solution.py:530
  49.2 8.8 %collective-permute-start.5 = (f32[24,128]{1,0:T(8,128)S(1)}, f32[24,128]{1,0:T(8,128)S(1)}, u32[]{:S(2)}, u32[]{:S(2)}) collective-permute-start(f32[24,128]{1,0:T(8,128)S(1)} %reshape.15.vmid), channel_id=1, source_target_pairs={{1,2},{3,4},{5,6},{7,8},{9,10},{11,12},{13,14},{2,1},{4,3},{6,5},{... | collective-permute-start | bytes 36872 | tf_op jit(solution)/shard_map/ppermute | solution.py:525
  56.1 3.1 %collective-permute-start.4 = (f32[24,128]{1,0:T(8,128)S(1)}, f32[24,128]{1,0:T(8,128)S(1)}, u32[]{:S(2)}, u32[]{:S(2)}) collective-permute-start(f32[24,128]{1,0:T(8,128)S(1)} %reshape.15.vmid), channel_id=1, source_target_pairs={{0,1},{2,3},{4,5},{6,7},{8,9},{10,11},{12,13},{14,15},{1,0},{3,2},... | collective-permute-start | bytes 36872 | tf_op jit(solution)/shard_map/ppermute | solution.py:525
  59.2 7.0 %collective-permute-start.6 = (f32[512,128]{1,0:T(8,128)S(1)}, f32[512,128]{1,0:T(8,128)S(1)}, u32[]{:S(2)}, u32[]{:S(2)}) collective-permute-start(f32[512,128]{1,0:T(8,128)S(1)} %bitcast.10), channel_id=1, source_target_pairs={{0,1},{2,3},{4,5},{6,7},{8,9},{10,11},{12,13},{14,15},{1,0},{3,2},... | collective-permute-start | bytes 786440 | tf_op jit(solution)/shard_map/ppermute | solution.py:525

commit v10 on v8

--- a/solution.py
+++ b/solution.py
@@ -139,7 +139,7 @@
 
 
 def down_kernel(
-    own, xnear, xfar, far, near, packed, v0_out, f0_out, f1_out, wx0, wy0, wz0, inv0, wx1, wy1, wz1, inv1
+    own, xnear, xfar, far, near, lower, higher, v1_out, v0_out, f0_out, f1_out, wx0, wy0, wz0, inv0, wx1, wy1, wz1, inv1
 ):
     first = core_mask(8)
 
@@ -181,8 +181,12 @@
     for i in range(4):
         c = v[i][8:16]
         c = jnp.where(even, c, lanes(rows(c, 2), -1))
-        packed[2 * i + 2 : 2 * i + 3, :] = c[0:1]
-        packed[2 * i + 3 : 2 * i + 4, :] = c[4:5]
+        for n, line in enumerate((c[0:1], c[4:5])):
+            v1_out[2 * i + n : 2 * i + n + 1, :] = line
+            if i < 3:
+                lower[2 * i + n + 2 : 2 * i + n + 3, :] = line
+            if i > 0:
+                higher[2 * i + n : 2 * i + n + 1, :] = line
     r = middle.residual(v, source, 0, 4)
 
     source = [0.5 * block_sum(r[2 * i], r[2 * i + 1], 2)[8:16] for i in range(2)]
@@ -194,7 +198,9 @@
         dense = [jnp.take_along_axis(t, pick, axis=1) for t in planes]
         dense = jnp.where(group < 2, dense[0], dense[1])
         dense = jnp.where(row == 4 * (group % 2), dense, 0.0)
-        packed[c : c + 1, :] = jnp.sum(dense, axis=0, keepdims=True)
+        dense = jnp.sum(dense, axis=0, keepdims=True)
+        lower[c : c + 1, :] = dense
+        higher[c : c + 1, :] = dense
 
 
 class Coarse:
@@ -247,12 +253,12 @@
     return jnp.concatenate([rows(c[8:], -1), c[:8]], axis=0)
 
 
-UNROLL = 15
+UNROLL = 10
 PAD = 3
 
 
 def up_kernel(
-    mine, other, v0, f0, f1, wx0, wy0, wz0, inv0, wx1, wy1, wz1, inv1, vmid, vnear, vfar, out,
+    mine, other, v0, f0, f1, wx0, wy0, wz0, inv0, wx1, wy1, wz1, inv1, vmid, vfar, vnear, out,
     k2, f2, va, vb, wxi, wxe, wyi, wye, wz2, diag2, inv2, sumk, sumr, e3,
 ):
     gx, gy = lax.axis_index("gx"), lax.axis_index("gy")
@@ -464,7 +470,7 @@
     second = (iota((ROWS, 128), 0) & 2) != 0
 
     def received(i):
-        n = 2 * i + 8
+        n = 2 * i + 6
         c = [jnp.where(upper_half, r[n + 1 : n + 2], r[n : n + 1]) for r in (vmid, vnear, vfar)]
         c = joined(first, *c)
         return jnp.where(second, lanes(c, 1), c)
@@ -527,22 +533,26 @@
     from_far = swap(to_far, "gy", 1)
     from_near = swap(to_near, "gy", 0)
 
-    packed, *window = pl.pallas_call(
+    lower, higher, v1, *window = pl.pallas_call(
         down_kernel,
         in_specs=[array] * 5,
-        out_shape=(f32(10, 128),) + tuple(f32(n, ROWS, 128) for n in WINDOW_PLANES),
+        out_shape=(f32(8, 128),) * 3 + tuple(f32(n, ROWS, 128) for n in WINDOW_PLANES),
         compiler_params=params,
         name="down",
     )(own, near, far, from_far, from_near)
 
-    blocks = to_all(packed.reshape(1, 1280), "gx", 32)
+    gx = lax.axis_index("gx")
+    before = lax.broadcasted_iota(jnp.int32, (32, 1, 1), 0) < gx
+    blocks = jnp.where(before, lower.reshape(1, 1, 1024), higher.reshape(1, 1, 1024))
+    blocks = lax.all_to_all(blocks, "gx", 0, 0)
     same_core = [[2 * z + c for z in range(8)] for c in range(2)]
     mine = to_all(blocks[:, :, :256].reshape(64, 128), "gy", 8, same_core).reshape(512, 128)
-    v1 = jnp.pad(blocks[:, 0, 256:], ((1, 1), (0, 0)))
-    place = (lax.axis_index("gx"), jnp.int32(0))
-    vmid = lax.dynamic_slice(v1, place, (3, 1024)).reshape(24, 128)
+    beside = jnp.pad(blocks[:, 0, 256:], ((1, 1), (0, 0)))
+    low = lax.dynamic_slice(beside, (gx, jnp.int32(0)), (1, 768))
+    high = lax.dynamic_slice(beside, (gx + 2, jnp.int32(0)), (1, 768))
+    vmid = jnp.concatenate([low.reshape(6, 128), v1, high.reshape(6, 128)])
     vnear, vfar = swap(vmid, "gy", 0), swap(vmid, "gy", 1)
-    mine, vnear, vfar = lax.optimization_barrier((mine, vnear, vfar))
+    mine, vfar, vnear = lax.optimization_barrier((mine, vfar, vnear))
     other = swap(mine, "gy", 0)
 
     plane = pltpu.VMEM((32 + 2 * PAD, 16, 128), jnp.float32)
@@ -553,7 +563,7 @@
         scratch_shapes=[plane] * 13 + [pltpu.VMEM((8, 16, 128), jnp.float32)],
         compiler_params=params,
         name="up",
-    )(mine, other, *window, vmid, vnear, vfar)
+    )(mine, other, *window, vmid, vfar, vnear)
 
 
 def solution(mesh):

time: 75.1 us -> 74.7 us (level)
  blocking collectives: 18.2 us -> 20.7 us
  Pallas kernels: 10.1 us -> 8.57 us
  waiting for transfers between devices: 5.59 us -> 4.5 us
    all_to_all x1, blocking collectives: 18.2 us -> 20.7 us  [shards(): blocks = lax.all_to_all(blocks, 'gx', 0, 0)]
    pallas_call x1, Pallas kernels: 8.45 us -> 6.96 us  [shards(): pl.pallas_call(up_kernel, in_specs=[array] * (5 + len(WINDOW_PLANES)), ou...]
    ppermute x7, waiting for transfers between devices: 5.58 us -> 4.5 us  [swap(): return lax.ppermute(x, axis, pairs + [(b, a) for a, b in pairs])]
where the time goes in v10:
time: 74.7 us; the launch traced here: 74.3 us
  starting transfers between devices  38.6 us (52%)
  blocking collectives  20.7 us (28%)
  Pallas kernels  8.57 us (11%)
  waiting for transfers between devices  4.5 us (6%)
  other arithmetic  0.96 us (1%)
  local copies, waits for them, and re-layouts  0.8 us (1%)
    ppermute x7, starting transfers between devices, swap(): return lax.ppermute(x, axis, pairs + [(b, a) for a, b in pairs])  29.2 us
    all_to_all x1, blocking collectives, shards(): blocks = lax.all_to_all(blocks, 'gx', 0, 0)  20.7 us
    all_to_all x1, starting transfers between devices, to_all(): return lax.all_to_all(copies, axis, 0, 0, axis_index_groups=groups)  9.38 us
    pallas_call x1, Pallas kernels, shards(): pl.pallas_call(up_kernel, in_specs=[array] * (5 + len(WINDOW_PLANES)), ou...  6.96 us
    ppermute x7, waiting for transfers between devices, swap(): return lax.ppermute(x, axis, pairs + [(b, a) for a, b in pairs])  4.5 us
    pallas_call x1, Pallas kernels, shards(): pl.pallas_call(down_kernel, in_specs=[array] * 5, out_shape=(f32(8, 128),...  1.58 us
  transfers between devices with their start and end apart: 8, of which 4 were waited for; matrix products, arithmetic and copies ran while one was open for 0% of the time, Pallas kernels for 0%

profile of v10, /device:TPU:1, one launch (start us, length us, event | category | flops | bytes accessed | tf_op | source)
XLA Modules:
  0.0 74.3 jit_solution(8056810954934111130)
XLA Ops:
  0.0 0.8 %pad_maximum_fusion = f32[24,8,128]{2,1,0:T(8,128)S(1)} fusion(f32[8,8,128]{2,1,0:T(8,128)} %param.5, f32[8,8,128]{2,1,0:T(8,128)} %param.4, f32[8,8,128]{2,1,0:T(8,128)} %param.3), kind=kLoop, calls=%fused_computation.3 | loop fusion | flops 49152 | bytes 196608 | tf_op jit(solution)/shard_map/concatenate | solution.py:518
  0.8 4.0 %collective-permute-start = (f32[3,7,8,128]{3,2,1,0:T(8,128)S(1)}, f32[3,7,8,128]{3,2,1,0:T(8,128)S(1)}, u32[]{:S(2)}, u32[]{:S(2)}) collective-permute-start(f32[3,7,8,128]{3,2,1,0:T(8,128)S(1)} %get-tuple-element.46), channel_id=1, source_target_pairs={{0,16},{32,48},{64,80},{96,112},{128,144},{160,176},{192,208},{224... | collective-permute-start | bytes 258056 | tf_op jit(solution)/shard_map/ppermute | solution.py:508
  4.9 0.7 collective-permute-start.1
  5.5 1.2 %collective-permute-done.near.xnear = f32[3,7,8,128]{3,2,1,0:T(8,128)S(1)} collective-permute-done((f32[3,7,8,128]{3,2,1,0:T(8,128)S(1)}, f32[3,7,8,128]{3,2,1,0:T(8,128)S(1)}, u32[]{:S(2)}, u32[]{:S(2)}) %collective-permute-start) | collective-permute-done | bytes 86048 | tf_op jit(solution)/shard_map/ppermute | solution.py:508
  6.7 0.0 collective-permute-done.1.far.xfar
  6.8 5.9 %collective-permute-start.2 = (f32[49,8,128]{2,1,0:T(8,128)S(1)}, f32[49,8,128]{2,1,0:T(8,128)S(1)}, u32[]{:S(2)}, u32[]{:S(2)}) collective-permute-start(f32[49,8,128]{2,1,0:T(8,128)S(1)} %get-tuple-element.24), channel_id=1, source_target_pairs={{1,2},{3,4},{5,6},{7,8},{9,10},{11,12},{13,14},{2,1},{4,3},{6,5},{... | collective-permute-start | bytes 602120 | tf_op jit(solution)/shard_map/ppermute | solution.py:508
  12.6 4.1 %collective-permute-start.3 = (f32[49,8,128]{2,1,0:T(8,128)S(1)}, f32[49,8,128]{2,1,0:T(8,128)S(1)}, u32[]{:S(2)}, u32[]{:S(2)}) collective-permute-start(f32[49,8,128]{2,1,0:T(8,128)S(1)} %get-tuple-element.25), channel_id=1, source_target_pairs={{0,1},{2,3},{4,5},{6,7},{8,9},{10,11},{12,13},{14,15},{1,0},{3,2},... | collective-permute-start | bytes 602120 | tf_op jit(solution)/shard_map/ppermute | solution.py:508
  16.7 0.0 collective-permute-done.2.far
  16.7 1.0 %collective-permute-done.3.near = f32[49,8,128]{2,1,0:T(8,128)S(1)} collective-permute-done((f32[49,8,128]{2,1,0:T(8,128)S(1)}, f32[49,8,128]{2,1,0:T(8,128)S(1)}, u32[]{:S(2)}, u32[]{:S(2)}) %collective-permute-start.3) | collective-permute-done | bytes 200736 | tf_op jit(solution)/shard_map/ppermute | solution.py:508
  17.8 1.6 %down.1 = (f32[8,128]{1,0:T(8,128)S(1)}, f32[8,128]{1,0:T(8,128)S(1)}, f32[8,128]{1,0:T(8,128)S(1)}, f32[12,24,128]{2,1,0:T(8,128)S(1)}, f32[10,24,128]{2,1,0:T(...) custom-call(f32[3,8,8,128]{3,2,1,0:T(8,128)S(1)} %bitcast.12, ...), custom_call_target="tpu_custom_call" | custom-call | tf_op jit(solution)/shard_map/down/pallas_call | solution.py:536
  19.4 0.1 broadcast_select_fusion
  19.5 20.7 %all_to_all.10 = f32[32,1,1024]{2,1,0:T(1,128)S(1)} all-to-all(f32[32,1,1024]{2,1,0:T(1,128)S(1)} %broadcast_select_fusion), channel_id=1, replica_groups=mesh['gx'=32,'gy'=16] {'gx'}, dimensions={0} | all-to-all | bytes 262144 | tf_op jit(solution)/shard_map/all_to_all | solution.py:547
  40.2 0.7 broadcast_in_dim.41
  40.9 9.4 %all-to-all-start.1 = ((f32[8,64,128]{2,1,0:T(8,128)}), f32[8,64,128]{2,1,0:T(8,128)S(1)}, u32[]{:S(2)}, u32[]{:S(2)}) async-start(f32[8,64,128]{2,1,0:T(8,128)} %broadcast_in_dim.41), calls=%async_computation.1 | async-start | bytes 524288 | tf_op jit(solution)/shard_map/all_to_all | solution.py:513
  50.4 6.9 %collective-permute-start.4 = (f32[20,128]{1,0:T(8,128)S(1)}, f32[20,128]{1,0:T(8,128)S(1)}, u32[]{:S(2)}, u32[]{:S(2)}) collective-permute-start(f32[20,128]{1,0:T(8,128)S(1)} %pad_maximum_fusion.1.vmid), channel_id=1, source_target_pairs={{1,2},{3,4},{5,6},{7,8},{9,10},{11,12},{13,14},{2,1},{4,3},{6,5},{... | collective-permute-start | bytes 30728 | tf_op jit(solution)/shard_map/ppermute | solution.py:508
  57.3 1.9 %collective-permute-start.5 = (f32[20,128]{1,0:T(8,128)S(1)}, f32[20,128]{1,0:T(8,128)S(1)}, u32[]{:S(2)}, u32[]{:S(2)}) collective-permute-start(f32[20,128]{1,0:T(8,128)S(1)} %pad_maximum_fusion.1.vmid), channel_id=1, source_target_pairs={{0,1},{2,3},{4,5},{6,7},{8,9},{10,11},{12,13},{14,15},{1,0},{3,2},... | collective-permute-start | bytes 30728 | tf_op jit(solution)/shard_map/ppermute | solution.py:508
  59.2 0.0 collective-permute-done.4.vfar
  59.2 1.1 %collective-permute-done.5.vnear = f32[20,128]{1,0:T(8,128)S(1)} collective-permute-done((f32[20,128]{1,0:T(8,128)S(1)}, f32[20,128]{1,0:T(8,128)S(1)}, u32[]{:S(2)}, u32[]{:S(2)}) %collective-permute-start.5) | collective-permute-done | bytes 10272 | tf_op jit(solution)/shard_map/ppermute | solution.py:508
  60.4 0.0 all-to-all-done.1
  60.4 5.8 %collective-permute-start.6 = (f32[512,128]{1,0:T(8,128)S(1)}, f32[512,128]{1,0:T(8,128)S(1)}, u32[]{:S(2)}, u32[]{:S(2)}) collective-permute-start(f32[512,128]{1,0:T(8,128)S(1)} %bitcast.13), channel_id=1, source_target_pairs={{0,1},{2,3},{4,5},{6,7},{8,9},{10,11},{12,13},{14,15},{1,0},{3,2},... | collective-permute-start | bytes 786440 | tf_op jit(solution)/shard_map/ppermute | solution.py:508
  66.2 1.1 %collective-permute-done.6.other = f32[512,128]{1,0:T(8,128)S(1)} collective-permute-done((f32[512,128]{1,0:T(8,128)S(1)}, f32[512,128]{1,0:T(8,128)S(1)}, u32[]{:S(2)}, u32[]{:S(2)}) %collective-permute-start.6) | collective-permute-done | bytes 262176 | tf_op jit(solution)/shard_map/ppermute | solution.py:508
  67.3 7.0 %up.1 = f32[8,8,128]{2,1,0:T(8,128)} custom-call(f32[512,128]{1,0:T(8,128)S(1)} %bitcast.14, f32[512,128]{1,0:T(8,128)S(1)} %collective-permute-done.6.other, f32[12,24,128]{2,1,0:T(8,128)S(1)} %get-tuple-element.30.v0, f32[10,24,128]{2,1,0:T(8,128)S(1)} %get-tuple-element.31.f0, f32[8,24,128]{2,1,0:T(8,128)S(1)} %get-tuple-element.32.f1, ...), custom_call_target="tpu_custom_call" | custom-call | tf_op jit(solution)/shard_map/up/pallas_call | solution.py:559
  (8 shorter events, 0.1 us)
Async XLA Ops:
  0.8 5.9 %collective-permute-start = (f32[3,7,8,128]{3,2,1,0:T(8,128)S(1)}, f32[3,7,8,128]{3,2,1,0:T(8,128)S(1)}, u32[]{:S(2)}, u32[]{:S(2)}) collective-permute-start(f32[3,7,8,128]{3,2,1,0:T(8,128)S(1)} %get-tuple-element.46), channel_id=1, source_target_pairs={{0,16},{32,48},{64,80},{96,112},{128,144},{160,176},{192,208},{224... | collective-permute-start | bytes 258056 | tf_op jit(solution)/shard_map/ppermute | solution.py:508
  4.9 1.9 %collective-permute-start.1 = (f32[3,7,8,128]{3,2,1,0:T(8,128)S(1)}, f32[3,7,8,128]{3,2,1,0:T(8,128)S(1)}, u32[]{:S(2)}, u32[]{:S(2)}) collective-permute-start(f32[3,7,8,128]{3,2,1,0:T(8,128)S(1)} %get-tuple-element.45), channel_id=1, source_target_pairs={{16,32},{48,64},{80,96},{112,128},{144,160},{176,192},{208,224},{2... | collective-permute-start | bytes 258056 | tf_op jit(solution)/shard_map/ppermute | solution.py:508
  6.8 10.0 %collective-permute-start.2 = (f32[49,8,128]{2,1,0:T(8,128)S(1)}, f32[49,8,128]{2,1,0:T(8,128)S(1)}, u32[]{:S(2)}, u32[]{:S(2)}) collective-permute-start(f32[49,8,128]{2,1,0:T(8,128)S(1)} %get-tuple-element.24), channel_id=1, source_target_pairs={{1,2},{3,4},{5,6},{7,8},{9,10},{11,12},{13,14},{2,1},{4,3},{6,5},{... | collective-permute-start | bytes 602120 | tf_op jit(solution)/shard_map/ppermute | solution.py:508
  12.6 5.1 %collective-permute-start.3 = (f32[49,8,128]{2,1,0:T(8,128)S(1)}, f32[49,8,128]{2,1,0:T(8,128)S(1)}, u32[]{:S(2)}, u32[]{:S(2)}) collective-permute-start(f32[49,8,128]{2,1,0:T(8,128)S(1)} %get-tuple-element.25), channel_id=1, source_target_pairs={{0,1},{2,3},{4,5},{6,7},{8,9},{10,11},{12,13},{14,15},{1,0},{3,2},... | collective-permute-start | bytes 602120 | tf_op jit(solution)/shard_map/ppermute | solution.py:508
  40.9 19.5 %all-to-all-start.1 = ((f32[8,64,128]{2,1,0:T(8,128)}), f32[8,64,128]{2,1,0:T(8,128)S(1)}, u32[]{:S(2)}, u32[]{:S(2)}) async-start(f32[8,64,128]{2,1,0:T(8,128)} %broadcast_in_dim.41), calls=%async_computation.1 | async-start | bytes 524288 | tf_op jit(solution)/shard_map/all_to_all | solution.py:513
  50.4 8.8 %collective-permute-start.4 = (f32[20,128]{1,0:T(8,128)S(1)}, f32[20,128]{1,0:T(8,128)S(1)}, u32[]{:S(2)}, u32[]{:S(2)}) collective-permute-start(f32[20,128]{1,0:T(8,128)S(1)} %pad_maximum_fusion.1.vmid), channel_id=1, source_target_pairs={{1,2},{3,4},{5,6},{7,8},{9,10},{11,12},{13,14},{2,1},{4,3},{6,5},{... | collective-permute-start | bytes 30728 | tf_op jit(solution)/shard_map/ppermute | solution.py:508
  57.3 3.1 %collective-permute-start.5 = (f32[20,128]{1,0:T(8,128)S(1)}, f32[20,128]{1,0:T(8,128)S(1)}, u32[]{:S(2)}, u32[]{:S(2)}) collective-permute-start(f32[20,128]{1,0:T(8,128)S(1)} %pad_maximum_fusion.1.vmid), channel_id=1, source_target_pairs={{0,1},{2,3},{4,5},{6,7},{8,9},{10,11},{12,13},{14,15},{1,0},{3,2},... | collective-permute-start | bytes 30728 | tf_op jit(solution)/shard_map/ppermute | solution.py:508
  60.4 6.9 %collective-permute-start.6 = (f32[512,128]{1,0:T(8,128)S(1)}, f32[512,128]{1,0:T(8,128)S(1)}, u32[]{:S(2)}, u32[]{:S(2)}) collective-permute-start(f32[512,128]{1,0:T(8,128)S(1)} %bitcast.13), channel_id=1, source_target_pairs={{0,1},{2,3},{4,5},{6,7},{8,9},{10,11},{12,13},{14,15},{1,0},{3,2},... | collective-permute-start | bytes 786440 | tf_op jit(solution)/shard_map/ppermute | solution.py:508

commit v11 on v10

--- a/solution.py
+++ b/solution.py
@@ -113,7 +113,7 @@
     return planes
 
 
-def pack_kernel(own, near, far, to_near, to_far):
+def pack_kernel(own, far, near, to_near, to_far):
     first = core_mask(8)
     row = iota((8, 128), 0)
     at = 0
@@ -139,7 +139,7 @@
 
 
 def down_kernel(
-    own, xnear, xfar, far, near, lower, higher, v1_out, v0_out, f0_out, f1_out, wx0, wy0, wz0, inv0, wx1, wy1, wz1, inv1
+    own, xfar, xnear, far, near, lower, higher, v1_out, v0_out, f0_out, f1_out, wx0, wy0, wz0, inv0, wx1, wy1, wz1, inv1
 ):
     first = core_mask(8)
 
@@ -253,7 +253,7 @@
     return jnp.concatenate([rows(c[8:], -1), c[:8]], axis=0)
 
 
-UNROLL = 10
+UNROLL = 6
 PAD = 3
 
 
@@ -529,7 +529,7 @@
         out_shape=(f32(count, 8, 128),) * 2,
         compiler_params=params,
         name="pack",
-    )(own, near, far)
+    )(own, far, near)
     from_far = swap(to_far, "gy", 1)
     from_near = swap(to_near, "gy", 0)
 
@@ -539,7 +539,7 @@
         out_shape=(f32(8, 128),) * 3 + tuple(f32(n, ROWS, 128) for n in WINDOW_PLANES),
         compiler_params=params,
         name="down",
-    )(own, near, far, from_far, from_near)
+    )(own, far, near, from_far, from_near)
 
     gx = lax.axis_index("gx")
     before = lax.broadcasted_iota(jnp.int32, (32, 1, 1), 0) < gx

time: 74.7 us -> 73.6 us (0.985)
  blocking collectives: 20.7 us -> 18.1 us
  waiting for transfers between devices: 4.5 us -> 5.57 us
    all_to_all x1, blocking collectives: 20.7 us -> 18.1 us  [shards(): blocks = lax.all_to_all(blocks, 'gx', 0, 0)]
    ppermute x7, waiting for transfers between devices: 4.5 us -> 5.57 us  [swap(): return lax.ppermute(x, axis, pairs + [(b, a) for a, b in pairs])]
where the time goes in v11:
time: 73.6 us; the launch traced here: 73.1 us
  starting transfers between devices  38.8 us (53%)
  blocking collectives  18.1 us (25%)
  Pallas kernels  8.73 us (12%)
  waiting for transfers between devices  5.57 us (8%)
  other arithmetic  0.96 us (1%)
  local copies, waits for them, and re-layouts  0.8 us (1%)
    ppermute x7, starting transfers between devices, swap(): return lax.ppermute(x, axis, pairs + [(b, a) for a, b in pairs])  29.5 us
    all_to_all x1, blocking collectives, shards(): blocks = lax.all_to_all(blocks, 'gx', 0, 0)  18.1 us
    all_to_all x1, starting transfers between devices, to_all(): return lax.all_to_all(copies, axis, 0, 0, axis_index_groups=groups)  9.38 us
    pallas_call x1, Pallas kernels, shards(): pl.pallas_call(up_kernel, in_specs=[array] * (5 + len(WINDOW_PLANES)), ou...  7.12 us
    ppermute x7, waiting for transfers between devices, swap(): return lax.ppermute(x, axis, pairs + [(b, a) for a, b in pairs])  5.57 us
    pallas_call x1, Pallas kernels, shards(): pl.pallas_call(down_kernel, in_specs=[array] * 5, out_shape=(f32(8, 128),...  1.58 us
  transfers between devices with their start and end apart: 8, of which 4 were waited for; matrix products, arithmetic and copies ran while one was open for 0% of the time, Pallas kernels for 0%

profile of v11, /device:TPU:1, one launch (start us, length us, event | category | flops | bytes accessed | tf_op | source)
XLA Modules:
  0.0 73.1 jit_solution(11195628785767526034)
XLA Ops:
  0.0 0.8 %pad_maximum_fusion = f32[24,8,128]{2,1,0:T(8,128)S(1)} fusion(f32[8,8,128]{2,1,0:T(8,128)} %param.5, f32[8,8,128]{2,1,0:T(8,128)} %param.4, f32[8,8,128]{2,1,0:T(8,128)} %param.3), kind=kLoop, calls=%fused_computation.3 | loop fusion | flops 49152 | bytes 196608 | tf_op jit(solution)/shard_map/concatenate | solution.py:518
  0.8 0.7 collective-permute-start
  1.5 6.6 %collective-permute-start.1 = (f32[3,7,8,128]{3,2,1,0:T(8,128)S(1)}, f32[3,7,8,128]{3,2,1,0:T(8,128)S(1)}, u32[]{:S(2)}, u32[]{:S(2)}) collective-permute-start(f32[3,7,8,128]{3,2,1,0:T(8,128)S(1)} %get-tuple-element.45), channel_id=1, source_target_pairs={{0,16},{32,48},{64,80},{96,112},{128,144},{160,176},{192,208},{224... | collective-permute-start | bytes 258056 | tf_op jit(solution)/shard_map/ppermute | solution.py:508
  8.1 0.0 collective-permute-done.far.xfar
  8.1 1.8 %collective-permute-done.1.near.xnear = f32[3,7,8,128]{3,2,1,0:T(8,128)S(1)} collective-permute-done((f32[3,7,8,128]{3,2,1,0:T(8,128)S(1)}, f32[3,7,8,128]{3,2,1,0:T(8,128)S(1)}, u32[]{:S(2)}, u32[]{:S(2)}) %collective-permute-start.1) | collective-permute-done | bytes 86048 | tf_op jit(solution)/shard_map/ppermute | solution.py:508
  10.0 5.7 %collective-permute-start.2 = (f32[49,8,128]{2,1,0:T(8,128)S(1)}, f32[49,8,128]{2,1,0:T(8,128)S(1)}, u32[]{:S(2)}, u32[]{:S(2)}) collective-permute-start(f32[49,8,128]{2,1,0:T(8,128)S(1)} %get-tuple-element.24), channel_id=1, source_target_pairs={{1,2},{3,4},{5,6},{7,8},{9,10},{11,12},{13,14},{2,1},{4,3},{6,5},{... | collective-permute-start | bytes 602120 | tf_op jit(solution)/shard_map/ppermute | solution.py:508
  15.7 1.9 %collective-permute-start.3 = (f32[49,8,128]{2,1,0:T(8,128)S(1)}, f32[49,8,128]{2,1,0:T(8,128)S(1)}, u32[]{:S(2)}, u32[]{:S(2)}) collective-permute-start(f32[49,8,128]{2,1,0:T(8,128)S(1)} %get-tuple-element.25), channel_id=1, source_target_pairs={{0,1},{2,3},{4,5},{6,7},{8,9},{10,11},{12,13},{14,15},{1,0},{3,2},... | collective-permute-start | bytes 602120 | tf_op jit(solution)/shard_map/ppermute | solution.py:508
  17.6 1.4 %collective-permute-done.2.far = f32[49,8,128]{2,1,0:T(8,128)S(1)} collective-permute-done((f32[49,8,128]{2,1,0:T(8,128)S(1)}, f32[49,8,128]{2,1,0:T(8,128)S(1)}, u32[]{:S(2)}, u32[]{:S(2)}) %collective-permute-start.2) | collective-permute-done | bytes 200736 | tf_op jit(solution)/shard_map/ppermute | solution.py:508
  19.1 0.0 collective-permute-done.3.near
  19.1 1.6 %down.1 = (f32[8,128]{1,0:T(8,128)S(1)}, f32[8,128]{1,0:T(8,128)S(1)}, f32[8,128]{1,0:T(8,128)S(1)}, f32[12,24,128]{2,1,0:T(8,128)S(1)}, f32[10,24,128]{2,1,0:T(...) custom-call(f32[3,8,8,128]{3,2,1,0:T(8,128)S(1)} %bitcast.12, ...), custom_call_target="tpu_custom_call" | custom-call | tf_op jit(solution)/shard_map/down/pallas_call | solution.py:536
  20.7 0.1 broadcast_select_fusion
  20.8 18.1 %all_to_all.10 = f32[32,1,1024]{2,1,0:T(1,128)S(1)} all-to-all(f32[32,1,1024]{2,1,0:T(1,128)S(1)} %broadcast_select_fusion), channel_id=1, replica_groups=mesh['gx'=32,'gy'=16] {'gx'}, dimensions={0} | all-to-all | bytes 262144 | tf_op jit(solution)/shard_map/all_to_all | solution.py:547
  38.9 0.7 broadcast_in_dim.41
  39.6 9.4 %all-to-all-start.1 = ((f32[8,64,128]{2,1,0:T(8,128)}), f32[8,64,128]{2,1,0:T(8,128)S(1)}, u32[]{:S(2)}, u32[]{:S(2)}) async-start(f32[8,64,128]{2,1,0:T(8,128)} %broadcast_in_dim.41), calls=%async_computation.1 | async-start | bytes 524288 | tf_op jit(solution)/shard_map/all_to_all | solution.py:513
  49.1 6.9 %collective-permute-start.4 = (f32[20,128]{1,0:T(8,128)S(1)}, f32[20,128]{1,0:T(8,128)S(1)}, u32[]{:S(2)}, u32[]{:S(2)}) collective-permute-start(f32[20,128]{1,0:T(8,128)S(1)} %pad_maximum_fusion.1.vmid), channel_id=1, source_target_pairs={{1,2},{3,4},{5,6},{7,8},{9,10},{11,12},{13,14},{2,1},{4,3},{6,5},{... | collective-permute-start | bytes 30728 | tf_op jit(solution)/shard_map/ppermute | solution.py:508
  56.0 1.9 %collective-permute-start.5 = (f32[20,128]{1,0:T(8,128)S(1)}, f32[20,128]{1,0:T(8,128)S(1)}, u32[]{:S(2)}, u32[]{:S(2)}) collective-permute-start(f32[20,128]{1,0:T(8,128)S(1)} %pad_maximum_fusion.1.vmid), channel_id=1, source_target_pairs={{0,1},{2,3},{4,5},{6,7},{8,9},{10,11},{12,13},{14,15},{1,0},{3,2},... | collective-permute-start | bytes 30728 | tf_op jit(solution)/shard_map/ppermute | solution.py:508
  57.9 0.0 collective-permute-done.4.vfar
  57.9 1.1 %collective-permute-done.5.vnear = f32[20,128]{1,0:T(8,128)S(1)} collective-permute-done((f32[20,128]{1,0:T(8,128)S(1)}, f32[20,128]{1,0:T(8,128)S(1)}, u32[]{:S(2)}, u32[]{:S(2)}) %collective-permute-start.5) | collective-permute-done | bytes 10272 | tf_op jit(solution)/shard_map/ppermute | solution.py:508
  59.1 0.0 all-to-all-done.1
  59.1 5.8 %collective-permute-start.6 = (f32[512,128]{1,0:T(8,128)S(1)}, f32[512,128]{1,0:T(8,128)S(1)}, u32[]{:S(2)}, u32[]{:S(2)}) collective-permute-start(f32[512,128]{1,0:T(8,128)S(1)} %bitcast.13), channel_id=1, source_target_pairs={{0,1},{2,3},{4,5},{6,7},{8,9},{10,11},{12,13},{14,15},{1,0},{3,2},... | collective-permute-start | bytes 786440 | tf_op jit(solution)/shard_map/ppermute | solution.py:508
  64.9 1.1 %collective-permute-done.6.other = f32[512,128]{1,0:T(8,128)S(1)} collective-permute-done((f32[512,128]{1,0:T(8,128)S(1)}, f32[512,128]{1,0:T(8,128)S(1)}, u32[]{:S(2)}, u32[]{:S(2)}) %collective-permute-start.6) | collective-permute-done | bytes 262176 | tf_op jit(solution)/shard_map/ppermute | solution.py:508
  66.0 7.1 %up.1 = f32[8,8,128]{2,1,0:T(8,128)} custom-call(f32[512,128]{1,0:T(8,128)S(1)} %bitcast.14, f32[512,128]{1,0:T(8,128)S(1)} %collective-permute-done.6.other, f32[12,24,128]{2,1,0:T(8,128)S(1)} %get-tuple-element.30.v0, f32[10,24,128]{2,1,0:T(8,128)S(1)} %get-tuple-element.31.f0, f32[8,24,128]{2,1,0:T(8,128)S(1)} %get-tuple-element.32.f1, ...), custom_call_target="tpu_custom_call" | custom-call | tf_op jit(solution)/shard_map/up/pallas_call | solution.py:559
  (8 shorter events, 0.2 us)
Async XLA Ops:
  0.8 7.3 %collective-permute-start = (f32[3,7,8,128]{3,2,1,0:T(8,128)S(1)}, f32[3,7,8,128]{3,2,1,0:T(8,128)S(1)}, u32[]{:S(2)}, u32[]{:S(2)}) collective-permute-start(f32[3,7,8,128]{3,2,1,0:T(8,128)S(1)} %get-tuple-element.46), channel_id=1, source_target_pairs={{16,32},{48,64},{80,96},{112,128},{144,160},{176,192},{208,224},{2... | collective-permute-start | bytes 258056 | tf_op jit(solution)/shard_map/ppermute | solution.py:508
  1.5 8.4 %collective-permute-start.1 = (f32[3,7,8,128]{3,2,1,0:T(8,128)S(1)}, f32[3,7,8,128]{3,2,1,0:T(8,128)S(1)}, u32[]{:S(2)}, u32[]{:S(2)}) collective-permute-start(f32[3,7,8,128]{3,2,1,0:T(8,128)S(1)} %get-tuple-element.45), channel_id=1, source_target_pairs={{0,16},{32,48},{64,80},{96,112},{128,144},{160,176},{192,208},{224... | collective-permute-start | bytes 258056 | tf_op jit(solution)/shard_map/ppermute | solution.py:508
  10.0 9.1 %collective-permute-start.2 = (f32[49,8,128]{2,1,0:T(8,128)S(1)}, f32[49,8,128]{2,1,0:T(8,128)S(1)}, u32[]{:S(2)}, u32[]{:S(2)}) collective-permute-start(f32[49,8,128]{2,1,0:T(8,128)S(1)} %get-tuple-element.24), channel_id=1, source_target_pairs={{1,2},{3,4},{5,6},{7,8},{9,10},{11,12},{13,14},{2,1},{4,3},{6,5},{... | collective-permute-start | bytes 602120 | tf_op jit(solution)/shard_map/ppermute | solution.py:508
  15.7 3.4 %collective-permute-start.3 = (f32[49,8,128]{2,1,0:T(8,128)S(1)}, f32[49,8,128]{2,1,0:T(8,128)S(1)}, u32[]{:S(2)}, u32[]{:S(2)}) collective-permute-start(f32[49,8,128]{2,1,0:T(8,128)S(1)} %get-tuple-element.25), channel_id=1, source_target_pairs={{0,1},{2,3},{4,5},{6,7},{8,9},{10,11},{12,13},{14,15},{1,0},{3,2},... | collective-permute-start | bytes 602120 | tf_op jit(solution)/shard_map/ppermute | solution.py:508
  39.6 19.5 %all-to-all-start.1 = ((f32[8,64,128]{2,1,0:T(8,128)}), f32[8,64,128]{2,1,0:T(8,128)S(1)}, u32[]{:S(2)}, u32[]{:S(2)}) async-start(f32[8,64,128]{2,1,0:T(8,128)} %broadcast_in_dim.41), calls=%async_computation.1 | async-start | bytes 524288 | tf_op jit(solution)/shard_map/all_to_all | solution.py:513
  49.1 8.8 %collective-permute-start.4 = (f32[20,128]{1,0:T(8,128)S(1)}, f32[20,128]{1,0:T(8,128)S(1)}, u32[]{:S(2)}, u32[]{:S(2)}) collective-permute-start(f32[20,128]{1,0:T(8,128)S(1)} %pad_maximum_fusion.1.vmid), channel_id=1, source_target_pairs={{1,2},{3,4},{5,6},{7,8},{9,10},{11,12},{13,14},{2,1},{4,3},{6,5},{... | collective-permute-start | bytes 30728 | tf_op jit(solution)/shard_map/ppermute | solution.py:508
  56.0 3.1 %collective-permute-start.5 = (f32[20,128]{1,0:T(8,128)S(1)}, f32[20,128]{1,0:T(8,128)S(1)}, u32[]{:S(2)}, u32[]{:S(2)}) collective-permute-start(f32[20,128]{1,0:T(8,128)S(1)} %pad_maximum_fusion.1.vmid), channel_id=1, source_target_pairs={{0,1},{2,3},{4,5},{6,7},{8,9},{10,11},{12,13},{14,15},{1,0},{3,2},... | collective-permute-start | bytes 30728 | tf_op jit(solution)/shard_map/ppermute | solution.py:508
  59.1 6.9 %collective-permute-start.6 = (f32[512,128]{1,0:T(8,128)S(1)}, f32[512,128]{1,0:T(8,128)S(1)}, u32[]{:S(2)}, u32[]{:S(2)}) collective-permute-start(f32[512,128]{1,0:T(8,128)S(1)} %bitcast.13), channel_id=1, source_target_pairs={{0,1},{2,3},{4,5},{6,7},{8,9},{10,11},{12,13},{14,15},{1,0},{3,2},... | collective-permute-start | bytes 786440 | tf_op jit(solution)/shard_map/ppermute | solution.py:508

commit v12 on v11

--- a/solution.py
+++ b/solution.py
@@ -253,7 +253,7 @@
     return jnp.concatenate([rows(c[8:], -1), c[:8]], axis=0)
 
 
-UNROLL = 6
+UNROLL = 10
 PAD = 3
 
 

time: 73.6 us -> 73.4 us (level)
  no operation moved by 1% of the time
where the time goes in v12:
time: 73.4 us; the launch traced here: 72.9 us
  starting transfers between devices  38.8 us (53%)
  blocking collectives  18.1 us (25%)
  Pallas kernels  8.57 us (12%)
  waiting for transfers between devices  5.57 us (8%)
  other arithmetic  0.96 us (1%)
  local copies, waits for them, and re-layouts  0.8 us (1%)
    ppermute x7, starting transfers between devices, swap(): return lax.ppermute(x, axis, pairs + [(b, a) for a, b in pairs])  29.5 us
    all_to_all x1, blocking collectives, shards(): blocks = lax.all_to_all(blocks, 'gx', 0, 0)  18.1 us
    all_to_all x1, starting transfers between devices, to_all(): return lax.all_to_all(copies, axis, 0, 0, axis_index_groups=groups)  9.38 us
    pallas_call x1, Pallas kernels, shards(): pl.pallas_call(up_kernel, in_specs=[array] * (5 + len(WINDOW_PLANES)), ou...  6.96 us
    ppermute x7, waiting for transfers between devices, swap(): return lax.ppermute(x, axis, pairs + [(b, a) for a, b in pairs])  5.57 us
    pallas_call x1, Pallas kernels, shards(): pl.pallas_call(down_kernel, in_specs=[array] * 5, out_shape=(f32(8, 128),...  1.58 us
  transfers between devices with their start and end apart: 8, of which 4 were waited for; matrix products, arithmetic and copies ran while one was open for 0% of the time, Pallas kernels for 0%

profile of v12, /device:TPU:1, one launch (start us, length us, event | category | flops | bytes accessed | tf_op | source)
XLA Modules:
  0.0 72.9 jit_solution(663136504581545970)
XLA Ops:
  0.0 0.8 %pad_maximum_fusion = f32[24,8,128]{2,1,0:T(8,128)S(1)} fusion(f32[8,8,128]{2,1,0:T(8,128)} %param.5, f32[8,8,128]{2,1,0:T(8,128)} %param.4, f32[8,8,128]{2,1,0:T(8,128)} %param.3), kind=kLoop, calls=%fused_computation.3 | loop fusion | flops 49152 | bytes 196608 | tf_op jit(solution)/shard_map/concatenate | solution.py:518
  0.8 0.7 collective-permute-start
  1.5 6.6 %collective-permute-start.1 = (f32[3,7,8,128]{3,2,1,0:T(8,128)S(1)}, f32[3,7,8,128]{3,2,1,0:T(8,128)S(1)}, u32[]{:S(2)}, u32[]{:S(2)}) collective-permute-start(f32[3,7,8,128]{3,2,1,0:T(8,128)S(1)} %get-tuple-element.45), channel_id=1, source_target_pairs={{0,16},{32,48},{64,80},{96,112},{128,144},{160,176},{192,208},{224... | collective-permute-start | bytes 258056 | tf_op jit(solution)/shard_map/ppermute | solution.py:508
  8.1 0.0 collective-permute-done.far.xfar
  8.1 1.8 %collective-permute-done.1.near.xnear = f32[3,7,8,128]{3,2,1,0:T(8,128)S(1)} collective-permute-done((f32[3,7,8,128]{3,2,1,0:T(8,128)S(1)}, f32[3,7,8,128]{3,2,1,0:T(8,128)S(1)}, u32[]{:S(2)}, u32[]{:S(2)}) %collective-permute-start.1) | collective-permute-done | bytes 86048 | tf_op jit(solution)/shard_map/ppermute | solution.py:508
  10.0 5.7 %collective-permute-start.2 = (f32[49,8,128]{2,1,0:T(8,128)S(1)}, f32[49,8,128]{2,1,0:T(8,128)S(1)}, u32[]{:S(2)}, u32[]{:S(2)}) collective-permute-start(f32[49,8,128]{2,1,0:T(8,128)S(1)} %get-tuple-element.24), channel_id=1, source_target_pairs={{1,2},{3,4},{5,6},{7,8},{9,10},{11,12},{13,14},{2,1},{4,3},{6,5},{... | collective-permute-start | bytes 602120 | tf_op jit(solution)/shard_map/ppermute | solution.py:508
  15.7 1.9 %collective-permute-start.3 = (f32[49,8,128]{2,1,0:T(8,128)S(1)}, f32[49,8,128]{2,1,0:T(8,128)S(1)}, u32[]{:S(2)}, u32[]{:S(2)}) collective-permute-start(f32[49,8,128]{2,1,0:T(8,128)S(1)} %get-tuple-element.25), channel_id=1, source_target_pairs={{0,1},{2,3},{4,5},{6,7},{8,9},{10,11},{12,13},{14,15},{1,0},{3,2},... | collective-permute-start | bytes 602120 | tf_op jit(solution)/shard_map/ppermute | solution.py:508
  17.6 1.4 %collective-permute-done.2.far = f32[49,8,128]{2,1,0:T(8,128)S(1)} collective-permute-done((f32[49,8,128]{2,1,0:T(8,128)S(1)}, f32[49,8,128]{2,1,0:T(8,128)S(1)}, u32[]{:S(2)}, u32[]{:S(2)}) %collective-permute-start.2) | collective-permute-done | bytes 200736 | tf_op jit(solution)/shard_map/ppermute | solution.py:508
  19.1 0.0 collective-permute-done.3.near
  19.1 1.6 %down.1 = (f32[8,128]{1,0:T(8,128)S(1)}, f32[8,128]{1,0:T(8,128)S(1)}, f32[8,128]{1,0:T(8,128)S(1)}, f32[12,24,128]{2,1,0:T(8,128)S(1)}, f32[10,24,128]{2,1,0:T(...) custom-call(f32[3,8,8,128]{3,2,1,0:T(8,128)S(1)} %bitcast.12, ...), custom_call_target="tpu_custom_call" | custom-call | tf_op jit(solution)/shard_map/down/pallas_call | solution.py:536
  20.7 0.1 broadcast_select_fusion
  20.8 18.1 %all_to_all.10 = f32[32,1,1024]{2,1,0:T(1,128)S(1)} all-to-all(f32[32,1,1024]{2,1,0:T(1,128)S(1)} %broadcast_select_fusion), channel_id=1, replica_groups=mesh['gx'=32,'gy'=16] {'gx'}, dimensions={0} | all-to-all | bytes 262144 | tf_op jit(solution)/shard_map/all_to_all | solution.py:547
  38.9 0.7 broadcast_in_dim.41
  39.6 9.4 %all-to-all-start.1 = ((f32[8,64,128]{2,1,0:T(8,128)}), f32[8,64,128]{2,1,0:T(8,128)S(1)}, u32[]{:S(2)}, u32[]{:S(2)}) async-start(f32[8,64,128]{2,1,0:T(8,128)} %broadcast_in_dim.41), calls=%async_computation.1 | async-start | bytes 524288 | tf_op jit(solution)/shard_map/all_to_all | solution.py:513
  49.1 6.9 %collective-permute-start.4 = (f32[20,128]{1,0:T(8,128)S(1)}, f32[20,128]{1,0:T(8,128)S(1)}, u32[]{:S(2)}, u32[]{:S(2)}) collective-permute-start(f32[20,128]{1,0:T(8,128)S(1)} %pad_maximum_fusion.1.vmid), channel_id=1, source_target_pairs={{1,2},{3,4},{5,6},{7,8},{9,10},{11,12},{13,14},{2,1},{4,3},{6,5},{... | collective-permute-start | bytes 30728 | tf_op jit(solution)/shard_map/ppermute | solution.py:508
  56.0 1.9 %collective-permute-start.5 = (f32[20,128]{1,0:T(8,128)S(1)}, f32[20,128]{1,0:T(8,128)S(1)}, u32[]{:S(2)}, u32[]{:S(2)}) collective-permute-start(f32[20,128]{1,0:T(8,128)S(1)} %pad_maximum_fusion.1.vmid), channel_id=1, source_target_pairs={{0,1},{2,3},{4,5},{6,7},{8,9},{10,11},{12,13},{14,15},{1,0},{3,2},... | collective-permute-start | bytes 30728 | tf_op jit(solution)/shard_map/ppermute | solution.py:508
  57.9 0.0 collective-permute-done.4.vfar
  57.9 1.1 %collective-permute-done.5.vnear = f32[20,128]{1,0:T(8,128)S(1)} collective-permute-done((f32[20,128]{1,0:T(8,128)S(1)}, f32[20,128]{1,0:T(8,128)S(1)}, u32[]{:S(2)}, u32[]{:S(2)}) %collective-permute-start.5) | collective-permute-done | bytes 10272 | tf_op jit(solution)/shard_map/ppermute | solution.py:508
  59.1 0.0 all-to-all-done.1
  59.1 5.8 %collective-permute-start.6 = (f32[512,128]{1,0:T(8,128)S(1)}, f32[512,128]{1,0:T(8,128)S(1)}, u32[]{:S(2)}, u32[]{:S(2)}) collective-permute-start(f32[512,128]{1,0:T(8,128)S(1)} %bitcast.13), channel_id=1, source_target_pairs={{0,1},{2,3},{4,5},{6,7},{8,9},{10,11},{12,13},{14,15},{1,0},{3,2},... | collective-permute-start | bytes 786440 | tf_op jit(solution)/shard_map/ppermute | solution.py:508
  64.9 1.1 %collective-permute-done.6.other = f32[512,128]{1,0:T(8,128)S(1)} collective-permute-done((f32[512,128]{1,0:T(8,128)S(1)}, f32[512,128]{1,0:T(8,128)S(1)}, u32[]{:S(2)}, u32[]{:S(2)}) %collective-permute-start.6) | collective-permute-done | bytes 262176 | tf_op jit(solution)/shard_map/ppermute | solution.py:508
  66.0 7.0 %up.1 = f32[8,8,128]{2,1,0:T(8,128)} custom-call(f32[512,128]{1,0:T(8,128)S(1)} %bitcast.14, f32[512,128]{1,0:T(8,128)S(1)} %collective-permute-done.6.other, f32[12,24,128]{2,1,0:T(8,128)S(1)} %get-tuple-element.30.v0, f32[10,24,128]{2,1,0:T(8,128)S(1)} %get-tuple-element.31.f0, f32[8,24,128]{2,1,0:T(8,128)S(1)} %get-tuple-element.32.f1, ...), custom_call_target="tpu_custom_call" | custom-call | tf_op jit(solution)/shard_map/up/pallas_call | solution.py:559
  (8 shorter events, 0.2 us)
Async XLA Ops:
  0.8 7.3 %collective-permute-start = (f32[3,7,8,128]{3,2,1,0:T(8,128)S(1)}, f32[3,7,8,128]{3,2,1,0:T(8,128)S(1)}, u32[]{:S(2)}, u32[]{:S(2)}) collective-permute-start(f32[3,7,8,128]{3,2,1,0:T(8,128)S(1)} %get-tuple-element.46), channel_id=1, source_target_pairs={{16,32},{48,64},{80,96},{112,128},{144,160},{176,192},{208,224},{2... | collective-permute-start | bytes 258056 | tf_op jit(solution)/shard_map/ppermute | solution.py:508
  1.5 8.4 %collective-permute-start.1 = (f32[3,7,8,128]{3,2,1,0:T(8,128)S(1)}, f32[3,7,8,128]{3,2,1,0:T(8,128)S(1)}, u32[]{:S(2)}, u32[]{:S(2)}) collective-permute-start(f32[3,7,8,128]{3,2,1,0:T(8,128)S(1)} %get-tuple-element.45), channel_id=1, source_target_pairs={{0,16},{32,48},{64,80},{96,112},{128,144},{160,176},{192,208},{224... | collective-permute-start | bytes 258056 | tf_op jit(solution)/shard_map/ppermute | solution.py:508
  10.0 9.1 %collective-permute-start.2 = (f32[49,8,128]{2,1,0:T(8,128)S(1)}, f32[49,8,128]{2,1,0:T(8,128)S(1)}, u32[]{:S(2)}, u32[]{:S(2)}) collective-permute-start(f32[49,8,128]{2,1,0:T(8,128)S(1)} %get-tuple-element.24), channel_id=1, source_target_pairs={{1,2},{3,4},{5,6},{7,8},{9,10},{11,12},{13,14},{2,1},{4,3},{6,5},{... | collective-permute-start | bytes 602120 | tf_op jit(solution)/shard_map/ppermute | solution.py:508
  15.7 3.4 %collective-permute-start.3 = (f32[49,8,128]{2,1,0:T(8,128)S(1)}, f32[49,8,128]{2,1,0:T(8,128)S(1)}, u32[]{:S(2)}, u32[]{:S(2)}) collective-permute-start(f32[49,8,128]{2,1,0:T(8,128)S(1)} %get-tuple-element.25), channel_id=1, source_target_pairs={{0,1},{2,3},{4,5},{6,7},{8,9},{10,11},{12,13},{14,15},{1,0},{3,2},... | collective-permute-start | bytes 602120 | tf_op jit(solution)/shard_map/ppermute | solution.py:508
  39.6 19.5 %all-to-all-start.1 = ((f32[8,64,128]{2,1,0:T(8,128)}), f32[8,64,128]{2,1,0:T(8,128)S(1)}, u32[]{:S(2)}, u32[]{:S(2)}) async-start(f32[8,64,128]{2,1,0:T(8,128)} %broadcast_in_dim.41), calls=%async_computation.1 | async-start | bytes 524288 | tf_op jit(solution)/shard_map/all_to_all | solution.py:513
  49.1 8.8 %collective-permute-start.4 = (f32[20,128]{1,0:T(8,128)S(1)}, f32[20,128]{1,0:T(8,128)S(1)}, u32[]{:S(2)}, u32[]{:S(2)}) collective-permute-start(f32[20,128]{1,0:T(8,128)S(1)} %pad_maximum_fusion.1.vmid), channel_id=1, source_target_pairs={{1,2},{3,4},{5,6},{7,8},{9,10},{11,12},{13,14},{2,1},{4,3},{6,5},{... | collective-permute-start | bytes 30728 | tf_op jit(solution)/shard_map/ppermute | solution.py:508
  56.0 3.1 %collective-permute-start.5 = (f32[20,128]{1,0:T(8,128)S(1)}, f32[20,128]{1,0:T(8,128)S(1)}, u32[]{:S(2)}, u32[]{:S(2)}) collective-permute-start(f32[20,128]{1,0:T(8,128)S(1)} %pad_maximum_fusion.1.vmid), channel_id=1, source_target_pairs={{0,1},{2,3},{4,5},{6,7},{8,9},{10,11},{12,13},{14,15},{1,0},{3,2},... | collective-permute-start | bytes 30728 | tf_op jit(solution)/shard_map/ppermute | solution.py:508
  59.1 6.9 %collective-permute-start.6 = (f32[512,128]{1,0:T(8,128)S(1)}, f32[512,128]{1,0:T(8,128)S(1)}, u32[]{:S(2)}, u32[]{:S(2)}) collective-permute-start(f32[512,128]{1,0:T(8,128)S(1)} %bitcast.13), channel_id=1, source_target_pairs={{0,1},{2,3},{4,5},{6,7},{8,9},{10,11},{12,13},{14,15},{1,0},{3,2},... | collective-permute-start | bytes 786440 | tf_op jit(solution)/shard_map/ppermute | solution.py:508

commit v13 on v12

--- a/solution.py
+++ b/solution.py
@@ -257,6 +257,12 @@
 PAD = 3
 
 
+def order_kernel(blocks, planes):
+    for c in range(2):
+        for i in range(32):
+            planes[c, i] = blocks[pl.ds(2 * i + c, 8, stride=64), :]
+
+
 def up_kernel(
     mine, other, v0, f0, f1, wx0, wy0, wz0, inv0, wx1, wy1, wz1, inv1, vmid, vfar, vnear, out,
     k2, f2, va, vb, wxi, wxe, wyi, wye, wz2, diag2, inv2, sumk, sumr, e3,
@@ -275,8 +281,7 @@
             ref[32 + PAD + i] = zero
     for i in range(32):
         for c, ref in ((0, f2), (1, k2)):
-            here = pl.ds(2 * i + c, 8, stride=64)
-            a, b = mine[here, :], other[here, :]
+            a, b = mine[c, i], other[c, i]
             ref[i + PAD, :8] = jnp.where(first, a, b)
             ref[i + PAD, 8:] = jnp.where(first, b, a)
 
@@ -547,6 +552,13 @@
     blocks = lax.all_to_all(blocks, "gx", 0, 0)
     same_core = [[2 * z + c for z in range(8)] for c in range(2)]
     mine = to_all(blocks[:, :, :256].reshape(64, 128), "gy", 8, same_core).reshape(512, 128)
+    mine = pl.pallas_call(
+        order_kernel,
+        in_specs=[array],
+        out_shape=f32(2, 32, 8, 128),
+        compiler_params=params,
+        name="order",
+    )(mine)
     beside = jnp.pad(blocks[:, 0, 256:], ((1, 1), (0, 0)))
     low = lax.dynamic_slice(beside, (gx, jnp.int32(0)), (1, 768))
     high = lax.dynamic_slice(beside, (gx + 2, jnp.int32(0)), (1, 768))

time: 73.4 us -> 73.4 us (level)
  transfers between devices with their start and end apart: 8 -> 8, of which waited for: 4 -> 5; matrix products, arithmetic and copies ran while one was open for 0% -> 0% of each run, Pallas kernels for 0% -> 0%
where the time goes in v13:
time: 73.4 us; the launch traced here: 72.9 us
  starting transfers between devices  39 us (53%)
  blocking collectives  18.1 us (25%)
  Pallas kernels  8.49 us (12%)
  waiting for transfers between devices  5.41 us (7%)
  other arithmetic  0.96 us (1%)
  local copies, waits for them, and re-layouts  0.8 us (1%)
    ppermute x7, starting transfers between devices, swap(): return lax.ppermute(x, axis, pairs + [(b, a) for a, b in pairs])  29.6 us
    all_to_all x1, blocking collectives, shards(): blocks = lax.all_to_all(blocks, 'gx', 0, 0)  18.1 us
    all_to_all x1, starting transfers between devices, to_all(): return lax.all_to_all(copies, axis, 0, 0, axis_index_groups=groups)  9.38 us
    pallas_call x1, Pallas kernels, shards(): pl.pallas_call(up_kernel, in_specs=[array] * (5 + len(WINDOW_PLANES)), ou...  6.72 us
    ppermute x7, waiting for transfers between devices, swap(): return lax.ppermute(x, axis, pairs + [(b, a) for a, b in pairs])  4.9 us
    pallas_call x1, Pallas kernels, shards(): pl.pallas_call(down_kernel, in_specs=[array] * 5, out_shape=(f32(8, 128),...  1.58 us
  transfers between devices with their start and end apart: 8, of which 5 were waited for; matrix products, arithmetic and copies ran while one was open for 0% of the time, Pallas kernels for 0%

profile of v13, /device:TPU:1, one launch (start us, length us, event | category | flops | bytes accessed | tf_op | source)
XLA Modules:
  0.0 72.9 jit_solution(7840160263451352551)
XLA Ops:
  0.0 0.8 %pad_maximum_fusion = f32[24,8,128]{2,1,0:T(8,128)S(1)} fusion(f32[8,8,128]{2,1,0:T(8,128)} %param.5, f32[8,8,128]{2,1,0:T(8,128)} %param.4, f32[8,8,128]{2,1,0:T(8,128)} %param.3), kind=kLoop, calls=%fused_computation.3 | loop fusion | flops 49152 | bytes 196608 | tf_op jit(solution)/shard_map/concatenate | solution.py:523
  0.8 0.7 collective-permute-start
  1.5 6.6 %collective-permute-start.1 = (f32[3,7,8,128]{3,2,1,0:T(8,128)S(1)}, f32[3,7,8,128]{3,2,1,0:T(8,128)S(1)}, u32[]{:S(2)}, u32[]{:S(2)}) collective-permute-start(f32[3,7,8,128]{3,2,1,0:T(8,128)S(1)} %get-tuple-element.45), channel_id=1, source_target_pairs={{0,16},{32,48},{64,80},{96,112},{128,144},{160,176},{192,208},{224... | collective-permute-start | bytes 258056 | tf_op jit(solution)/shard_map/ppermute | solution.py:513
  8.1 0.0 collective-permute-done.far.xfar
  8.1 1.8 %collective-permute-done.1.near.xnear = f32[3,7,8,128]{3,2,1,0:T(8,128)S(1)} collective-permute-done((f32[3,7,8,128]{3,2,1,0:T(8,128)S(1)}, f32[3,7,8,128]{3,2,1,0:T(8,128)S(1)}, u32[]{:S(2)}, u32[]{:S(2)}) %collective-permute-start.1) | collective-permute-done | bytes 86048 | tf_op jit(solution)/shard_map/ppermute | solution.py:513
  10.0 5.7 %collective-permute-start.2 = (f32[49,8,128]{2,1,0:T(8,128)S(1)}, f32[49,8,128]{2,1,0:T(8,128)S(1)}, u32[]{:S(2)}, u32[]{:S(2)}) collective-permute-start(f32[49,8,128]{2,1,0:T(8,128)S(1)} %get-tuple-element.24), channel_id=1, source_target_pairs={{1,2},{3,4},{5,6},{7,8},{9,10},{11,12},{13,14},{2,1},{4,3},{6,5},{... | collective-permute-start | bytes 602120 | tf_op jit(solution)/shard_map/ppermute | solution.py:513
  15.7 1.9 %collective-permute-start.3 = (f32[49,8,128]{2,1,0:T(8,128)S(1)}, f32[49,8,128]{2,1,0:T(8,128)S(1)}, u32[]{:S(2)}, u32[]{:S(2)}) collective-permute-start(f32[49,8,128]{2,1,0:T(8,128)S(1)} %get-tuple-element.25), channel_id=1, source_target_pairs={{0,1},{2,3},{4,5},{6,7},{8,9},{10,11},{12,13},{14,15},{1,0},{3,2},... | collective-permute-start | bytes 602120 | tf_op jit(solution)/shard_map/ppermute | solution.py:513
  17.6 1.4 %collective-permute-done.2.far = f32[49,8,128]{2,1,0:T(8,128)S(1)} collective-permute-done((f32[49,8,128]{2,1,0:T(8,128)S(1)}, f32[49,8,128]{2,1,0:T(8,128)S(1)}, u32[]{:S(2)}, u32[]{:S(2)}) %collective-permute-start.2) | collective-permute-done | bytes 200736 | tf_op jit(solution)/shard_map/ppermute | solution.py:513
  19.1 0.0 collective-permute-done.3.near
  19.1 1.6 %down.1 = (f32[8,128]{1,0:T(8,128)S(1)}, f32[8,128]{1,0:T(8,128)S(1)}, f32[8,128]{1,0:T(8,128)S(1)}, f32[12,24,128]{2,1,0:T(8,128)S(1)}, f32[10,24,128]{2,1,0:T(...) custom-call(f32[3,8,8,128]{3,2,1,0:T(8,128)S(1)} %bitcast.12, ...), custom_call_target="tpu_custom_call" | custom-call | tf_op jit(solution)/shard_map/down/pallas_call | solution.py:541
  20.7 0.1 broadcast_select_fusion
  20.8 18.1 %all_to_all.10 = f32[32,1,1024]{2,1,0:T(1,128)S(1)} all-to-all(f32[32,1,1024]{2,1,0:T(1,128)S(1)} %broadcast_select_fusion), channel_id=1, replica_groups=mesh['gx'=32,'gy'=16] {'gx'}, dimensions={0} | all-to-all | bytes 262144 | tf_op jit(solution)/shard_map/all_to_all | solution.py:552
  38.9 0.7 broadcast_in_dim.41
  39.6 9.4 %all-to-all-start.1 = ((f32[8,64,128]{2,1,0:T(8,128)}), f32[8,64,128]{2,1,0:T(8,128)S(1)}, u32[]{:S(2)}, u32[]{:S(2)}) async-start(f32[8,64,128]{2,1,0:T(8,128)} %broadcast_in_dim.41), calls=%async_computation.1 | async-start | bytes 524288 | tf_op jit(solution)/shard_map/all_to_all | solution.py:518
  49.1 6.9 %collective-permute-start.4 = (f32[20,128]{1,0:T(8,128)S(1)}, f32[20,128]{1,0:T(8,128)S(1)}, u32[]{:S(2)}, u32[]{:S(2)}) collective-permute-start(f32[20,128]{1,0:T(8,128)S(1)} %pad_maximum_fusion.1.vmid), channel_id=1, source_target_pairs={{1,2},{3,4},{5,6},{7,8},{9,10},{11,12},{13,14},{2,1},{4,3},{6,5},{... | collective-permute-start | bytes 30728 | tf_op jit(solution)/shard_map/ppermute | solution.py:513
  56.0 1.9 %collective-permute-start.5 = (f32[20,128]{1,0:T(8,128)S(1)}, f32[20,128]{1,0:T(8,128)S(1)}, u32[]{:S(2)}, u32[]{:S(2)}) collective-permute-start(f32[20,128]{1,0:T(8,128)S(1)} %pad_maximum_fusion.1.vmid), channel_id=1, source_target_pairs={{0,1},{2,3},{4,5},{6,7},{8,9},{10,11},{12,13},{14,15},{1,0},{3,2},... | collective-permute-start | bytes 30728 | tf_op jit(solution)/shard_map/ppermute | solution.py:513
  57.9 0.5 all-to-all-done.1
  58.4 0.2 order.1.mine
  58.6 0.0 collective-permute-done.4.vfar
  58.6 0.5 collective-permute-done.5.vnear
  59.1 6.0 %collective-permute-start.6 = (f32[2,32,8,128]{3,2,1,0:T(8,128)S(1)}, f32[2,32,8,128]{3,2,1,0:T(8,128)S(1)}, u32[]{:S(2)}, u32[]{:S(2)}) collective-permute-start(f32[2,32,8,128]{3,2,1,0:T(8,128)S(1)} %order.1.mine), channel_id=1, source_target_pairs={{0,1},{2,3},{4,5},{6,7},{8,9},{10,11},{12,13},{14,15},{1,0},{3,2},... | collective-permute-start | bytes 786440 | tf_op jit(solution)/shard_map/ppermute | solution.py:513
  65.0 1.1 %collective-permute-done.6.other = f32[2,32,8,128]{3,2,1,0:T(8,128)S(1)} collective-permute-done((f32[2,32,8,128]{3,2,1,0:T(8,128)S(1)}, f32[2,32,8,128]{3,2,1,0:T(8,128)S(1)}, u32[]{:S(2)}, u32[]{:S(2)}) %collective-permute-start.6) | collective-permute-done | bytes 262176 | tf_op jit(solution)/shard_map/ppermute | solution.py:513
  66.2 6.7 %up.1 = f32[8,8,128]{2,1,0:T(8,128)} custom-call(f32[2,32,8,128]{3,2,1,0:T(8,128)S(1)} %order.1.mine, f32[2,32,8,128]{3,2,1,0:T(8,128)S(1)} %collective-permute-done.6.other, f32[12,24,128]{2,1,0:T(8,128)S(1)} %get-tuple-element.30.v0, f32[10,24,128]{2,1,0:T(8,128)S(1)} %get-tuple-element.31.f0, f32[8,24,128]{2,1,0:T(8,128)S(1)} %get-tuple-element.32.f1, ...), custom_call_target="tpu_custom_call" | custom-call | tf_op jit(solution)/shard_map/up/pallas_call | solution.py:571
  (8 shorter events, 0.2 us)
Async XLA Ops:
  0.8 7.3 %collective-permute-start = (f32[3,7,8,128]{3,2,1,0:T(8,128)S(1)}, f32[3,7,8,128]{3,2,1,0:T(8,128)S(1)}, u32[]{:S(2)}, u32[]{:S(2)}) collective-permute-start(f32[3,7,8,128]{3,2,1,0:T(8,128)S(1)} %get-tuple-element.46), channel_id=1, source_target_pairs={{16,32},{48,64},{80,96},{112,128},{144,160},{176,192},{208,224},{2... | collective-permute-start | bytes 258056 | tf_op jit(solution)/shard_map/ppermute | solution.py:513
  1.5 8.4 %collective-permute-start.1 = (f32[3,7,8,128]{3,2,1,0:T(8,128)S(1)}, f32[3,7,8,128]{3,2,1,0:T(8,128)S(1)}, u32[]{:S(2)}, u32[]{:S(2)}) collective-permute-start(f32[3,7,8,128]{3,2,1,0:T(8,128)S(1)} %get-tuple-element.45), channel_id=1, source_target_pairs={{0,16},{32,48},{64,80},{96,112},{128,144},{160,176},{192,208},{224... | collective-permute-start | bytes 258056 | tf_op jit(solution)/shard_map/ppermute | solution.py:513
  10.0 9.1 %collective-permute-start.2 = (f32[49,8,128]{2,1,0:T(8,128)S(1)}, f32[49,8,128]{2,1,0:T(8,128)S(1)}, u32[]{:S(2)}, u32[]{:S(2)}) collective-permute-start(f32[49,8,128]{2,1,0:T(8,128)S(1)} %get-tuple-element.24), channel_id=1, source_target_pairs={{1,2},{3,4},{5,6},{7,8},{9,10},{11,12},{13,14},{2,1},{4,3},{6,5},{... | collective-permute-start | bytes 602120 | tf_op jit(solution)/shard_map/ppermute | solution.py:513
  15.7 3.4 %collective-permute-start.3 = (f32[49,8,128]{2,1,0:T(8,128)S(1)}, f32[49,8,128]{2,1,0:T(8,128)S(1)}, u32[]{:S(2)}, u32[]{:S(2)}) collective-permute-start(f32[49,8,128]{2,1,0:T(8,128)S(1)} %get-tuple-element.25), channel_id=1, source_target_pairs={{0,1},{2,3},{4,5},{6,7},{8,9},{10,11},{12,13},{14,15},{1,0},{3,2},... | collective-permute-start | bytes 602120 | tf_op jit(solution)/shard_map/ppermute | solution.py:513
  39.6 18.8 %all-to-all-start.1 = ((f32[8,64,128]{2,1,0:T(8,128)}), f32[8,64,128]{2,1,0:T(8,128)S(1)}, u32[]{:S(2)}, u32[]{:S(2)}) async-start(f32[8,64,128]{2,1,0:T(8,128)} %broadcast_in_dim.41), calls=%async_computation.1 | async-start | bytes 524288 | tf_op jit(solution)/shard_map/all_to_all | solution.py:518
  49.1 9.5 %collective-permute-start.4 = (f32[20,128]{1,0:T(8,128)S(1)}, f32[20,128]{1,0:T(8,128)S(1)}, u32[]{:S(2)}, u32[]{:S(2)}) collective-permute-start(f32[20,128]{1,0:T(8,128)S(1)} %pad_maximum_fusion.1.vmid), channel_id=1, source_target_pairs={{1,2},{3,4},{5,6},{7,8},{9,10},{11,12},{13,14},{2,1},{4,3},{6,5},{... | collective-permute-start | bytes 30728 | tf_op jit(solution)/shard_map/ppermute | solution.py:513
  56.0 3.1 %collective-permute-start.5 = (f32[20,128]{1,0:T(8,128)S(1)}, f32[20,128]{1,0:T(8,128)S(1)}, u32[]{:S(2)}, u32[]{:S(2)}) collective-permute-start(f32[20,128]{1,0:T(8,128)S(1)} %pad_maximum_fusion.1.vmid), channel_id=1, source_target_pairs={{0,1},{2,3},{4,5},{6,7},{8,9},{10,11},{12,13},{14,15},{1,0},{3,2},... | collective-permute-start | bytes 30728 | tf_op jit(solution)/shard_map/ppermute | solution.py:513
  59.1 7.1 %collective-permute-start.6 = (f32[2,32,8,128]{3,2,1,0:T(8,128)S(1)}, f32[2,32,8,128]{3,2,1,0:T(8,128)S(1)}, u32[]{:S(2)}, u32[]{:S(2)}) collective-permute-start(f32[2,32,8,128]{3,2,1,0:T(8,128)S(1)} %order.1.mine), channel_id=1, source_target_pairs={{0,1},{2,3},{4,5},{6,7},{8,9},{10,11},{12,13},{14,15},{1,0},{3,2},... | collective-permute-start | bytes 786440 | tf_op jit(solution)/shard_map/ppermute | solution.py:513

commit v14 on v13

--- a/solution.py
+++ b/solution.py
@@ -257,6 +257,11 @@
 PAD = 3
 
 
+def copies_kernel(block, copies):
+    for i in range(copies.shape[0]):
+        copies[i] = block[...]
+
+
 def order_kernel(blocks, planes):
     for c in range(2):
         for i in range(32):
@@ -513,11 +518,6 @@
     return lax.ppermute(x, axis, pairs + [(b, a) for a, b in pairs])
 
 
-def to_all(x, axis, count, groups=None):
-    copies = jnp.broadcast_to(x[None], (count,) + x.shape)
-    return lax.all_to_all(copies, axis, 0, 0, axis_index_groups=groups)
-
-
 def shards(right_side, coefficient, previous):
     even = lax.axis_index("gx") % 2 == 0
     own = lax.optimization_barrier(jnp.concatenate([right_side, coefficient, previous])).reshape(3, 8, 8, 128)
@@ -551,7 +551,14 @@
     blocks = jnp.where(before, lower.reshape(1, 1, 1024), higher.reshape(1, 1, 1024))
     blocks = lax.all_to_all(blocks, "gx", 0, 0)
     same_core = [[2 * z + c for z in range(8)] for c in range(2)]
-    mine = to_all(blocks[:, :, :256].reshape(64, 128), "gy", 8, same_core).reshape(512, 128)
+    copies = pl.pallas_call(
+        copies_kernel,
+        in_specs=[array],
+        out_shape=f32(8, 64, 128),
+        compiler_params=params,
+        name="copies",
+    )(blocks[:, :, :256].reshape(64, 128))
+    mine = lax.all_to_all(copies, "gy", 0, 0, axis_index_groups=same_core).reshape(512, 128)
     mine = pl.pallas_call(
         order_kernel,
         in_specs=[array],

time: 73.4 us -> 73.4 us (level)
  no operation moved by 1% of the time
where the time goes in v14:
time: 73.4 us; the launch traced here: 72.9 us
  starting transfers between devices  39 us (53%)
  blocking collectives  18.1 us (25%)
  Pallas kernels  9.21 us (13%)
  waiting for transfers between devices  5.41 us (7%)
  other arithmetic  0.96 us (1%)
    ppermute x7, starting transfers between devices, swap(): return lax.ppermute(x, axis, pairs + [(b, a) for a, b in pairs])  29.6 us
    all_to_all x1, blocking collectives, shards(): blocks = lax.all_to_all(blocks, 'gx', 0, 0)  18.1 us
    all_to_all x1, starting transfers between devices, shards(): lax.all_to_all(copies, 'gy', 0, 0, axis_index_groups=same_core)  9.38 us
    pallas_call x1, Pallas kernels, shards(): pl.pallas_call(up_kernel, in_specs=[array] * (5 + len(WINDOW_PLANES)), ou...  6.72 us
    ppermute x7, waiting for transfers between devices, swap(): return lax.ppermute(x, axis, pairs + [(b, a) for a, b in pairs])  4.9 us
    pallas_call x1, Pallas kernels, shards(): pl.pallas_call(down_kernel, in_specs=[array] * 5, out_shape=(f32(8, 128),...  1.58 us
  transfers between devices with their start and end apart: 8, of which 5 were waited for; matrix products, arithmetic and copies ran while one was open for 0% of the time, Pallas kernels for 0%

profile of v14, /device:TPU:1, one launch (start us, length us, event | category | flops | bytes accessed | tf_op | source)
XLA Modules:
  0.0 72.9 jit_solution(13378438853145824698)
XLA Ops:
  0.0 0.8 %pad_maximum_fusion = f32[24,8,128]{2,1,0:T(8,128)S(1)} fusion(f32[8,8,128]{2,1,0:T(8,128)} %param.5, f32[8,8,128]{2,1,0:T(8,128)} %param.4, f32[8,8,128]{2,1,0:T(8,128)} %param.3), kind=kLoop, calls=%fused_computation.3 | loop fusion | flops 49152 | bytes 196608 | tf_op jit(solution)/shard_map/concatenate | solution.py:523
  0.8 0.7 collective-permute-start
  1.5 6.6 %collective-permute-start.1 = (f32[3,7,8,128]{3,2,1,0:T(8,128)S(1)}, f32[3,7,8,128]{3,2,1,0:T(8,128)S(1)}, u32[]{:S(2)}, u32[]{:S(2)}) collective-permute-start(f32[3,7,8,128]{3,2,1,0:T(8,128)S(1)} %get-tuple-element.45), channel_id=1, source_target_pairs={{0,16},{32,48},{64,80},{96,112},{128,144},{160,176},{192,208},{224... | collective-permute-start | bytes 258056 | tf_op jit(solution)/shard_map/ppermute | solution.py:518
  8.1 0.0 collective-permute-done.far.xfar
  8.1 1.8 %collective-permute-done.1.near.xnear = f32[3,7,8,128]{3,2,1,0:T(8,128)S(1)} collective-permute-done((f32[3,7,8,128]{3,2,1,0:T(8,128)S(1)}, f32[3,7,8,128]{3,2,1,0:T(8,128)S(1)}, u32[]{:S(2)}, u32[]{:S(2)}) %collective-permute-start.1) | collective-permute-done | bytes 86048 | tf_op jit(solution)/shard_map/ppermute | solution.py:518
  10.0 5.7 %collective-permute-start.2 = (f32[49,8,128]{2,1,0:T(8,128)S(1)}, f32[49,8,128]{2,1,0:T(8,128)S(1)}, u32[]{:S(2)}, u32[]{:S(2)}) collective-permute-start(f32[49,8,128]{2,1,0:T(8,128)S(1)} %get-tuple-element.24), channel_id=1, source_target_pairs={{1,2},{3,4},{5,6},{7,8},{9,10},{11,12},{13,14},{2,1},{4,3},{6,5},{... | collective-permute-start | bytes 602120 | tf_op jit(solution)/shard_map/ppermute | solution.py:518
  15.7 1.9 %collective-permute-start.3 = (f32[49,8,128]{2,1,0:T(8,128)S(1)}, f32[49,8,128]{2,1,0:T(8,128)S(1)}, u32[]{:S(2)}, u32[]{:S(2)}) collective-permute-start(f32[49,8,128]{2,1,0:T(8,128)S(1)} %get-tuple-element.25), channel_id=1, source_target_pairs={{0,1},{2,3},{4,5},{6,7},{8,9},{10,11},{12,13},{14,15},{1,0},{3,2},... | collective-permute-start | bytes 602120 | tf_op jit(solution)/shard_map/ppermute | solution.py:518
  17.6 1.4 %collective-permute-done.2.far = f32[49,8,128]{2,1,0:T(8,128)S(1)} collective-permute-done((f32[49,8,128]{2,1,0:T(8,128)S(1)}, f32[49,8,128]{2,1,0:T(8,128)S(1)}, u32[]{:S(2)}, u32[]{:S(2)}) %collective-permute-start.2) | collective-permute-done | bytes 200736 | tf_op jit(solution)/shard_map/ppermute | solution.py:518
  19.1 0.0 collective-permute-done.3.near
  19.1 1.6 %down.1 = (f32[8,128]{1,0:T(8,128)S(1)}, f32[8,128]{1,0:T(8,128)S(1)}, f32[8,128]{1,0:T(8,128)S(1)}, f32[12,24,128]{2,1,0:T(8,128)S(1)}, f32[10,24,128]{2,1,0:T(...) custom-call(f32[3,8,8,128]{3,2,1,0:T(8,128)S(1)} %bitcast.12, ...), custom_call_target="tpu_custom_call" | custom-call | tf_op jit(solution)/shard_map/down/pallas_call | solution.py:541
  20.7 0.1 broadcast_select_fusion
  20.8 18.1 %all_to_all.10 = f32[32,1,1024]{2,1,0:T(1,128)S(1)} all-to-all(f32[32,1,1024]{2,1,0:T(1,128)S(1)} %broadcast_select_fusion), channel_id=1, replica_groups=mesh['gx'=32,'gy'=16] {'gx'}, dimensions={0} | all-to-all | bytes 262144 | tf_op jit(solution)/shard_map/all_to_all | solution.py:552
  38.9 0.7 copies.1
  39.6 9.4 %all-to-all-start.1 = ((f32[8,64,128]{2,1,0:T(8,128)}), f32[8,64,128]{2,1,0:T(8,128)S(1)}, u32[]{:S(2)}, u32[]{:S(2)}) async-start(f32[8,64,128]{2,1,0:T(8,128)} %copies.1), calls=%async_computation.1 | async-start | bytes 524288 | tf_op jit(solution)/shard_map/all_to_all | solution.py:561
  49.1 6.9 %collective-permute-start.4 = (f32[20,128]{1,0:T(8,128)S(1)}, f32[20,128]{1,0:T(8,128)S(1)}, u32[]{:S(2)}, u32[]{:S(2)}) collective-permute-start(f32[20,128]{1,0:T(8,128)S(1)} %pad_maximum_fusion.1.vmid), channel_id=1, source_target_pairs={{1,2},{3,4},{5,6},{7,8},{9,10},{11,12},{13,14},{2,1},{4,3},{6,5},{... | collective-permute-start | bytes 30728 | tf_op jit(solution)/shard_map/ppermute | solution.py:518
  56.0 1.9 %collective-permute-start.5 = (f32[20,128]{1,0:T(8,128)S(1)}, f32[20,128]{1,0:T(8,128)S(1)}, u32[]{:S(2)}, u32[]{:S(2)}) collective-permute-start(f32[20,128]{1,0:T(8,128)S(1)} %pad_maximum_fusion.1.vmid), channel_id=1, source_target_pairs={{0,1},{2,3},{4,5},{6,7},{8,9},{10,11},{12,13},{14,15},{1,0},{3,2},... | collective-permute-start | bytes 30728 | tf_op jit(solution)/shard_map/ppermute | solution.py:518
  57.9 0.5 all-to-all-done.1
  58.4 0.2 order.1.mine
  58.6 0.0 collective-permute-done.4.vfar
  58.6 0.5 collective-permute-done.5.vnear
  59.1 6.0 %collective-permute-start.6 = (f32[2,32,8,128]{3,2,1,0:T(8,128)S(1)}, f32[2,32,8,128]{3,2,1,0:T(8,128)S(1)}, u32[]{:S(2)}, u32[]{:S(2)}) collective-permute-start(f32[2,32,8,128]{3,2,1,0:T(8,128)S(1)} %order.1.mine), channel_id=1, source_target_pairs={{0,1},{2,3},{4,5},{6,7},{8,9},{10,11},{12,13},{14,15},{1,0},{3,2},... | collective-permute-start | bytes 786440 | tf_op jit(solution)/shard_map/ppermute | solution.py:518
  65.0 1.1 %collective-permute-done.6.other = f32[2,32,8,128]{3,2,1,0:T(8,128)S(1)} collective-permute-done((f32[2,32,8,128]{3,2,1,0:T(8,128)S(1)}, f32[2,32,8,128]{3,2,1,0:T(8,128)S(1)}, u32[]{:S(2)}, u32[]{:S(2)}) %collective-permute-start.6) | collective-permute-done | bytes 262176 | tf_op jit(solution)/shard_map/ppermute | solution.py:518
  66.2 6.7 %up.1 = f32[8,8,128]{2,1,0:T(8,128)} custom-call(f32[2,32,8,128]{3,2,1,0:T(8,128)S(1)} %order.1.mine, f32[2,32,8,128]{3,2,1,0:T(8,128)S(1)} %collective-permute-done.6.other, f32[12,24,128]{2,1,0:T(8,128)S(1)} %get-tuple-element.30.v0, f32[10,24,128]{2,1,0:T(8,128)S(1)} %get-tuple-element.31.f0, f32[8,24,128]{2,1,0:T(8,128)S(1)} %get-tuple-element.32.f1, ...), custom_call_target="tpu_custom_call" | custom-call | tf_op jit(solution)/shard_map/up/pallas_call | solution.py:578
  (8 shorter events, 0.2 us)
Async XLA Ops:
  0.8 7.3 %collective-permute-start = (f32[3,7,8,128]{3,2,1,0:T(8,128)S(1)}, f32[3,7,8,128]{3,2,1,0:T(8,128)S(1)}, u32[]{:S(2)}, u32[]{:S(2)}) collective-permute-start(f32[3,7,8,128]{3,2,1,0:T(8,128)S(1)} %get-tuple-element.46), channel_id=1, source_target_pairs={{16,32},{48,64},{80,96},{112,128},{144,160},{176,192},{208,224},{2... | collective-permute-start | bytes 258056 | tf_op jit(solution)/shard_map/ppermute | solution.py:518
  1.5 8.4 %collective-permute-start.1 = (f32[3,7,8,128]{3,2,1,0:T(8,128)S(1)}, f32[3,7,8,128]{3,2,1,0:T(8,128)S(1)}, u32[]{:S(2)}, u32[]{:S(2)}) collective-permute-start(f32[3,7,8,128]{3,2,1,0:T(8,128)S(1)} %get-tuple-element.45), channel_id=1, source_target_pairs={{0,16},{32,48},{64,80},{96,112},{128,144},{160,176},{192,208},{224... | collective-permute-start | bytes 258056 | tf_op jit(solution)/shard_map/ppermute | solution.py:518
  10.0 9.1 %collective-permute-start.2 = (f32[49,8,128]{2,1,0:T(8,128)S(1)}, f32[49,8,128]{2,1,0:T(8,128)S(1)}, u32[]{:S(2)}, u32[]{:S(2)}) collective-permute-start(f32[49,8,128]{2,1,0:T(8,128)S(1)} %get-tuple-element.24), channel_id=1, source_target_pairs={{1,2},{3,4},{5,6},{7,8},{9,10},{11,12},{13,14},{2,1},{4,3},{6,5},{... | collective-permute-start | bytes 602120 | tf_op jit(solution)/shard_map/ppermute | solution.py:518
  15.7 3.4 %collective-permute-start.3 = (f32[49,8,128]{2,1,0:T(8,128)S(1)}, f32[49,8,128]{2,1,0:T(8,128)S(1)}, u32[]{:S(2)}, u32[]{:S(2)}) collective-permute-start(f32[49,8,128]{2,1,0:T(8,128)S(1)} %get-tuple-element.25), channel_id=1, source_target_pairs={{0,1},{2,3},{4,5},{6,7},{8,9},{10,11},{12,13},{14,15},{1,0},{3,2},... | collective-permute-start | bytes 602120 | tf_op jit(solution)/shard_map/ppermute | solution.py:518
  39.6 18.8 %all-to-all-start.1 = ((f32[8,64,128]{2,1,0:T(8,128)}), f32[8,64,128]{2,1,0:T(8,128)S(1)}, u32[]{:S(2)}, u32[]{:S(2)}) async-start(f32[8,64,128]{2,1,0:T(8,128)} %copies.1), calls=%async_computation.1 | async-start | bytes 524288 | tf_op jit(solution)/shard_map/all_to_all | solution.py:561
  49.1 9.5 %collective-permute-start.4 = (f32[20,128]{1,0:T(8,128)S(1)}, f32[20,128]{1,0:T(8,128)S(1)}, u32[]{:S(2)}, u32[]{:S(2)}) collective-permute-start(f32[20,128]{1,0:T(8,128)S(1)} %pad_maximum_fusion.1.vmid), channel_id=1, source_target_pairs={{1,2},{3,4},{5,6},{7,8},{9,10},{11,12},{13,14},{2,1},{4,3},{6,5},{... | collective-permute-start | bytes 30728 | tf_op jit(solution)/shard_map/ppermute | solution.py:518
  56.0 3.1 %collective-permute-start.5 = (f32[20,128]{1,0:T(8,128)S(1)}, f32[20,128]{1,0:T(8,128)S(1)}, u32[]{:S(2)}, u32[]{:S(2)}) collective-permute-start(f32[20,128]{1,0:T(8,128)S(1)} %pad_maximum_fusion.1.vmid), channel_id=1, source_target_pairs={{0,1},{2,3},{4,5},{6,7},{8,9},{10,11},{12,13},{14,15},{1,0},{3,2},... | collective-permute-start | bytes 30728 | tf_op jit(solution)/shard_map/ppermute | solution.py:518
  59.1 7.1 %collective-permute-start.6 = (f32[2,32,8,128]{3,2,1,0:T(8,128)S(1)}, f32[2,32,8,128]{3,2,1,0:T(8,128)S(1)}, u32[]{:S(2)}, u32[]{:S(2)}) collective-permute-start(f32[2,32,8,128]{3,2,1,0:T(8,128)S(1)} %order.1.mine), channel_id=1, source_target_pairs={{0,1},{2,3},{4,5},{6,7},{8,9},{10,11},{12,13},{14,15},{1,0},{3,2},... | collective-permute-start | bytes 786440 | tf_op jit(solution)/shard_map/ppermute | solution.py:518

commit v15 on v14

--- a/solution.py
+++ b/solution.py
@@ -257,9 +257,12 @@
 PAD = 3
 
 
-def copies_kernel(block, copies):
-    for i in range(copies.shape[0]):
-        copies[i] = block[...]
+def copies_kernel(block, copies, sems):
+    started = [pltpu.make_async_copy(block, copies.at[i], sems.at[i]) for i in range(8)]
+    for copy in started:
+        copy.start()
+    for copy in started:
+        copy.wait()
 
 
 def order_kernel(blocks, planes):
@@ -554,7 +557,9 @@
     copies = pl.pallas_call(
         copies_kernel,
         in_specs=[array],
+        out_specs=pl.BlockSpec(memory_space=pl.ANY),
         out_shape=f32(8, 64, 128),
+        scratch_shapes=[pltpu.SemaphoreType.DMA((8,))],
         compiler_params=params,
         name="copies",
     )(blocks[:, :, :256].reshape(64, 128))

time: 73.4 us -> 73.4 us (level)
  no operation moved by 1% of the time
where the time goes in v15:
time: 73.4 us; the launch traced here: 73 us
  starting transfers between devices  39 us (53%)
  blocking collectives  18.1 us (25%)
  Pallas kernels  9.26 us (13%)
  waiting for transfers between devices  5.41 us (7%)
  other arithmetic  0.96 us (1%)
    ppermute x7, starting transfers between devices, swap(): return lax.ppermute(x, axis, pairs + [(b, a) for a, b in pairs])  29.6 us
    all_to_all x1, blocking collectives, shards(): blocks = lax.all_to_all(blocks, 'gx', 0, 0)  18.1 us
    all_to_all x1, starting transfers between devices, shards(): lax.all_to_all(copies, 'gy', 0, 0, axis_index_groups=same_core)  9.39 us
    pallas_call x1, Pallas kernels, shards(): pl.pallas_call(up_kernel, in_specs=[array] * (5 + len(WINDOW_PLANES)), ou...  6.72 us
    ppermute x7, waiting for transfers between devices, swap(): return lax.ppermute(x, axis, pairs + [(b, a) for a, b in pairs])  4.9 us
    pallas_call x1, Pallas kernels, shards(): pl.pallas_call(down_kernel, in_specs=[array] * 5, out_shape=(f32(8, 128),...  1.58 us
  transfers between devices with their start and end apart: 8, of which 5 were waited for; matrix products, arithmetic and copies ran while one was open for 0% of the time, Pallas kernels for 0%

profile of v15, /device:TPU:1, one launch (start us, length us, event | category | flops | bytes accessed | tf_op | source)
XLA Modules:
  0.0 73.0 jit_solution(10017110334936342718)
XLA Ops:
  0.0 0.8 %pad_maximum_fusion = f32[24,8,128]{2,1,0:T(8,128)S(1)} fusion(f32[8,8,128]{2,1,0:T(8,128)} %param.5, f32[8,8,128]{2,1,0:T(8,128)} %param.4, f32[8,8,128]{2,1,0:T(8,128)} %param.3), kind=kLoop, calls=%fused_computation.3 | loop fusion | flops 49152 | bytes 196608 | tf_op jit(solution)/shard_map/concatenate | solution.py:526
  0.8 0.7 collective-permute-start
  1.5 6.6 %collective-permute-start.1 = (f32[3,7,8,128]{3,2,1,0:T(8,128)S(1)}, f32[3,7,8,128]{3,2,1,0:T(8,128)S(1)}, u32[]{:S(2)}, u32[]{:S(2)}) collective-permute-start(f32[3,7,8,128]{3,2,1,0:T(8,128)S(1)} %get-tuple-element.45), channel_id=1, source_target_pairs={{0,16},{32,48},{64,80},{96,112},{128,144},{160,176},{192,208},{224... | collective-permute-start | bytes 258056 | tf_op jit(solution)/shard_map/ppermute | solution.py:521
  8.1 0.0 collective-permute-done.far.xfar
  8.1 1.8 %collective-permute-done.1.near.xnear = f32[3,7,8,128]{3,2,1,0:T(8,128)S(1)} collective-permute-done((f32[3,7,8,128]{3,2,1,0:T(8,128)S(1)}, f32[3,7,8,128]{3,2,1,0:T(8,128)S(1)}, u32[]{:S(2)}, u32[]{:S(2)}) %collective-permute-start.1) | collective-permute-done | bytes 86048 | tf_op jit(solution)/shard_map/ppermute | solution.py:521
  10.0 5.7 %collective-permute-start.2 = (f32[49,8,128]{2,1,0:T(8,128)S(1)}, f32[49,8,128]{2,1,0:T(8,128)S(1)}, u32[]{:S(2)}, u32[]{:S(2)}) collective-permute-start(f32[49,8,128]{2,1,0:T(8,128)S(1)} %get-tuple-element.24), channel_id=1, source_target_pairs={{1,2},{3,4},{5,6},{7,8},{9,10},{11,12},{13,14},{2,1},{4,3},{6,5},{... | collective-permute-start | bytes 602120 | tf_op jit(solution)/shard_map/ppermute | solution.py:521
  15.7 1.9 %collective-permute-start.3 = (f32[49,8,128]{2,1,0:T(8,128)S(1)}, f32[49,8,128]{2,1,0:T(8,128)S(1)}, u32[]{:S(2)}, u32[]{:S(2)}) collective-permute-start(f32[49,8,128]{2,1,0:T(8,128)S(1)} %get-tuple-element.25), channel_id=1, source_target_pairs={{0,1},{2,3},{4,5},{6,7},{8,9},{10,11},{12,13},{14,15},{1,0},{3,2},... | collective-permute-start | bytes 602120 | tf_op jit(solution)/shard_map/ppermute | solution.py:521
  17.6 1.4 %collective-permute-done.2.far = f32[49,8,128]{2,1,0:T(8,128)S(1)} collective-permute-done((f32[49,8,128]{2,1,0:T(8,128)S(1)}, f32[49,8,128]{2,1,0:T(8,128)S(1)}, u32[]{:S(2)}, u32[]{:S(2)}) %collective-permute-start.2) | collective-permute-done | bytes 200736 | tf_op jit(solution)/shard_map/ppermute | solution.py:521
  19.1 0.0 collective-permute-done.3.near
  19.1 1.6 %down.1 = (f32[8,128]{1,0:T(8,128)S(1)}, f32[8,128]{1,0:T(8,128)S(1)}, f32[8,128]{1,0:T(8,128)S(1)}, f32[12,24,128]{2,1,0:T(8,128)S(1)}, f32[10,24,128]{2,1,0:T(...) custom-call(f32[3,8,8,128]{3,2,1,0:T(8,128)S(1)} %bitcast.12, ...), custom_call_target="tpu_custom_call" | custom-call | tf_op jit(solution)/shard_map/down/pallas_call | solution.py:544
  20.7 0.1 broadcast_select_fusion
  20.8 18.1 %all_to_all.10 = f32[32,1,1024]{2,1,0:T(1,128)S(1)} all-to-all(f32[32,1,1024]{2,1,0:T(1,128)S(1)} %broadcast_select_fusion), channel_id=1, replica_groups=mesh['gx'=32,'gy'=16] {'gx'}, dimensions={0} | all-to-all | bytes 262144 | tf_op jit(solution)/shard_map/all_to_all | solution.py:555
  38.9 0.8 %copies.1 = f32[8,64,128]{2,1,0:T(8,128)} custom-call(f32[64,128]{1,0:T(8,128)S(1)} %bitcast.14), custom_call_target="tpu_custom_call" | custom-call | tf_op jit(solution)/shard_map/copies/pallas_call | solution.py:557
  39.7 9.4 %all-to-all-start.1 = ((f32[8,64,128]{2,1,0:T(8,128)}), f32[8,64,128]{2,1,0:T(8,128)S(1)}, u32[]{:S(2)}, u32[]{:S(2)}) async-start(f32[8,64,128]{2,1,0:T(8,128)} %copies.1), calls=%async_computation.1 | async-start | bytes 524288 | tf_op jit(solution)/shard_map/all_to_all | solution.py:566
  49.2 6.9 %collective-permute-start.4 = (f32[20,128]{1,0:T(8,128)S(1)}, f32[20,128]{1,0:T(8,128)S(1)}, u32[]{:S(2)}, u32[]{:S(2)}) collective-permute-start(f32[20,128]{1,0:T(8,128)S(1)} %pad_maximum_fusion.1.vmid), channel_id=1, source_target_pairs={{1,2},{3,4},{5,6},{7,8},{9,10},{11,12},{13,14},{2,1},{4,3},{6,5},{... | collective-permute-start | bytes 30728 | tf_op jit(solution)/shard_map/ppermute | solution.py:521
  56.1 1.9 %collective-permute-start.5 = (f32[20,128]{1,0:T(8,128)S(1)}, f32[20,128]{1,0:T(8,128)S(1)}, u32[]{:S(2)}, u32[]{:S(2)}) collective-permute-start(f32[20,128]{1,0:T(8,128)S(1)} %pad_maximum_fusion.1.vmid), channel_id=1, source_target_pairs={{0,1},{2,3},{4,5},{6,7},{8,9},{10,11},{12,13},{14,15},{1,0},{3,2},... | collective-permute-start | bytes 30728 | tf_op jit(solution)/shard_map/ppermute | solution.py:521
  58.0 0.5 all-to-all-done.1
  58.5 0.2 order.1.mine
  58.7 0.0 collective-permute-done.4.vfar
  58.7 0.5 collective-permute-done.5.vnear
  59.1 6.0 %collective-permute-start.6 = (f32[2,32,8,128]{3,2,1,0:T(8,128)S(1)}, f32[2,32,8,128]{3,2,1,0:T(8,128)S(1)}, u32[]{:S(2)}, u32[]{:S(2)}) collective-permute-start(f32[2,32,8,128]{3,2,1,0:T(8,128)S(1)} %order.1.mine), channel_id=1, source_target_pairs={{0,1},{2,3},{4,5},{6,7},{8,9},{10,11},{12,13},{14,15},{1,0},{3,2},... | collective-permute-start | bytes 786440 | tf_op jit(solution)/shard_map/ppermute | solution.py:521
  65.1 1.1 %collective-permute-done.6.other = f32[2,32,8,128]{3,2,1,0:T(8,128)S(1)} collective-permute-done((f32[2,32,8,128]{3,2,1,0:T(8,128)S(1)}, f32[2,32,8,128]{3,2,1,0:T(8,128)S(1)}, u32[]{:S(2)}, u32[]{:S(2)}) %collective-permute-start.6) | collective-permute-done | bytes 262176 | tf_op jit(solution)/shard_map/ppermute | solution.py:521
  66.3 6.7 %up.1 = f32[8,8,128]{2,1,0:T(8,128)} custom-call(f32[2,32,8,128]{3,2,1,0:T(8,128)S(1)} %order.1.mine, f32[2,32,8,128]{3,2,1,0:T(8,128)S(1)} %collective-permute-done.6.other, f32[12,24,128]{2,1,0:T(8,128)S(1)} %get-tuple-element.30.v0, f32[10,24,128]{2,1,0:T(8,128)S(1)} %get-tuple-element.31.f0, f32[8,24,128]{2,1,0:T(8,128)S(1)} %get-tuple-element.32.f1, ...), custom_call_target="tpu_custom_call" | custom-call | tf_op jit(solution)/shard_map/up/pallas_call | solution.py:583
  (8 shorter events, 0.2 us)
Async XLA Ops:
  0.8 7.3 %collective-permute-start = (f32[3,7,8,128]{3,2,1,0:T(8,128)S(1)}, f32[3,7,8,128]{3,2,1,0:T(8,128)S(1)}, u32[]{:S(2)}, u32[]{:S(2)}) collective-permute-start(f32[3,7,8,128]{3,2,1,0:T(8,128)S(1)} %get-tuple-element.46), channel_id=1, source_target_pairs={{16,32},{48,64},{80,96},{112,128},{144,160},{176,192},{208,224},{2... | collective-permute-start | bytes 258056 | tf_op jit(solution)/shard_map/ppermute | solution.py:521
  1.5 8.4 %collective-permute-start.1 = (f32[3,7,8,128]{3,2,1,0:T(8,128)S(1)}, f32[3,7,8,128]{3,2,1,0:T(8,128)S(1)}, u32[]{:S(2)}, u32[]{:S(2)}) collective-permute-start(f32[3,7,8,128]{3,2,1,0:T(8,128)S(1)} %get-tuple-element.45), channel_id=1, source_target_pairs={{0,16},{32,48},{64,80},{96,112},{128,144},{160,176},{192,208},{224... | collective-permute-start | bytes 258056 | tf_op jit(solution)/shard_map/ppermute | solution.py:521
  10.0 9.1 %collective-permute-start.2 = (f32[49,8,128]{2,1,0:T(8,128)S(1)}, f32[49,8,128]{2,1,0:T(8,128)S(1)}, u32[]{:S(2)}, u32[]{:S(2)}) collective-permute-start(f32[49,8,128]{2,1,0:T(8,128)S(1)} %get-tuple-element.24), channel_id=1, source_target_pairs={{1,2},{3,4},{5,6},{7,8},{9,10},{11,12},{13,14},{2,1},{4,3},{6,5},{... | collective-permute-start | bytes 602120 | tf_op jit(solution)/shard_map/ppermute | solution.py:521
  15.7 3.4 %collective-permute-start.3 = (f32[49,8,128]{2,1,0:T(8,128)S(1)}, f32[49,8,128]{2,1,0:T(8,128)S(1)}, u32[]{:S(2)}, u32[]{:S(2)}) collective-permute-start(f32[49,8,128]{2,1,0:T(8,128)S(1)} %get-tuple-element.25), channel_id=1, source_target_pairs={{0,1},{2,3},{4,5},{6,7},{8,9},{10,11},{12,13},{14,15},{1,0},{3,2},... | collective-permute-start | bytes 602120 | tf_op jit(solution)/shard_map/ppermute | solution.py:521
  39.7 18.8 %all-to-all-start.1 = ((f32[8,64,128]{2,1,0:T(8,128)}), f32[8,64,128]{2,1,0:T(8,128)S(1)}, u32[]{:S(2)}, u32[]{:S(2)}) async-start(f32[8,64,128]{2,1,0:T(8,128)} %copies.1), calls=%async_computation.1 | async-start | bytes 524288 | tf_op jit(solution)/shard_map/all_to_all | solution.py:566
  49.2 9.5 %collective-permute-start.4 = (f32[20,128]{1,0:T(8,128)S(1)}, f32[20,128]{1,0:T(8,128)S(1)}, u32[]{:S(2)}, u32[]{:S(2)}) collective-permute-start(f32[20,128]{1,0:T(8,128)S(1)} %pad_maximum_fusion.1.vmid), channel_id=1, source_target_pairs={{1,2},{3,4},{5,6},{7,8},{9,10},{11,12},{13,14},{2,1},{4,3},{6,5},{... | collective-permute-start | bytes 30728 | tf_op jit(solution)/shard_map/ppermute | solution.py:521
  56.1 3.1 %collective-permute-start.5 = (f32[20,128]{1,0:T(8,128)S(1)}, f32[20,128]{1,0:T(8,128)S(1)}, u32[]{:S(2)}, u32[]{:S(2)}) collective-permute-start(f32[20,128]{1,0:T(8,128)S(1)} %pad_maximum_fusion.1.vmid), channel_id=1, source_target_pairs={{0,1},{2,3},{4,5},{6,7},{8,9},{10,11},{12,13},{14,15},{1,0},{3,2},... | collective-permute-start | bytes 30728 | tf_op jit(solution)/shard_map/ppermute | solution.py:521
  59.1 7.1 %collective-permute-start.6 = (f32[2,32,8,128]{3,2,1,0:T(8,128)S(1)}, f32[2,32,8,128]{3,2,1,0:T(8,128)S(1)}, u32[]{:S(2)}, u32[]{:S(2)}) collective-permute-start(f32[2,32,8,128]{3,2,1,0:T(8,128)S(1)} %order.1.mine), channel_id=1, source_target_pairs={{0,1},{2,3},{4,5},{6,7},{8,9},{10,11},{12,13},{14,15},{1,0},{3,2},... | collective-permute-start | bytes 786440 | tf_op jit(solution)/shard_map/ppermute | solution.py:521
